TPU v7x, 128 devices: a whole 4x4x4 slice. The times are simulated.
128 devices in a mesh: load: 8 (over z_hi, y), space: 16 (over z_lo, x, core).
Axes of the slice: x: 4, y: 4, z: 4 (z_hi: 2, z_lo: 2; z = z_hi * 2 + z_lo), core: 2. Of those that a mesh axis runs over, the one named last changes fastest.
Arguments:
- density: float32 [32, 64, 256], P('space', 'load'), may hold values from 0.2 to 1
- fixed_dofs: int32 [3, 32, 64, 256], P(None, 'space'), may hold values 0 or 1
- body_loads: float32 [8, 3, 32, 64, 256], P('load', None, 'space'), may hold values from -6 to 6
- point_nodes: int32 [8, 128], P('load'), may hold values from 0 to 524287
- point_forces: float32 [8, 3, 128], P('load'), may hold values from -24 to 24
Outputs:
- displacement: float32 [8, 3, 32, 64, 256], P('load', None, 'space')
- filtered: float32 [32, 64, 256], P('space', 'load')
All inputs are finite; a program needn't handle non-finite values. No bound on the sum of `fixed_dofs` on one device may be relied on, other than what follows from the above.
Results may differ from a plain program's by a relative error of at most 0.0003.
Values sent between devices are 32-bit elements; how exact they have to be, the bound alone decides.
No kernel may reach another device: no remote copies, remote signals or barrier semaphores. Data moves between devices by JAX's collectives and lax.ppermute only.
A program may use at most 64 MiB of HBM per device.

v0:
```python
import math

import jax
import jax.numpy as jnp
from jax import lax
from jax.experimental import pallas as pl
from jax.experimental.pallas import tpu as pltpu
from jax.sharding import PartitionSpec as P

CX = 2
NY = 64
NZ = 256
ROWS = 8
CHUNKS = NY // ROWS
ZBITS = 8
EMIN = 0.001
PENALTY = 3.0
RADIUS = 1.5
POISSON = 0.3
LAME = POISSON / ((1.0 + POISSON) * (1.0 - 2.0 * POISSON))
SHEAR = 1.0 / (2.0 * (1.0 + POISSON))
KDIAG = (LAME + 4.0 * SHEAR) / 9.0
F32 = jnp.float32
VMEM_LIMIT = 56 * 1024 * 1024
PAIRS = ("ss", "sd", "ds", "dd")


def kernel_call(fn, outs, n_smem, n_in, scratch=()):
    vmem = pl.BlockSpec(memory_space=pltpu.VMEM)
    smem = pl.BlockSpec(memory_space=pltpu.SMEM)
    return pl.pallas_call(
        fn,
        out_shape=[jax.ShapeDtypeStruct(shape, F32) for shape in outs],
        in_specs=[smem] * n_smem + [vmem] * n_in,
        out_specs=[vmem] * len(outs),
        scratch_shapes=list(scratch),
        compiler_params=pltpu.CompilerParams(vmem_limit_bytes=VMEM_LIMIT),
    )


def lane_ids(shape):
    return lax.broadcasted_iota(jnp.int32, shape, 1)


def row_ids(shape):
    return lax.broadcasted_iota(jnp.int32, shape, 0)


def from_above(field):
    return jnp.where(lane_ids(field.shape) == NZ - 1, 0.0, pltpu.roll(field, NZ - 1, 1))


def from_below(field):
    return jnp.where(lane_ids(field.shape) == 0, 0.0, pltpu.roll(field, 1, 1))


def rows_at(chunk):
    return pl.ds(pl.multiple_of(chunk * ROWS, ROWS), ROWS)


def store_z_modes(zs_ref, zd_ref, plane, comp, rows, field):
    up = from_above(field)
    zs_ref[plane, comp, rows] = field + up
    zd_ref[plane, comp, rows] = up - field


def y_modes(cur, nxt):
    first = row_ids(cur.shape) == 0
    up = pltpu.roll(jnp.where(first, nxt, cur), ROWS - 1, 0)
    return cur + up, up - cur


def plane_modes(zs_ref, zd_ref, plane, chunk):
    out = []
    for comp in range(3):
        here, after = rows_at(chunk), rows_at(chunk + 1)
        ss, ds = y_modes(zs_ref[plane, comp, here], zs_ref[plane, comp, after])
        sd, dd = y_modes(zd_ref[plane, comp, here], zd_ref[plane, comp, after])
        out.append({"ss": ss, "sd": sd, "ds": ds, "dd": dd})
    return out


def element_modes(low, high):
    modes = []
    for comp in range(3):
        field = {}
        for pair in PAIRS:
            field["d" + pair] = high[comp][pair] - low[comp][pair]
            if pair != "ss":
                field["s" + pair] = high[comp][pair] + low[comp][pair]
        modes.append(field)
    return modes


NORMAL = ((0, "dss"), (1, "sds"), (2, "ssd"))
SHEARS = (((0, "sds"), (1, "dss")), ((0, "ssd"), (2, "dss")), ((1, "ssd"), (2, "sds")))
BENDS = (((0, "dsd"), (1, "sdd")), ((0, "dds"), (2, "sdd")), ((1, "dds"), (2, "dsd")))
TWISTS = ((0, "sdd"), (1, "dsd"), (2, "dds"))


def element_response(modes, modulus):
    k_lame = modulus * (LAME / 16.0)
    k_two = modulus * (SHEAR / 8.0)
    k_shear = modulus * (SHEAR / 16.0)
    k_bend = modulus * (LAME / 48.0)
    k_twist = modulus * (SHEAR / 48.0)
    k_last = modulus * ((LAME + 4.0 * SHEAR) / 144.0)
    force = [{}, {}, {}]
    get = lambda key: modes[key[0]][key[1]]
    trace = k_lame * (get(NORMAL[0]) + get(NORMAL[1]) + get(NORMAL[2]))
    for comp, name in NORMAL:
        force[comp][name] = k_two * modes[comp][name] + trace
    for one, two in SHEARS:
        both = k_shear * (get(one) + get(two))
        force[one[0]][one[1]] = both
        force[two[0]][two[1]] = both
    for one, two in BENDS:
        both = k_bend * (get(one) + get(two))
        force[one[0]][one[1]] = k_shear * get(one) + both
        force[two[0]][two[1]] = k_shear * get(two) + both
    total = get(TWISTS[0]) + get(TWISTS[1]) + get(TWISTS[2])
    for comp, name in TWISTS:
        force[comp][name] = k_twist * (modes[comp][name] + total)
    for comp in range(3):
        force[comp]["ddd"] = k_last * modes[comp]["ddd"]
    return force


def element_energy(modes):
    get = lambda key: modes[key[0]][key[1]]
    square = lambda value: value * value
    normal = [get(key) for key in NORMAL]
    twist = [get(key) for key in TWISTS]
    energy = (LAME / 16.0) * square(normal[0] + normal[1] + normal[2])
    energy += (SHEAR / 8.0) * (square(normal[0]) + square(normal[1]) + square(normal[2]))
    shear = sum(square(get(one) + get(two)) for one, two in SHEARS)
    shear += sum(square(get(one)) + square(get(two)) for one, two in BENDS)
    energy += (SHEAR / 16.0) * shear
    energy += (LAME / 48.0) * sum(square(get(one) + get(two)) for one, two in BENDS)
    twisted = square(twist[0]) + square(twist[1]) + square(twist[2])
    energy += (SHEAR / 48.0) * (twisted + square(twist[0] + twist[1] + twist[2]))
    last = square(modes[0]["ddd"]) + square(modes[1]["ddd"]) + square(modes[2]["ddd"])
    return energy + ((LAME + 4.0 * SHEAR) / 144.0) * last


def split_x(force):
    low, high = [], []
    for comp in range(3):
        lo, hi = {}, {}
        for pair in PAIRS:
            diff = force[comp]["d" + pair]
            if pair == "ss":
                lo[pair], hi[pair] = -diff, diff
            else:
                mean = force[comp]["s" + pair]
                lo[pair], hi[pair] = mean - diff, mean + diff
        low.append(lo)
        high.append(hi)
    return low, high


def node_force(acc, prev):
    sides = []
    for y_mode in ("s", "d"):
        mean, diff = acc[y_mode + "s"], acc[y_mode + "d"]
        sides.append((mean - diff) + from_below(mean + diff))
    low, high = sides[0] - sides[1], sides[0] + sides[1]
    last = row_ids(low.shape) == ROWS - 1
    return low + pltpu.roll(jnp.where(last, prev, high), 1, 0), high


def apply_rows(zs_ref, zd_ref, planes, e_ref, e_first, e_pad, carry_ref, chunk):
    low = plane_modes(zs_ref, zd_ref, 0, chunk)
    partial = None
    for plane in range(planes - 1):
        high = plane_modes(zs_ref, zd_ref, plane + 1, chunk)
        modulus = e_ref[e_first + plane, rows_at(chunk + e_pad)]
        to_low, to_high = split_x(element_response(element_modes(low, high), modulus))
        if partial is not None:
            forces = []
            for comp in range(3):
                acc = {pair: partial[comp][pair] + to_low[comp][pair] for pair in PAIRS}
                force, carry = node_force(acc, carry_ref[plane - 1, comp])
                carry_ref[plane - 1, comp] = carry
                forces.append(force)
            yield plane, forces
        partial, low = to_high, high


def loads_kernel(space_ref, body_ref, fixed_ref, node_ref, force_ref, all_ref, right_ref, far_ref):
    cells = CX * NY * NZ
    local = node_ref[...] - space_ref[0] * cells
    valid = (local >= 0) & (local < cells)
    local = jnp.where(valid, local, -1)
    line = lax.shift_right_arithmetic(local, ZBITS)
    depth = lax.bitwise_and(local, NZ - 1)
    points = local.shape[1]
    on_line = row_ids((CX * NY, points)) == line
    lines = [jnp.where(on_line, force_ref[comp : comp + 1, :], 0.0) for comp in range(3)]
    at_depth = jnp.where(row_ids((NZ, points)) == depth, 1.0, 0.0)
    added = lax.dot_general(
        jnp.concatenate(lines, axis=0),
        at_depth,
        (((1,), (1,)), ((), ())),
        precision=lax.Precision.HIGHEST,
        preferred_element_type=F32,
    )
    for plane in range(CX):
        for comp in range(3):
            keep = 1.0 - fixed_ref[comp, plane].astype(F32)
            first = (comp * CX + plane) * NY
            load = keep * (body_ref[comp, plane] + added[first : first + NY])
            all_ref[plane, comp] = load
            right_ref[plane, comp] = load
            all_ref[3 - plane, comp] = keep
            if plane == 0:
                far_ref[0, comp] = load
            else:
                right_ref[2, comp] = keep


def krylov_kernel(
    space_ref, own_ref, left_ref, right_ref, far_ref, dens_ref,
    v0_ref, v1_ref, v2_ref, edge_ref, mom_ref,
    e_ref, inv_ref, zs0, zd0, zs1, zd1, zs2, zd2, carry1, carry2,
):
    first_x = space_ref[0] * CX
    limit = space_ref[1] * CX
    zero_rows = jnp.zeros((ROWS, NZ), F32)
    for plane in range(8):
        at = first_x - 3 + plane
        scale = jnp.where((at >= 0) & (at < limit), 1.0, 0.0).astype(F32)
        e_ref[plane, 0:ROWS] = zero_rows
        for block in range(CHUNKS):
            dens = dens_ref[block, plane]
            rows = slice((block + 1) * ROWS, (block + 2) * ROWS)
            e_ref[plane, rows] = scale * (EMIN + (1.0 - EMIN) * (dens * dens * dens))
    tail = slice(NY, NY + ROWS)
    for comp in range(3):
        for refs, planes in (((zs0, zd0), 7), ((zs1, zd1), 5), ((zs2, zd2), 3)):
            for ref in refs:
                for plane in range(planes):
                    ref[plane, comp, tail] = zero_rows
        for ref, planes in ((carry1, 5), (carry2, 3)):
            for plane in range(planes):
                ref[plane, comp] = zero_rows

    loads = [left_ref.at[0], left_ref.at[1], own_ref.at[0], own_ref.at[1],
             right_ref.at[0], right_ref.at[1], far_ref.at[0]]
    keeps = [left_ref.at[2], own_ref.at[3], own_ref.at[2], right_ref.at[3], right_ref.at[2]]

    def start(chunk, total):
        here = rows_at(chunk)
        last = row_ids((ROWS, NZ)) == ROWS - 1
        for plane in range(7):
            cur = e_ref[plane, rows_at(chunk + 1)] + e_ref[plane + 1, rows_at(chunk + 1)]
            before = e_ref[plane, rows_at(chunk)] + e_ref[plane + 1, rows_at(chunk)]
            cur = cur + pltpu.roll(jnp.where(last, before, cur), 1, 0)
            diag = KDIAG * (cur + from_below(cur))
            inverse = 1.0 / jnp.where(diag > 0.0, diag, 1.0)
            if 1 <= plane <= 5:
                inv_ref[plane - 1, here] = inverse
            for comp in range(3):
                load = loads[plane][comp, here]
                value = load * inverse
                if 1 <= plane <= 5:
                    v0_ref[plane - 1, comp, here] = value
                if plane in (2, 3):
                    total = total + load * value
                store_z_modes(zs0, zd0, plane, comp, here, value)
        return total

    zero = jnp.zeros((ROWS, NZ), F32)
    mom0 = lax.fori_loop(0, CHUNKS, start, zero)

    def first(chunk, totals):
        here = rows_at(chunk)
        odd, even = totals
        for plane, forces in apply_rows(zs0, zd0, 7, e_ref, 1, 1, carry1, chunk):
            inverse = inv_ref[plane - 1, here]
            for comp in range(3):
                kept = keeps[plane - 1][comp, here] > 0.0
                before = v0_ref[plane - 1, comp, here]
                image = jnp.where(kept, forces[comp], before)
                value = jnp.where(kept, forces[comp] * inverse, before)
                v1_ref[plane - 1, comp, here] = value
                store_z_modes(zs1, zd1, plane - 1, comp, here, value)
                if plane in (2, 3):
                    odd = odd + before * image
                    even = even + value * image
        return odd, even

    mom1, mom2 = lax.fori_loop(0, CHUNKS, first, (zero, zero))

    def second(chunk, totals):
        here = rows_at(chunk)
        odd, even = totals
        for plane, forces in apply_rows(zs1, zd1, 5, e_ref, 2, 1, carry2, chunk):
            inverse = inv_ref[plane, here]
            for comp in range(3):
                kept = keeps[plane][comp, here] > 0.0
                before = v1_ref[plane, comp, here]
                image = jnp.where(kept, forces[comp], before)
                value = jnp.where(kept, forces[comp] * inverse, before)
                v2_ref[plane - 1, comp, here] = value
                if plane == 2:
                    edge_ref[comp, here] = value
                store_z_modes(zs2, zd2, plane - 1, comp, here, value)
                if plane in (1, 2):
                    odd = odd + before * image
                    even = even + value * image
        return odd, even

    mom3, mom4 = lax.fori_loop(0, CHUNKS, second, (zero, zero))

    def third(chunk, total):
        low = plane_modes(zs2, zd2, 0, chunk)
        for plane in range(2):
            high = plane_modes(zs2, zd2, plane + 1, chunk)
            energy = element_energy(element_modes(low, high))
            total = total + e_ref[3 + plane, rows_at(chunk + 1)] * energy
            low = high
        return total

    mom5 = lax.fori_loop(0, CHUNKS, third, zero)
    rows = []
    for value in (mom0, mom1, mom2, mom3, mom4, mom5, zero, zero):
        rows.append(jnp.sum(value[:, :128] + value[:, 128:], axis=0, keepdims=True))
    mom_ref[...] = jnp.concatenate(rows, axis=0)


def energy_kernel(v0_ref, v1_ref, v2_ref, left_ref, right_ref, mom_ref, u_ref, out_ref, zs, zd, e_ref):
    total = mom_ref[0]
    for device in range(1, mom_ref.shape[0]):
        total = total + mom_ref[device]
    total = jnp.broadcast_to(jnp.sum(total, axis=1, keepdims=True), (8, 128))
    m0, m1, m2, m3, m4, m5 = [total[k : k + 1] for k in range(6)]
    low10 = m2 / m1
    low20 = m3 / m1
    piv1 = m3 - low10 * m2
    mix = m4 - low20 * m2
    good1 = piv1 > 1e-7 * m3
    safe1 = jnp.where(good1, piv1, 1.0)
    low21 = jnp.where(good1, mix / safe1, 0.0)
    piv2 = m5 - low20 * m3 - low21 * mix
    good2 = good1 & (piv2 > 1e-7 * m5)
    y1 = m1 - low10 * m0
    y2 = m2 - low20 * m0 - low21 * y1
    c2 = jnp.where(good2, y2 / jnp.where(good2, piv2, 1.0), 0.0)
    c1 = jnp.where(good1, y1 / safe1 - low21 * c2, 0.0)
    c0 = m0 / m1 - low10 * c1 - low20 * c2
    c0, c1, c2 = [jnp.broadcast_to(jnp.concatenate([c, c], axis=1), (ROWS, NZ)) for c in (c0, c1, c2)]

    zero_rows = jnp.zeros((ROWS, NZ), F32)
    for plane in range(5):
        for comp in range(3):
            zs[plane, comp, NY : NY + ROWS] = zero_rows
            zd[plane, comp, NY : NY + ROWS] = zero_rows
    for plane in range(4):
        e_ref[plane, 0:ROWS] = zero_rows
        e_ref[plane, NY + ROWS : NY + 2 * ROWS] = zero_rows
    v2_planes = [left_ref, v2_ref.at[0], v2_ref.at[1], v2_ref.at[2], right_ref]

    def combine(chunk, done):
        here = rows_at(chunk)
        for plane in range(5):
            for comp in range(3):
                value = c0 * v0_ref[plane, comp, here] + c1 * v1_ref[plane, comp, here]
                value = value + c2 * v2_planes[plane][comp, here]
                if plane in (1, 2):
                    u_ref[comp, plane - 1, here] = value
                store_z_modes(zs, zd, plane, comp, here, value)
        return done

    lax.fori_loop(0, CHUNKS, combine, 0)

    def measure(chunk, done):
        low = plane_modes(zs, zd, 0, chunk)
        for plane in range(4):
            high = plane_modes(zs, zd, plane + 1, chunk)
            e_ref[plane, rows_at(chunk + 1)] = element_energy(element_modes(low, high))
            low = high
        return done

    lax.fori_loop(0, CHUNKS, measure, 0)
    span = ROWS + 2
    for block in range(CHUNKS):
        for plane in range(4):
            first = ROWS - 1 + block * ROWS
            out_ref[block, plane * span : (plane + 1) * span] = e_ref[plane, first : first + span]


def weigh(planes):
    near = RADIUS - 1.0
    edge = RADIUS - math.sqrt(2.0)
    beside = [from_below(p) + from_above(p) for p in planes]
    cross = []
    full = []
    for p, side in zip(planes, beside):
        up_down = p[0:ROWS] + p[2 : 2 + ROWS]
        mid, mid_side = p[1 : 1 + ROWS], side[1 : 1 + ROWS]
        cross.append(near * mid + edge * (mid_side + up_down))
        diagonal = side[0:ROWS] + side[2 : 2 + ROWS]
        full.append(RADIUS * mid + near * (mid_side + up_down) + edge * diagonal)
    return [full[k] + cross[k - 1] + cross[k + 1] for k in range(1, 1 + CX)]


def filter_kernel(place_ref, energy_ref, dens_ref, out_ref):
    space, n_space, load, n_load = [place_ref[k] for k in range(4)]
    total = energy_ref[0]
    for block in range(1, energy_ref.shape[0]):
        total = total + energy_ref[block]
    span = ROWS + 2
    before = jnp.maximum(load - 1, 0)
    after = jnp.minimum(load + 1, n_load - 1)
    at_y = load * ROWS - 1 + row_ids((span, NZ))
    in_y = (at_y >= 0) & (at_y < n_load * ROWS)
    weighted, inside, own = [], [], []
    for plane in range(4):
        dens = jnp.concatenate(
            [
                dens_ref[before, 2 + plane][ROWS - 1 : ROWS],
                dens_ref[load, 2 + plane],
                dens_ref[after, 2 + plane][0:1],
            ],
            axis=0,
        )
        at_x = space * CX - 1 + plane
        scale = jnp.where((at_x >= 0) & (at_x < n_space * CX), 1.0, 0.0).astype(F32)
        present = scale * jnp.where(in_y, 1.0, 0.0)
        energy = total[plane * span : (plane + 1) * span]
        sensitivity = -PENALTY * (1.0 - EMIN) * (dens * dens) * energy
        weighted.append(present * (dens * sensitivity))
        inside.append(present)
        if 1 <= plane <= CX:
            own.append(dens[1 : 1 + ROWS])
    sums, counts = weigh(weighted), weigh(inside)
    for plane in range(CX):
        out_ref[plane] = sums[plane] / (own[plane] * counts[plane])


def shifted(array, axis, distance):
    size = lax.axis_size(axis)
    route = [(i, i + distance) for i in range(size) if 0 <= i + distance < size]
    return lax.ppermute(array, axis, route)


def body(density, fixed_dofs, body_loads, point_nodes, point_forces):
    n_load, n_space = lax.axis_size("load"), lax.axis_size("space")
    load, space = lax.axis_index("load"), lax.axis_index("space")
    place = jnp.stack([space, jnp.int32(n_space), load, jnp.int32(n_load)]).astype(jnp.int32)
    plane = (3, NY, NZ)
    own, to_right, to_far = kernel_call(
        loads_kernel, [(4,) + plane, (3,) + plane, (1,) + plane], 1, 4
    )(place, body_loads[0], fixed_dofs, point_nodes, point_forces[0])
    dens = jnp.concatenate(
        [
            shifted(density[1:2], "space", 2),
            shifted(density, "space", 1),
            density,
            shifted(density, "space", -1),
            shifted(density[0:1], "space", -2),
        ],
        axis=0,
    )
    left = shifted(to_right, "space", 1)
    right = shifted(own, "space", -1)
    far = shifted(to_far, "space", -2)
    dens = lax.all_to_all(jnp.broadcast_to(dens[None], (n_load,) + dens.shape), "load", 0, 0)

    padded = (NY + ROWS, NZ)
    zed = lambda planes: pltpu.VMEM((planes, 3) + padded, F32)
    v0, v1, v2, edge, mom = kernel_call(
        krylov_kernel,
        [(5,) + plane, (5,) + plane, (3,) + plane, plane, (8, 128)],
        1,
        5,
        [pltpu.VMEM((8,) + padded, F32), pltpu.VMEM((5, NY, NZ), F32)]
        + [zed(7), zed(7), zed(5), zed(5), zed(3), zed(3)]
        + [pltpu.VMEM((5, 3, ROWS, NZ), F32), pltpu.VMEM((3, 3, ROWS, NZ), F32)],
    )(place, own, left, right, far, dens)
    edge_left = shifted(edge, "space", 1)
    edge_right = shifted(edge, "space", -1)
    mom = lax.all_to_all(jnp.broadcast_to(mom[None], (n_space,) + mom.shape), "space", 0, 0)
    moved, energy = kernel_call(
        energy_kernel,
        [(3, CX, NY, NZ), (CHUNKS, 4 * (ROWS + 2), NZ)],
        0,
        6,
        [zed(5), zed(5), pltpu.VMEM((4, NY + 2 * ROWS, NZ), F32)],
    )(v0, v1, v2, edge_left, edge_right, mom)
    energy = lax.all_to_all(energy, "load", 0, 0)
    (filtered,) = kernel_call(filter_kernel, [(CX, ROWS, NZ)], 1, 2)(place, energy, dens)
    return (moved[None], filtered)


def solution(mesh):
    placed = (
        P("space", "load", None),
        P(None, "space", None, None),
        P("load", None, "space", None, None),
        P("load", None),
        P("load", None, None),
    )
    return jax.shard_map(
        body,
        mesh=mesh,
        in_specs=placed,
        out_specs=(P("load", None, "space", None, None), P("space", "load", None)),
        check_vma=False,
    )
```

profile of v0, /device:TPU:1, one launch (start us, length us, event | category | flops | bytes accessed | tf_op | source)
XLA Modules:
  0.0 102.7 jit_solution(16896769600652009132)
XLA Ops:
  0.6 4.5 %collective-permute-start.4 = (f32[2,8,256]{2,1,0:T(8,128)}, f32[2,8,256]{2,1,0:T(8,128)S(1)}, u32[]{:S(2)}, u32[]{:S(2)}) collective-permute-start(f32[2,8,256]{2,1,0:T(8,128)} %param.5), channel_id=1, source_target_pairs={{0,1},{1,2},{2,3},{3,4},{4,5},{5,6},{6,7},{7,8},{8,9},{9,10},{10,1... | collective-permute-start | bytes 49160 | tf_op jit(solution)/shard_map/ppermute | solution.py:445
  5.1 1.9 %collective-permute-start.5 = (f32[2,8,256]{2,1,0:T(8,128)}, f32[2,8,256]{2,1,0:T(8,128)S(1)}, u32[]{:S(2)}, u32[]{:S(2)}) collective-permute-start(f32[2,8,256]{2,1,0:T(8,128)} %param.5), channel_id=1, source_target_pairs={{1,0},{2,1},{3,2},{4,3},{5,4},{6,5},{7,6},{8,7},{9,8},{10,9},{11,1... | collective-permute-start | bytes 49160 | tf_op jit(solution)/shard_map/ppermute | solution.py:445
  7.1 0.7 fusion
  7.8 1.3 %collective-permute-start.6 = (f32[1,8,256]{2,1,0:T(8,128)S(1)}, f32[1,8,256]{2,1,0:T(8,128)S(1)}, u32[]{:S(2)}, u32[]{:S(2)}) collective-permute-start(f32[1,8,256]{2,1,0:T(8,128)S(1)} %get-tuple-element.22), channel_id=1, source_target_pairs={{2,0},{3,1},{4,2},{5,3},{6,4},{7,5},{8,6},{9,7},{10,8},{11,9},{12,... | collective-permute-start | bytes 24584 | tf_op jit(solution)/shard_map/ppermute | solution.py:445
  9.1 4.0 %collective-permute-start.3 = (f32[1,8,256]{2,1,0:T(8,128)S(1)}, f32[1,8,256]{2,1,0:T(8,128)S(1)}, u32[]{:S(2)}, u32[]{:S(2)}) collective-permute-start(f32[1,8,256]{2,1,0:T(8,128)S(1)} %get-tuple-element.23), channel_id=1, source_target_pairs={{0,2},{1,3},{2,4},{3,5},{4,6},{5,7},{6,8},{7,9},{8,10},{9,11},{10,... | collective-permute-start | bytes 24584 | tf_op jit(solution)/shard_map/ppermute | solution.py:445
  14.3 2.7 %shard_map.68 = (f32[4,3,64,256]{3,2,1,0:T(8,128)}, f32[3,3,64,256]{3,2,1,0:T(8,128)}, f32[1,3,64,256]{3,2,1,0:T(8,128)}) custom-call(s32[4]{0:T(128)} %pad_add_fusion.space_ref.place_ref, f32[3,2,64,256]{3,2,1,0:T(8,128)} %bitcast.7, s32[3,2,64,256]{3,2,1,0:T(8,128)} %fixed_ref.1, s32[1,128]{1,0:T(1,128)} %node_ref.1, f32[3,128]{1,0:T(4,128)} %bitcast.8), custom_call_target="tpu_custom_call" | custom-call | tf_op jit(solution)/shard_map/pallas_call | solution.py:453
  17.1 4.2 %collective-permute-start = (f32[3,3,64,256]{3,2,1,0:T(8,128)}, f32[3,3,64,256]{3,2,1,0:T(8,128)S(1)}, u32[]{:S(2)}, u32[]{:S(2)}) collective-permute-start(f32[3,3,64,256]{3,2,1,0:T(8,128)} %get-tuple-element.13), channel_id=1, source_target_pairs={{0,1},{1,2},{2,3},{3,4},{4,5},{5,6},{6,7},{7,8},{8,9},{9,10},{10,1... | collective-permute-start | bytes 1769480 | tf_op jit(solution)/shard_map/ppermute | solution.py:445
  21.3 1.9 %collective-permute-start.1 = (f32[4,3,64,256]{3,2,1,0:T(8,128)}, f32[4,3,64,256]{3,2,1,0:T(8,128)S(1)}, u32[]{:S(2)}, u32[]{:S(2)}) collective-permute-start(f32[4,3,64,256]{3,2,1,0:T(8,128)} %get-tuple-element.12.own_ref), channel_id=1, source_target_pairs={{1,0},{2,1},{3,2},{4,3},{5,4},{6,5},{7,6},{8,7},{9,8},{10,9},{11,1... | collective-permute-start | bytes 2359304 | tf_op jit(solution)/shard_map/ppermute | solution.py:445
  23.3 0.7 copy-done.6
  24.0 0.9 broadcast_in_dim.6
  24.9 7.6 %all-to-all-start = ((f32[8,8,8,256]{3,2,1,0:T(8,128)}), f32[8,8,8,256]{3,2,1,0:T(8,128)S(1)}, u32[]{:S(2)}, u32[]{:S(2)}) async-start(f32[8,8,8,256]{3,2,1,0:T(8,128)} %broadcast_in_dim.6), calls=%async_computation | async-start | bytes 1048576 | tf_op jit(solution)/shard_map/all_to_all | solution.py:469
  32.5 1.3 %collective-permute-start.2 = (f32[1,3,64,256]{3,2,1,0:T(8,128)S(1)}, f32[1,3,64,256]{3,2,1,0:T(8,128)S(1)}, u32[]{:S(2)}, u32[]{:S(2)}) collective-permute-start(f32[1,3,64,256]{3,2,1,0:T(8,128)S(1)} %copy-done.8), channel_id=1, source_target_pairs={{2,0},{3,1},{4,2},{5,3},{6,4},{7,5},{8,6},{9,7},{10,8},{11,9},{12,... | collective-permute-start | bytes 589832 | tf_op jit(solution)/shard_map/ppermute | solution.py:445
  33.8 6.7 %collective-permute-done.2.far_ref = f32[1,3,64,256]{3,2,1,0:T(8,128)S(1)} collective-permute-done((f32[1,3,64,256]{3,2,1,0:T(8,128)S(1)}, f32[1,3,64,256]{3,2,1,0:T(8,128)S(1)}, u32[]{:S(2)}, u32[]{:S(2)}) %collective-permute-start.2) | collective-permute-done | bytes 196640 | tf_op jit(solution)/shard_map/ppermute | solution.py:445
  40.5 2.2 %all-to-all-done.dens_ref = f32[8,8,8,256]{3,2,1,0:T(8,128)S(1)} async-done(((f32[8,8,8,256]{3,2,1,0:T(8,128)}), f32[8,8,8,256]{3,2,1,0:T(8,128)S(1)}, u32[]{:S(2)}, u32[]{:S(2)}) %all-to-all-start) | async-done | bytes 524320 | tf_op jit(solution)/shard_map/all_to_all | solution.py:469
  42.7 0.8 copy-done
  43.7 0.9 copy-done.1
  44.6 11.5 %shard_map.69 = (f32[5,3,64,256]{3,2,1,0:T(8,128)}, f32[5,3,64,256]{3,2,1,0:T(8,128)}, f32[3,3,64,256]{3,2,1,0:T(8,128)}, f32[3,64,256]{2,1,0:T(8,128)}, f32[8,128]{1,0:T(8,128)}) custom-call(s32[4]{0:T(128)} %pad_add_fusion.space_ref.place_ref, f32[4,3,64,256]{3,2,1,0:T(8,128)} %get-tuple-element.12.own_ref, f32[3,3,64,256]{3,2,1,0:T(8,128)} %copy-done.2, ...), custom_call_target="tpu_custom_call" | custom-call | tf_op jit(solution)/shard_map/pallas_call | solution.py:473
  56.0 2.1 %collective-permute-start.8 = (f32[3,64,256]{2,1,0:T(8,128)}, f32[3,64,256]{2,1,0:T(8,128)S(1)}, u32[]{:S(2)}, u32[]{:S(2)}) collective-permute-start(f32[3,64,256]{2,1,0:T(8,128)} %get-tuple-element.18), channel_id=1, source_target_pairs={{1,0},{2,1},{3,2},{4,3},{5,4},{6,5},{7,6},{8,7},{9,8},{10,9},{11,1... | collective-permute-start | bytes 589832 | tf_op jit(solution)/shard_map/ppermute | solution.py:445
  58.2 5.1 %collective-permute-start.7 = (f32[3,64,256]{2,1,0:T(8,128)}, f32[3,64,256]{2,1,0:T(8,128)S(1)}, u32[]{:S(2)}, u32[]{:S(2)}) collective-permute-start(f32[3,64,256]{2,1,0:T(8,128)} %get-tuple-element.18), channel_id=1, source_target_pairs={{0,1},{1,2},{2,3},{3,4},{4,5},{5,6},{6,7},{7,8},{8,9},{9,10},{10,1... | collective-permute-start | bytes 589832 | tf_op jit(solution)/shard_map/ppermute | solution.py:445
  63.3 0.7 broadcast_in_dim.7
  64.0 17.1 %all_to_all.15.mom_ref = f32[16,8,128]{2,1,0:T(8,128)} all-to-all(f32[16,8,128]{2,1,0:T(8,128)S(1)} %broadcast_in_dim.7), channel_id=1, replica_groups=mesh['load'=8,'space'=16] {'space'}, dimensions={0} | all-to-all | bytes 131072 | tf_op jit(solution)/shard_map/all_to_all | solution.py:484
  81.9 4.6 %shard_map.70 = (f32[3,2,64,256]{3,2,1,0:T(8,128)}, f32[8,40,256]{2,1,0:T(8,128)}) custom-call(f32[5,3,64,256]{3,2,1,0:T(8,128)} %get-tuple-element.15.v0_ref, f32[5,3,64,256]{3,2,1,0:T(8,128)} %get-tuple-element.16.v1_ref, f32[3,3,64,256]{3,2,1,0:T(8,128)} %get-tuple-element.17.v2_ref, f32[3,64,256]{2,1,0:T(8,128)} %copy-done.5, f32[3,64,256]{2,1,0:T(8,128)} %copy-done.4, ...), custom_call_target="tpu_custom_call" | custom-call | tf_op jit(solution)/shard_map/pallas_call | solution.py:485
  86.5 14.3 %all_to_all.16.energy_ref = f32[8,40,256]{2,1,0:T(8,128)} all-to-all(f32[8,40,256]{2,1,0:T(8,128)} %get-tuple-element.21), channel_id=1, replica_groups=mesh['load'=8,'space'=16] {'load'}, dimensions={0} | all-to-all | bytes 655360 | tf_op jit(solution)/shard_map/all_to_all | solution.py:492
  100.8 1.9 %shard_map.71 = f32[2,8,256]{2,1,0:T(8,128)} custom-call(s32[4]{0:T(128)} %pad_add_fusion.space_ref.place_ref, f32[8,40,256]{2,1,0:T(8,128)} %all_to_all.16.energy_ref, f32[8,8,8,256]{3,2,1,0:T(8,128)} %copy-done), custom_call_target="tpu_custom_call" | custom-call | tf_op jit(solution)/shard_map/pallas_call | solution.py:493
  (30 shorter events, 2.2 us)
Async XLA Ops:
  0.6 22.7 %collective-permute-start.4 = (f32[2,8,256]{2,1,0:T(8,128)}, f32[2,8,256]{2,1,0:T(8,128)S(1)}, u32[]{:S(2)}, u32[]{:S(2)}) collective-permute-start(f32[2,8,256]{2,1,0:T(8,128)} %param.5), channel_id=1, source_target_pairs={{0,1},{1,2},{2,3},{3,4},{4,5},{5,6},{6,7},{7,8},{8,9},{9,10},{10,1... | collective-permute-start | bytes 49160 | tf_op jit(solution)/shard_map/ppermute | solution.py:445
  5.1 18.8 %collective-permute-start.5 = (f32[2,8,256]{2,1,0:T(8,128)}, f32[2,8,256]{2,1,0:T(8,128)S(1)}, u32[]{:S(2)}, u32[]{:S(2)}) collective-permute-start(f32[2,8,256]{2,1,0:T(8,128)} %param.5), channel_id=1, source_target_pairs={{1,0},{2,1},{3,2},{4,3},{5,4},{6,5},{7,6},{8,7},{9,8},{10,9},{11,1... | collective-permute-start | bytes 49160 | tf_op jit(solution)/shard_map/ppermute | solution.py:445
  7.8 16.2 %collective-permute-start.6 = (f32[1,8,256]{2,1,0:T(8,128)S(1)}, f32[1,8,256]{2,1,0:T(8,128)S(1)}, u32[]{:S(2)}, u32[]{:S(2)}) collective-permute-start(f32[1,8,256]{2,1,0:T(8,128)S(1)} %get-tuple-element.22), channel_id=1, source_target_pairs={{2,0},{3,1},{4,2},{5,3},{6,4},{7,5},{8,6},{9,7},{10,8},{11,9},{12,... | collective-permute-start | bytes 24584 | tf_op jit(solution)/shard_map/ppermute | solution.py:445
  9.1 12.2 %collective-permute-start.3 = (f32[1,8,256]{2,1,0:T(8,128)S(1)}, f32[1,8,256]{2,1,0:T(8,128)S(1)}, u32[]{:S(2)}, u32[]{:S(2)}) collective-permute-start(f32[1,8,256]{2,1,0:T(8,128)S(1)} %get-tuple-element.23), channel_id=1, source_target_pairs={{0,2},{1,3},{2,4},{3,5},{4,6},{5,7},{6,8},{7,9},{8,10},{9,11},{10,... | collective-permute-start | bytes 24584 | tf_op jit(solution)/shard_map/ppermute | solution.py:445
  13.1 0.7 copy-start.7
  17.1 25.6 %collective-permute-start = (f32[3,3,64,256]{3,2,1,0:T(8,128)}, f32[3,3,64,256]{3,2,1,0:T(8,128)S(1)}, u32[]{:S(2)}, u32[]{:S(2)}) collective-permute-start(f32[3,3,64,256]{3,2,1,0:T(8,128)} %get-tuple-element.13), channel_id=1, source_target_pairs={{0,1},{1,2},{2,3},{3,4},{4,5},{5,6},{6,7},{7,8},{8,9},{9,10},{10,1... | collective-permute-start | bytes 1769480 | tf_op jit(solution)/shard_map/ppermute | solution.py:445
  21.3 21.4 %collective-permute-start.1 = (f32[4,3,64,256]{3,2,1,0:T(8,128)}, f32[4,3,64,256]{3,2,1,0:T(8,128)S(1)}, u32[]{:S(2)}, u32[]{:S(2)}) collective-permute-start(f32[4,3,64,256]{3,2,1,0:T(8,128)} %get-tuple-element.12.own_ref), channel_id=1, source_target_pairs={{1,0},{2,1},{3,2},{4,3},{5,4},{6,5},{7,6},{8,7},{9,8},{10,9},{11,1... | collective-permute-start | bytes 2359304 | tf_op jit(solution)/shard_map/ppermute | solution.py:445
  23.3 0.7 copy-start.6
  24.9 7.6 %copy-start.8 = (f32[1,3,64,256]{3,2,1,0:T(8,128)S(1)}, f32[1,3,64,256]{3,2,1,0:T(8,128)}, u32[]{:S(2)}) copy-start(f32[1,3,64,256]{3,2,1,0:T(8,128)} %get-tuple-element.14) | copy-start | bytes 589828
  24.9 17.8 %all-to-all-start = ((f32[8,8,8,256]{3,2,1,0:T(8,128)}), f32[8,8,8,256]{3,2,1,0:T(8,128)S(1)}, u32[]{:S(2)}, u32[]{:S(2)}) async-start(f32[8,8,8,256]{3,2,1,0:T(8,128)} %broadcast_in_dim.6), calls=%async_computation | async-start | bytes 1048576 | tf_op jit(solution)/shard_map/all_to_all | solution.py:469
  32.5 8.0 %collective-permute-start.2 = (f32[1,3,64,256]{3,2,1,0:T(8,128)S(1)}, f32[1,3,64,256]{3,2,1,0:T(8,128)S(1)}, u32[]{:S(2)}, u32[]{:S(2)}) collective-permute-start(f32[1,3,64,256]{3,2,1,0:T(8,128)S(1)} %copy-done.8), channel_id=1, source_target_pairs={{2,0},{3,1},{4,2},{5,3},{6,4},{7,5},{8,6},{9,7},{10,8},{11,9},{12,... | collective-permute-start | bytes 589832 | tf_op jit(solution)/shard_map/ppermute | solution.py:445
  40.5 2.2 %copy-start.3 = (f32[1,3,64,256]{3,2,1,0:T(8,128)}, f32[1,3,64,256]{3,2,1,0:T(8,128)S(1)}, u32[]{:S(2)}) copy-start(f32[1,3,64,256]{3,2,1,0:T(8,128)S(1)} %collective-permute-done.2.far_ref) | copy-start | bytes 589828
  42.7 0.8 copy-start
  42.7 1.0 copy-start.2
  43.7 0.9 copy-start.1
  56.0 25.1 %collective-permute-start.8 = (f32[3,64,256]{2,1,0:T(8,128)}, f32[3,64,256]{2,1,0:T(8,128)S(1)}, u32[]{:S(2)}, u32[]{:S(2)}) collective-permute-start(f32[3,64,256]{2,1,0:T(8,128)} %get-tuple-element.18), channel_id=1, source_target_pairs={{1,0},{2,1},{3,2},{4,3},{5,4},{6,5},{7,6},{8,7},{9,8},{10,9},{11,1... | collective-permute-start | bytes 589832 | tf_op jit(solution)/shard_map/ppermute | solution.py:445
  58.2 23.0 %collective-permute-start.7 = (f32[3,64,256]{2,1,0:T(8,128)}, f32[3,64,256]{2,1,0:T(8,128)S(1)}, u32[]{:S(2)}, u32[]{:S(2)}) collective-permute-start(f32[3,64,256]{2,1,0:T(8,128)} %get-tuple-element.18), channel_id=1, source_target_pairs={{0,1},{1,2},{2,3},{3,4},{4,5},{5,6},{6,7},{7,8},{8,9},{9,10},{10,1... | collective-permute-start | bytes 589832 | tf_op jit(solution)/shard_map/ppermute | solution.py:445
  81.2 0.7 copy-start.4
  81.2 0.7 copy-start.5
where the time goes:
time: 104 us; the launch traced here: 103 us
  starting transfers between devices  34 us (33%)
  blocking collectives  31.4 us (30%)
  Pallas kernels  20.7 us (20%)
  waiting for transfers between devices  8.9 us (9%)
  local copies, waits for them, and re-layouts  6.16 us (6%)
    ppermute x9, starting transfers between devices, shifted(): return lax.ppermute(array, axis, route)  26.4 us
    all_to_all x1, blocking collectives, body(): lax.all_to_all(jnp.broadcast_to(mom[None], (n_space,) + mom.shape), 'spac...  17.1 us
    all_to_all x1, blocking collectives, body(): energy = lax.all_to_all(energy, 'load', 0, 0)  14.3 us
    pallas_call x1, Pallas kernels, body(): kernel_call(krylov_kernel, [(5,) + plane, (5,) + plane, (3,) + plane, pla...  11.5 us
    all_to_all x1, starting transfers between devices, body(): lax.all_to_all(jnp.broadcast_to(dens[None], (n_load,) + dens.shape), 'loa...  7.64 us
    ppermute x9, waiting for transfers between devices, shifted(): return lax.ppermute(array, axis, route)  6.7 us
    pallas_call x1, Pallas kernels, body(): kernel_call(energy_kernel, [(3, CX, NY, NZ), (CHUNKS, 4 * (ROWS + 2), NZ)...  4.63 us
    unnamed x23, local copies, waits for them, and re-layouts  3.89 us
  transfers between devices with their start and end apart: 10, of which 2 were waited for; matrix products, arithmetic and copies ran while one was open for 3% of the time, Pallas kernels for 3%

commit v1 on v0

--- a/solution.py
+++ b/solution.py
@@ -187,9 +187,11 @@
         partial, low = to_high, high
 
 
-def loads_kernel(space_ref, body_ref, fixed_ref, node_ref, force_ref, all_ref, right_ref, far_ref):
+def loads_kernel(
+    body_ref, fixed_ref, node_ref, force_ref, load_ref, keep_ref, right_ref, left_ref
+):
     cells = CX * NY * NZ
-    local = node_ref[...] - space_ref[0] * cells
+    local = node_ref[...] - lax.axis_index("space") * cells
     valid = (local >= 0) & (local < cells)
     local = jnp.where(valid, local, -1)
     line = lax.shift_right_arithmetic(local, ZBITS)
@@ -210,126 +212,168 @@
             keep = 1.0 - fixed_ref[comp, plane].astype(F32)
             first = (comp * CX + plane) * NY
             load = keep * (body_ref[comp, plane] + added[first : first + NY])
-            all_ref[plane, comp] = load
-            right_ref[plane, comp] = load
-            all_ref[3 - plane, comp] = keep
+            load_ref[plane, comp] = load
+            keep_ref[plane, comp] = keep
+            left_ref[plane, comp] = load
             if plane == 0:
-                far_ref[0, comp] = load
+                left_ref[2, comp] = keep
             else:
-                right_ref[2, comp] = keep
-
-
-def krylov_kernel(
-    space_ref, own_ref, left_ref, right_ref, far_ref, dens_ref,
-    v0_ref, v1_ref, v2_ref, edge_ref, mom_ref,
-    e_ref, inv_ref, zs0, zd0, zs1, zd1, zs2, zd2, carry1, carry2,
+                right_ref[0, comp] = load
+                right_ref[1, comp] = keep
+
+
+def clear_tails(refs):
+    for ref in refs:
+        for plane in range(ref.shape[0]):
+            for comp in range(3):
+                ref[plane, comp, NY : NY + ROWS] = jnp.zeros((ROWS, NZ), F32)
+
+
+def clear_carry(ref):
+    for plane in range(ref.shape[0]):
+        for comp in range(3):
+            ref[plane, comp] = jnp.zeros((ROWS, NZ), F32)
+
+
+def folded(values):
+    rows = [jnp.sum(v[:, :128] + v[:, 128:], axis=0, keepdims=True) for v in values]
+    return jnp.concatenate(rows, axis=0)
+
+
+def advance(forces, kept, before, inverse):
+    image = jnp.where(kept, forces, before)
+    return image, jnp.where(kept, forces * inverse, before)
+
+
+def first_kernel(
+    load_ref, keep_ref, left_ref, right_ref, dens_ref,
+    v0_ref, v1_ref, v1_far_ref, e_ref, inv_ref, mom_ref,
+    zs, zd, carry,
 ):
-    first_x = space_ref[0] * CX
-    limit = space_ref[1] * CX
-    zero_rows = jnp.zeros((ROWS, NZ), F32)
-    for plane in range(8):
-        at = first_x - 3 + plane
+    first_x = lax.axis_index("space") * CX
+    limit = lax.axis_size("space") * CX
+    for plane in range(6):
+        at = first_x - 2 + plane
         scale = jnp.where((at >= 0) & (at < limit), 1.0, 0.0).astype(F32)
-        e_ref[plane, 0:ROWS] = zero_rows
+        e_ref[plane, 0:ROWS] = jnp.zeros((ROWS, NZ), F32)
         for block in range(CHUNKS):
             dens = dens_ref[block, plane]
             rows = slice((block + 1) * ROWS, (block + 2) * ROWS)
             e_ref[plane, rows] = scale * (EMIN + (1.0 - EMIN) * (dens * dens * dens))
-    tail = slice(NY, NY + ROWS)
-    for comp in range(3):
-        for refs, planes in (((zs0, zd0), 7), ((zs1, zd1), 5), ((zs2, zd2), 3)):
-            for ref in refs:
-                for plane in range(planes):
-                    ref[plane, comp, tail] = zero_rows
-        for ref, planes in ((carry1, 5), (carry2, 3)):
-            for plane in range(planes):
-                ref[plane, comp] = zero_rows
-
-    loads = [left_ref.at[0], left_ref.at[1], own_ref.at[0], own_ref.at[1],
-             right_ref.at[0], right_ref.at[1], far_ref.at[0]]
-    keeps = [left_ref.at[2], own_ref.at[3], own_ref.at[2], right_ref.at[3], right_ref.at[2]]
+    clear_tails([zs, zd])
+    clear_carry(carry)
+    loads = [left_ref.at[0], load_ref.at[0], load_ref.at[1], right_ref.at[0], right_ref.at[1]]
+    keeps = [keep_ref.at[0], keep_ref.at[1], right_ref.at[2]]
+    zero = jnp.zeros((ROWS, NZ), F32)
 
     def start(chunk, total):
         here = rows_at(chunk)
         last = row_ids((ROWS, NZ)) == ROWS - 1
-        for plane in range(7):
+        for plane in range(5):
             cur = e_ref[plane, rows_at(chunk + 1)] + e_ref[plane + 1, rows_at(chunk + 1)]
             before = e_ref[plane, rows_at(chunk)] + e_ref[plane + 1, rows_at(chunk)]
             cur = cur + pltpu.roll(jnp.where(last, before, cur), 1, 0)
             diag = KDIAG * (cur + from_below(cur))
             inverse = 1.0 / jnp.where(diag > 0.0, diag, 1.0)
-            if 1 <= plane <= 5:
-                inv_ref[plane - 1, here] = inverse
+            if plane < 4:
+                inv_ref[plane, here] = inverse
             for comp in range(3):
                 load = loads[plane][comp, here]
                 value = load * inverse
-                if 1 <= plane <= 5:
-                    v0_ref[plane - 1, comp, here] = value
-                if plane in (2, 3):
+                if plane < 3:
+                    v0_ref[plane, comp, here] = value
+                if plane in (1, 2):
                     total = total + load * value
-                store_z_modes(zs0, zd0, plane, comp, here, value)
+                store_z_modes(zs, zd, plane, comp, here, value)
         return total
 
-    zero = jnp.zeros((ROWS, NZ), F32)
     mom0 = lax.fori_loop(0, CHUNKS, start, zero)
 
-    def first(chunk, totals):
+    def apply(chunk, totals):
         here = rows_at(chunk)
         odd, even = totals
-        for plane, forces in apply_rows(zs0, zd0, 7, e_ref, 1, 1, carry1, chunk):
+        for plane, forces in apply_rows(zs, zd, 5, e_ref, 1, 1, carry, chunk):
+            inverse = inv_ref[plane, here]
+            for comp in range(3):
+                kept = keeps[plane - 1][comp, here] > 0.0
+                before = loads[plane][comp, here] * inverse
+                image, value = advance(forces[comp], kept, before, inverse)
+                if plane < 3:
+                    v1_ref[plane - 1, comp, here] = value
+                    odd = odd + before * image
+                    even = even + value * image
+                else:
+                    v1_far_ref[comp, here] = value
+        return odd, even
+
+    mom1, mom2 = lax.fori_loop(0, CHUNKS, apply, (zero, zero))
+    mom_ref[...] = folded([mom0, mom1, mom2] + [zero] * 5)
+
+
+def second_kernel(
+    v1_left_ref, v1_ref, v1_far_ref, keep_left_ref, keep_ref, e_ref, inv_ref, sofar_ref,
+    v2_ref, mom_ref,
+    zs, zd, zs2, zd2, carry,
+):
+    v1_planes = [v1_left_ref.at[0], v1_left_ref.at[1], v1_ref.at[0], v1_ref.at[1], v1_far_ref]
+    keeps = [keep_left_ref.at[1], keep_ref.at[0], keep_ref.at[1]]
+    clear_tails([zs, zd, zs2, zd2])
+    clear_carry(carry)
+    zero = jnp.zeros((ROWS, NZ), F32)
+
+    def start(chunk, done):
+        here = rows_at(chunk)
+        for plane in range(5):
+            for comp in range(3):
+                store_z_modes(zs, zd, plane, comp, here, v1_planes[plane][comp, here])
+        return done
+
+    lax.fori_loop(0, CHUNKS, start, 0)
+
+    def apply(chunk, totals):
+        here = rows_at(chunk)
+        odd, even = totals
+        for plane, forces in apply_rows(zs, zd, 5, e_ref, 0, 1, carry, chunk):
             inverse = inv_ref[plane - 1, here]
             for comp in range(3):
                 kept = keeps[plane - 1][comp, here] > 0.0
-                before = v0_ref[plane - 1, comp, here]
-                image = jnp.where(kept, forces[comp], before)
-                value = jnp.where(kept, forces[comp] * inverse, before)
-                v1_ref[plane - 1, comp, here] = value
-                store_z_modes(zs1, zd1, plane - 1, comp, here, value)
-                if plane in (2, 3):
+                before = v1_planes[plane][comp, here]
+                image, value = advance(forces[comp], kept, before, inverse)
+                v2_ref[plane - 1, comp, here] = value
+                store_z_modes(zs2, zd2, plane - 1, comp, here, value)
+                if plane > 1:
                     odd = odd + before * image
                     even = even + value * image
         return odd, even
 
-    mom1, mom2 = lax.fori_loop(0, CHUNKS, first, (zero, zero))
-
-    def second(chunk, totals):
-        here = rows_at(chunk)
-        odd, even = totals
-        for plane, forces in apply_rows(zs1, zd1, 5, e_ref, 2, 1, carry2, chunk):
-            inverse = inv_ref[plane, here]
-            for comp in range(3):
-                kept = keeps[plane][comp, here] > 0.0
-                before = v1_ref[plane, comp, here]
-                image = jnp.where(kept, forces[comp], before)
-                value = jnp.where(kept, forces[comp] * inverse, before)
-                v2_ref[plane - 1, comp, here] = value
-                if plane == 2:
-                    edge_ref[comp, here] = value
-                store_z_modes(zs2, zd2, plane - 1, comp, here, value)
-                if plane in (1, 2):
-                    odd = odd + before * image
-                    even = even + value * image
-        return odd, even
-
-    mom3, mom4 = lax.fori_loop(0, CHUNKS, second, (zero, zero))
-
-    def third(chunk, total):
-        low = plane_modes(zs2, zd2, 0, chunk)
-        for plane in range(2):
-            high = plane_modes(zs2, zd2, plane + 1, chunk)
-            energy = element_energy(element_modes(low, high))
-            total = total + e_ref[3 + plane, rows_at(chunk + 1)] * energy
-            low = high
+    mom3, mom4 = lax.fori_loop(0, CHUNKS, apply, (zero, zero))
+    at_end = end_flag()
+
+    def last(chunk, total):
+        for plane, energy in enumerate(energies(zs2, zd2, chunk)):
+            total = total + (e_ref[1 + plane, rows_at(chunk + 1)] * energy) * (at_end if plane == 2 else 1.0)
         return total
 
-    mom5 = lax.fori_loop(0, CHUNKS, third, zero)
-    rows = []
-    for value in (mom0, mom1, mom2, mom3, mom4, mom5, zero, zero):
-        rows.append(jnp.sum(value[:, :128] + value[:, 128:], axis=0, keepdims=True))
-    mom_ref[...] = jnp.concatenate(rows, axis=0)
-
-
-def energy_kernel(v0_ref, v1_ref, v2_ref, left_ref, right_ref, mom_ref, u_ref, out_ref, zs, zd, e_ref):
+    mom5 = lax.fori_loop(0, CHUNKS, last, zero)
+    total = sofar_ref[...] + folded([zero] * 3 + [mom3, mom4, mom5] + [zero] * 2)
+    for device in range(mom_ref.shape[0]):
+        mom_ref[device] = total
+
+
+def end_flag():
+    at_end = lax.axis_index("space") == lax.axis_size("space") - 1
+    return jnp.where(at_end, 1.0, 0.0).astype(F32)
+
+
+def energies(zs, zd, chunk):
+    planes = [plane_modes(zs, zd, plane, chunk) for plane in range(3)]
+    zero = {pair: jnp.zeros((ROWS, NZ), F32) for pair in PAIRS}
+    planes.append([zero] * 3)
+    for low, high in zip(planes[:-1], planes[1:]):
+        yield element_energy(element_modes(low, high))
+
+
+def energy_kernel(v0_ref, v1_left_ref, v1_ref, v2_ref, mom_ref, u_ref, out_ref, zs, zd, e_ref):
     total = mom_ref[0]
     for device in range(1, mom_ref.shape[0]):
         total = total + mom_ref[device]
@@ -351,41 +395,35 @@
     c0 = m0 / m1 - low10 * c1 - low20 * c2
     c0, c1, c2 = [jnp.broadcast_to(jnp.concatenate([c, c], axis=1), (ROWS, NZ)) for c in (c0, c1, c2)]
 
-    zero_rows = jnp.zeros((ROWS, NZ), F32)
-    for plane in range(5):
-        for comp in range(3):
-            zs[plane, comp, NY : NY + ROWS] = zero_rows
-            zd[plane, comp, NY : NY + ROWS] = zero_rows
-    for plane in range(4):
-        e_ref[plane, 0:ROWS] = zero_rows
-        e_ref[plane, NY + ROWS : NY + 2 * ROWS] = zero_rows
-    v2_planes = [left_ref, v2_ref.at[0], v2_ref.at[1], v2_ref.at[2], right_ref]
+    clear_tails([zs, zd])
+    for plane in range(3):
+        e_ref[plane, 0:ROWS] = jnp.zeros((ROWS, NZ), F32)
+        e_ref[plane, NY + ROWS : NY + 2 * ROWS] = jnp.zeros((ROWS, NZ), F32)
+    v1_planes = [v1_left_ref.at[1], v1_ref.at[0], v1_ref.at[1]]
 
     def combine(chunk, done):
         here = rows_at(chunk)
-        for plane in range(5):
-            for comp in range(3):
-                value = c0 * v0_ref[plane, comp, here] + c1 * v1_ref[plane, comp, here]
-                value = value + c2 * v2_planes[plane][comp, here]
-                if plane in (1, 2):
+        for plane in range(3):
+            for comp in range(3):
+                value = c0 * v0_ref[plane, comp, here] + c1 * v1_planes[plane][comp, here]
+                value = value + c2 * v2_ref[plane, comp, here]
+                if plane > 0:
                     u_ref[comp, plane - 1, here] = value
                 store_z_modes(zs, zd, plane, comp, here, value)
         return done
 
     lax.fori_loop(0, CHUNKS, combine, 0)
+    at_end = end_flag()
 
     def measure(chunk, done):
-        low = plane_modes(zs, zd, 0, chunk)
-        for plane in range(4):
-            high = plane_modes(zs, zd, plane + 1, chunk)
-            e_ref[plane, rows_at(chunk + 1)] = element_energy(element_modes(low, high))
-            low = high
+        for plane, energy in enumerate(energies(zs, zd, chunk)):
+            e_ref[plane, rows_at(chunk + 1)] = energy * (at_end if plane == 2 else 1.0)
         return done
 
     lax.fori_loop(0, CHUNKS, measure, 0)
     span = ROWS + 2
     for block in range(CHUNKS):
-        for plane in range(4):
+        for plane in range(3):
             first = ROWS - 1 + block * ROWS
             out_ref[block, plane * span : (plane + 1) * span] = e_ref[plane, first : first + span]
 
@@ -405,12 +443,17 @@
     return [full[k] + cross[k - 1] + cross[k + 1] for k in range(1, 1 + CX)]
 
 
-def filter_kernel(place_ref, energy_ref, dens_ref, out_ref):
-    space, n_space, load, n_load = [place_ref[k] for k in range(4)]
-    total = energy_ref[0]
-    for block in range(1, energy_ref.shape[0]):
-        total = total + energy_ref[block]
+def filter_kernel(energy_ref, next_ref, dens_ref, out_ref):
+    space, load = lax.axis_index("space"), lax.axis_index("load")
+    n_space, n_load = lax.axis_size("space"), lax.axis_size("load")
     span = ROWS + 2
+    part = lambda ref, k: ref[k * span : (k + 1) * span]
+    total = [
+        part(energy_ref, 0),
+        part(energy_ref, 1),
+        part(energy_ref, 2) + part(next_ref, 0),
+        part(next_ref, 1),
+    ]
     before = jnp.maximum(load - 1, 0)
     after = jnp.minimum(load + 1, n_load - 1)
     at_y = load * ROWS - 1 + row_ids((span, NZ))
@@ -419,17 +462,16 @@
     for plane in range(4):
         dens = jnp.concatenate(
             [
-                dens_ref[before, 2 + plane][ROWS - 1 : ROWS],
-                dens_ref[load, 2 + plane],
-                dens_ref[after, 2 + plane][0:1],
+                dens_ref[before, 1 + plane][ROWS - 1 : ROWS],
+                dens_ref[load, 1 + plane],
+                dens_ref[after, 1 + plane][0:1],
             ],
             axis=0,
         )
         at_x = space * CX - 1 + plane
         scale = jnp.where((at_x >= 0) & (at_x < n_space * CX), 1.0, 0.0).astype(F32)
         present = scale * jnp.where(in_y, 1.0, 0.0)
-        energy = total[plane * span : (plane + 1) * span]
-        sensitivity = -PENALTY * (1.0 - EMIN) * (dens * dens) * energy
+        sensitivity = -PENALTY * (1.0 - EMIN) * (dens * dens) * total[plane]
         weighted.append(present * (dens * sensitivity))
         inside.append(present)
         if 1 <= plane <= CX:
@@ -447,50 +489,47 @@
 
 def body(density, fixed_dofs, body_loads, point_nodes, point_forces):
     n_load, n_space = lax.axis_size("load"), lax.axis_size("space")
-    load, space = lax.axis_index("load"), lax.axis_index("space")
-    place = jnp.stack([space, jnp.int32(n_space), load, jnp.int32(n_load)]).astype(jnp.int32)
+    dens = jnp.concatenate(
+        [shifted(density, "space", 1), density, shifted(density, "space", -1)], axis=0
+    )
     plane = (3, NY, NZ)
-    own, to_right, to_far = kernel_call(
-        loads_kernel, [(4,) + plane, (3,) + plane, (1,) + plane], 1, 4
-    )(place, body_loads[0], fixed_dofs, point_nodes, point_forces[0])
-    dens = jnp.concatenate(
-        [
-            shifted(density[1:2], "space", 2),
-            shifted(density, "space", 1),
-            density,
-            shifted(density, "space", -1),
-            shifted(density[0:1], "space", -2),
-        ],
-        axis=0,
-    )
+    load, keep, to_right, to_left = kernel_call(
+        loads_kernel, [(2,) + plane, (2,) + plane, (2,) + plane, (3,) + plane], 0, 4
+    )(body_loads[0], fixed_dofs, point_nodes, point_forces[0])
     left = shifted(to_right, "space", 1)
-    right = shifted(own, "space", -1)
-    far = shifted(to_far, "space", -2)
+    right = shifted(to_left, "space", -1)
     dens = lax.all_to_all(jnp.broadcast_to(dens[None], (n_load,) + dens.shape), "load", 0, 0)
 
     padded = (NY + ROWS, NZ)
     zed = lambda planes: pltpu.VMEM((planes, 3) + padded, F32)
-    v0, v1, v2, edge, mom = kernel_call(
-        krylov_kernel,
-        [(5,) + plane, (5,) + plane, (3,) + plane, plane, (8, 128)],
-        1,
+    carry = pltpu.VMEM((3, 3, ROWS, NZ), F32)
+    v0, v1, v1_far, modulus, inverse, mom = kernel_call(
+        first_kernel,
+        [(3,) + plane, (2,) + plane, plane, (6,) + padded, (4, NY, NZ), (8, 128)],
+        0,
         5,
-        [pltpu.VMEM((8,) + padded, F32), pltpu.VMEM((5, NY, NZ), F32)]
-        + [zed(7), zed(7), zed(5), zed(5), zed(3), zed(3)]
-        + [pltpu.VMEM((5, 3, ROWS, NZ), F32), pltpu.VMEM((3, 3, ROWS, NZ), F32)],
-    )(place, own, left, right, far, dens)
-    edge_left = shifted(edge, "space", 1)
-    edge_right = shifted(edge, "space", -1)
-    mom = lax.all_to_all(jnp.broadcast_to(mom[None], (n_space,) + mom.shape), "space", 0, 0)
+        [zed(5), zed(5), carry],
+    )(load, keep, left, right, dens)
+    v1_left = shifted(v1, "space", 1)
+    v2, mom = kernel_call(
+        second_kernel,
+        [(3,) + plane, (n_space, 8, 128)],
+        0,
+        8,
+        [zed(5), zed(5), zed(3), zed(3), carry],
+    )(v1_left, v1, v1_far, left, keep, modulus, inverse, mom)
+    mom = lax.all_to_all(mom, "space", 0, 0)
+    span = ROWS + 2
     moved, energy = kernel_call(
         energy_kernel,
-        [(3, CX, NY, NZ), (CHUNKS, 4 * (ROWS + 2), NZ)],
+        [(3, CX, NY, NZ), (CHUNKS, 3 * span, NZ)],
         0,
-        6,
-        [zed(5), zed(5), pltpu.VMEM((4, NY + 2 * ROWS, NZ), F32)],
-    )(v0, v1, v2, edge_left, edge_right, mom)
-    energy = lax.all_to_all(energy, "load", 0, 0)
-    (filtered,) = kernel_call(filter_kernel, [(CX, ROWS, NZ)], 1, 2)(place, energy, dens)
+        5,
+        [zed(3), zed(3), pltpu.VMEM((3, NY + 2 * ROWS, NZ), F32)],
+    )(v0, v1_left, v1, v2, mom)
+    energy = jnp.sum(lax.all_to_all(energy, "load", 0, 0), axis=0)
+    following = shifted(energy[: 2 * span], "space", -1)
+    (filtered,) = kernel_call(filter_kernel, [(CX, ROWS, NZ)], 0, 3)(energy, following, dens)
     return (moved[None], filtered)
 
 

time: 104 us -> 95 us (0.913)
  starting transfers between devices: 34 us -> 17 us
  blocking collectives: 31.4 us -> 44.3 us
  local copies, waits for them, and re-layouts: 6.16 us -> 3.62 us
  waiting for transfers between devices: 8.9 us -> 7.41 us
    all_to_all x2 -> x3, blocking collectives: 31.4 us -> 44.3 us  [the longest x1 19.2 us: body(): lax.all_to_all(jnp.broadcast_to(dens[None], (n_load,) + dens.shape), 'loa...]
    ppermute x9 -> x6, starting transfers between devices: 26.4 us -> 17 us  [shifted(): return lax.ppermute(array, axis, route)]
    all_to_all x1 -> x0, starting transfers between devices: 7.64 us -> none  [body(): lax.all_to_all(jnp.broadcast_to(dens[None], (n_load,) + dens.shape), 'loa...]
    all_to_all x1 -> x0, waiting for transfers between devices: 2.2 us -> none  [body(): lax.all_to_all(jnp.broadcast_to(dens[None], (n_load,) + dens.shape), 'loa...]
    ppermute x9 -> x6, waiting for transfers between devices: 6.7 us -> 7.41 us  [shifted(): return lax.ppermute(array, axis, route)]
    pallas_call x4 -> x5, Pallas kernels: 20.7 us -> 21.2 us  [the longest x1 6.64 us: body(): kernel_call(second_kernel, [(3,) + plane, (n_space, 8, 128)], 0, 8, [zed(...]
    unnamed x23 -> x13, local copies, waits for them, and re-layouts: 3.89 us -> 3.59 us
  transfers between devices with their start and end apart: 10 -> 6, of which waited for: 2 -> 3; matrix products, arithmetic and copies ran while one was open for 3% -> 0% of each run, Pallas kernels for 3% -> 0%
where the time goes in v1:
time: 95 us; the launch traced here: 94.4 us
  blocking collectives  44.3 us (47%)
  Pallas kernels  21.2 us (22%)
  starting transfers between devices  17 us (18%)
  waiting for transfers between devices  7.41 us (8%)
  local copies, waits for them, and re-layouts  3.62 us (4%)
    all_to_all x1, blocking collectives, body(): lax.all_to_all(jnp.broadcast_to(dens[None], (n_load,) + dens.shape), 'loa...  19.2 us
    ppermute x6, starting transfers between devices, shifted(): return lax.ppermute(array, axis, route)  17 us
    all_to_all x1, blocking collectives, body(): mom = lax.all_to_all(mom, 'space', 0, 0)  13.3 us
    all_to_all x1, blocking collectives, body(): energy = jnp.sum(lax.all_to_all(energy, 'load', 0, 0), axis=0)  11.8 us
    ppermute x6, waiting for transfers between devices, shifted(): return lax.ppermute(array, axis, route)  7.41 us
    pallas_call x1, Pallas kernels, body(): kernel_call(second_kernel, [(3,) + plane, (n_space, 8, 128)], 0, 8, [zed(...  6.64 us
    pallas_call x1, Pallas kernels, body(): kernel_call(first_kernel, [(3,) + plane, (2,) + plane, plane, (6,) + padd...  6.18 us
    pallas_call x1, Pallas kernels, body(): kernel_call(energy_kernel, [(3, CX, NY, NZ), (CHUNKS, 3 * span, NZ)], 0,...  3.88 us
  transfers between devices with their start and end apart: 6, of which 3 were waited for; matrix products, arithmetic and copies ran while one was open for 0% of the time, Pallas kernels for 0%

profile of v1, /device:TPU:1, one launch (start us, length us, event | category | flops | bytes accessed | tf_op | source)
XLA Modules:
  0.0 94.4 jit_solution(16114498566033870894)
XLA Ops:
  0.6 1.3 %copy.9 = f32[1,3,128]{2,1,0:T(4,128)} copy(f32[1,3,128]{2,0,1:T(1,128)} %param.9) | data formatting | bytes 3072
  1.9 2.8 %shard_map.68 = (f32[2,3,64,256]{3,2,1,0:T(8,128)}, f32[2,3,64,256]{3,2,1,0:T(8,128)}, f32[2,3,64,256]{3,2,1,0:T(8,128)}, f32[3,3,64,256]{3,2,1,0:T(8,128)}) custom-call(f32[3,2,64,256]{3,2,1,0:T(8,128)} %bitcast.5, s32[3,2,64,256]{3,2,1,0:T(8,128)} %fixed_ref.1, s32[1,128]{1,0:T(1,128)} %node_ref.1, f32[3,128]{1,0:T(4,128)} %bitcast.6), custom_call_target="tpu_custom_call" | custom-call | tf_op jit(solution)/shard_map/pallas_call | solution.py:496
  4.6 3.3 %collective-permute-start.1 = (f32[3,3,64,256]{3,2,1,0:T(8,128)}, f32[3,3,64,256]{3,2,1,0:T(8,128)S(1)}, u32[]{:S(2)}, u32[]{:S(2)}) collective-permute-start(f32[3,3,64,256]{3,2,1,0:T(8,128)} %get-tuple-element.19), channel_id=1, source_target_pairs={{1,0},{2,1},{3,2},{4,3},{5,4},{6,5},{7,6},{8,7},{9,8},{10,9},{11,1... | collective-permute-start | bytes 1769480 | tf_op jit(solution)/shard_map/ppermute | solution.py:487
  8.0 3.1 %collective-permute-start.2 = (f32[2,8,256]{2,1,0:T(8,128)S(1)}, f32[2,8,256]{2,1,0:T(8,128)S(1)}, u32[]{:S(2)}, u32[]{:S(2)}) collective-permute-start(f32[2,8,256]{2,1,0:T(8,128)S(1)} %copy-done.5), channel_id=1, source_target_pairs={{0,1},{1,2},{2,3},{3,4},{4,5},{5,6},{6,7},{7,8},{8,9},{9,10},{10,1... | collective-permute-start | bytes 49160 | tf_op jit(solution)/shard_map/ppermute | solution.py:487
  11.1 1.9 %collective-permute-start.3 = (f32[2,8,256]{2,1,0:T(8,128)S(1)}, f32[2,8,256]{2,1,0:T(8,128)S(1)}, u32[]{:S(2)}, u32[]{:S(2)}) collective-permute-start(f32[2,8,256]{2,1,0:T(8,128)S(1)} %copy-done.5), channel_id=1, source_target_pairs={{1,0},{2,1},{3,2},{4,3},{5,4},{6,5},{7,6},{8,7},{9,8},{10,9},{11,1... | collective-permute-start | bytes 49160 | tf_op jit(solution)/shard_map/ppermute | solution.py:487
  13.0 3.6 %collective-permute-start = (f32[2,3,64,256]{3,2,1,0:T(8,128)}, f32[2,3,64,256]{3,2,1,0:T(8,128)S(1)}, u32[]{:S(2)}, u32[]{:S(2)}) collective-permute-start(f32[2,3,64,256]{3,2,1,0:T(8,128)} %get-tuple-element.18), channel_id=1, source_target_pairs={{0,1},{1,2},{2,3},{3,4},{4,5},{5,6},{6,7},{7,8},{8,9},{9,10},{10,1... | collective-permute-start | bytes 1179656 | tf_op jit(solution)/shard_map/ppermute | solution.py:487
  16.7 0.0 collective-permute-done.2
  16.7 0.4 collective-permute-done.3
  17.1 19.2 %all_to_all.15.dens_ref = f32[8,6,8,256]{3,2,1,0:T(8,128)} all-to-all(f32[8,6,8,256]{3,2,1,0:T(8,128)S(1)} %broadcast_in_dim.4), channel_id=1, replica_groups=mesh['load'=8,'space'=16] {'load'}, dimensions={0} | all-to-all | bytes 786432 | tf_op jit(solution)/shard_map/all_to_all | solution.py:501
  36.3 0.0 collective-permute-done.left_ref.keep_left_ref
  36.4 0.7 copy-done
  37.1 0.2 copy-done.2
  37.3 6.2 %shard_map.69 = (f32[3,3,64,256]{3,2,1,0:T(8,128)}, f32[2,3,64,256]{3,2,1,0:T(8,128)}, f32[3,64,256]{2,1,0:T(8,128)}, f32[6,72,256]{2,1,0:T(8,128)}, f32[4,64,256]{2,1,0:T(8,128)}, /*index=5*/f32[8,128]{1,0:T(8,128)}) custom-call(f32[2,3,64,256]{3,2,1,0:T(8,128)} %get-tuple-element.16.load_ref, f32[2,3,64,256]{3,2,1,0:T(8,128)} %get-tuple-element.17.keep_ref, ...), custom_call_target="tpu_custom_call" | custom-call | tf_op jit(solution)/shard_map/pallas_call | solution.py:506
  43.5 1.9 %collective-permute-start.4 = (f32[2,3,64,256]{3,2,1,0:T(8,128)}, f32[2,3,64,256]{3,2,1,0:T(8,128)S(1)}, u32[]{:S(2)}, u32[]{:S(2)}) collective-permute-start(f32[2,3,64,256]{3,2,1,0:T(8,128)} %get-tuple-element.21.v1_ref), channel_id=1, source_target_pairs={{0,1},{1,2},{2,3},{3,4},{4,5},{5,6},{6,7},{7,8},{8,9},{9,10},{10,1... | collective-permute-start | bytes 1179656 | tf_op jit(solution)/shard_map/ppermute | solution.py:487
  45.4 5.0 %collective-permute-done.4.v1_left_ref = f32[2,3,64,256]{3,2,1,0:T(8,128)S(1)} collective-permute-done((f32[2,3,64,256]{3,2,1,0:T(8,128)}, f32[2,3,64,256]{3,2,1,0:T(8,128)S(1)}, u32[]{:S(2)}, u32[]{:S(2)}) %collective-permute-start.4) | collective-permute-done | bytes 393248 | tf_op jit(solution)/shard_map/ppermute | solution.py:487
  50.4 0.8 copy-done.1
  51.2 6.6 %shard_map.70 = (f32[3,3,64,256]{3,2,1,0:T(8,128)}, f32[16,8,128]{2,1,0:T(8,128)}) custom-call(f32[2,3,64,256]{3,2,1,0:T(8,128)} %copy-done.1, f32[2,3,64,256]{3,2,1,0:T(8,128)} %get-tuple-element.21.v1_ref, f32[3,64,256]{2,1,0:T(8,128)} %get-tuple-element.22.v1_far_ref, f32[2,3,64,256]{3,2,1,0:T(8,128)} %copy-done, ...), custom_call_target="tpu_custom_call" | custom-call | tf_op jit(solution)/shard_map/pallas_call | solution.py:514
  57.8 13.3 %all_to_all.16.mom_ref = f32[16,8,128]{2,1,0:T(8,128)} all-to-all(f32[16,8,128]{2,1,0:T(8,128)} %get-tuple-element.27), channel_id=1, replica_groups=mesh['load'=8,'space'=16] {'space'}, dimensions={0} | all-to-all | bytes 131072 | tf_op jit(solution)/shard_map/all_to_all | solution.py:521
  71.2 3.9 %shard_map.71 = (f32[3,2,64,256]{3,2,1,0:T(8,128)}, f32[8,30,256]{2,1,0:T(8,128)}) custom-call(f32[3,3,64,256]{3,2,1,0:T(8,128)} %get-tuple-element.20.v0_ref, f32[2,3,64,256]{3,2,1,0:T(8,128)} %copy-done.1, f32[2,3,64,256]{3,2,1,0:T(8,128)} %get-tuple-element.21.v1_ref, f32[3,3,64,256]{3,2,1,0:T(8,128)} %get-tuple-element.26.v2_ref, ...), custom_call_target="tpu_custom_call" | custom-call | tf_op jit(solution)/shard_map/pallas_call | solution.py:523
  75.0 11.8 %all_to_all.17 = f32[8,30,256]{2,1,0:T(8,128)S(1)} all-to-all(f32[8,30,256]{2,1,0:T(8,128)} %get-tuple-element.29), channel_id=1, replica_groups=mesh['load'=8,'space'=16] {'load'}, dimensions={0} | all-to-all | bytes 491520 | tf_op jit(solution)/shard_map/all_to_all | solution.py:530
  86.9 3.2 %collective-permute-start.5 = (f32[20,256]{1,0:T(8,128)S(1)}, f32[20,256]{1,0:T(8,128)S(1)}, u32[]{:S(2)}, u32[]{:S(2)}) collective-permute-start(f32[20,256]{1,0:T(8,128)S(1)} %slice.4), channel_id=1, source_target_pairs={{1,0},{2,1},{3,2},{4,3},{5,4},{6,5},{7,6},{8,7},{9,8},{10,9},{11,1... | collective-permute-start | bytes 61448 | tf_op jit(solution)/shard_map/ppermute | solution.py:487
  90.1 2.0 %collective-permute-done.5.next_ref = f32[20,256]{1,0:T(8,128)S(1)} collective-permute-done((f32[20,256]{1,0:T(8,128)S(1)}, f32[20,256]{1,0:T(8,128)S(1)}, u32[]{:S(2)}, u32[]{:S(2)}) %collective-permute-start.5) | collective-permute-done | bytes 20512 | tf_op jit(solution)/shard_map/ppermute | solution.py:487
  92.0 0.6 copy-done.4
  92.6 1.8 %shard_map.72 = f32[2,8,256]{2,1,0:T(8,128)} custom-call(f32[30,256]{1,0:T(8,128)} %copy-done.3, f32[20,256]{1,0:T(8,128)} %copy-done.4, f32[8,6,8,256]{3,2,1,0:T(8,128)} %all_to_all.15.dens_ref), custom_call_target="tpu_custom_call" | custom-call | tf_op jit(solution)/shard_map/pallas_call | solution.py:532
  (13 shorter events, 0.1 us)
Async XLA Ops:
  1.9 6.1 %copy-start.5 = (f32[2,8,256]{2,1,0:T(8,128)S(1)}, f32[2,8,256]{2,1,0:T(8,128)}, u32[]{:S(2)}) copy-start(f32[2,8,256]{2,1,0:T(8,128)} %param.5) | copy-start | bytes 49156
  4.6 31.7 %collective-permute-start.1 = (f32[3,3,64,256]{3,2,1,0:T(8,128)}, f32[3,3,64,256]{3,2,1,0:T(8,128)S(1)}, u32[]{:S(2)}, u32[]{:S(2)}) collective-permute-start(f32[3,3,64,256]{3,2,1,0:T(8,128)} %get-tuple-element.19), channel_id=1, source_target_pairs={{1,0},{2,1},{3,2},{4,3},{5,4},{6,5},{7,6},{8,7},{9,8},{10,9},{11,1... | collective-permute-start | bytes 1769480 | tf_op jit(solution)/shard_map/ppermute | solution.py:487
  8.0 8.7 %collective-permute-start.2 = (f32[2,8,256]{2,1,0:T(8,128)S(1)}, f32[2,8,256]{2,1,0:T(8,128)S(1)}, u32[]{:S(2)}, u32[]{:S(2)}) collective-permute-start(f32[2,8,256]{2,1,0:T(8,128)S(1)} %copy-done.5), channel_id=1, source_target_pairs={{0,1},{1,2},{2,3},{3,4},{4,5},{5,6},{6,7},{7,8},{8,9},{9,10},{10,1... | collective-permute-start | bytes 49160 | tf_op jit(solution)/shard_map/ppermute | solution.py:487
  11.1 6.0 %collective-permute-start.3 = (f32[2,8,256]{2,1,0:T(8,128)S(1)}, f32[2,8,256]{2,1,0:T(8,128)S(1)}, u32[]{:S(2)}, u32[]{:S(2)}) collective-permute-start(f32[2,8,256]{2,1,0:T(8,128)S(1)} %copy-done.5), channel_id=1, source_target_pairs={{1,0},{2,1},{3,2},{4,3},{5,4},{6,5},{7,6},{8,7},{9,8},{10,9},{11,1... | collective-permute-start | bytes 49160 | tf_op jit(solution)/shard_map/ppermute | solution.py:487
  13.0 23.3 %collective-permute-start = (f32[2,3,64,256]{3,2,1,0:T(8,128)}, f32[2,3,64,256]{3,2,1,0:T(8,128)S(1)}, u32[]{:S(2)}, u32[]{:S(2)}) collective-permute-start(f32[2,3,64,256]{3,2,1,0:T(8,128)} %get-tuple-element.18), channel_id=1, source_target_pairs={{0,1},{1,2},{2,3},{3,4},{4,5},{5,6},{6,7},{7,8},{8,9},{9,10},{10,1... | collective-permute-start | bytes 1179656 | tf_op jit(solution)/shard_map/ppermute | solution.py:487
  36.3 0.8 copy-start
  36.3 1.0 %copy-start.2 = (f32[3,3,64,256]{3,2,1,0:T(8,128)}, f32[3,3,64,256]{3,2,1,0:T(8,128)S(1)}, u32[]{:S(2)}) copy-start(f32[3,3,64,256]{3,2,1,0:T(8,128)S(1)} %collective-permute-done.1.right_ref) | copy-start | bytes 1769476
  43.5 6.9 %collective-permute-start.4 = (f32[2,3,64,256]{3,2,1,0:T(8,128)}, f32[2,3,64,256]{3,2,1,0:T(8,128)S(1)}, u32[]{:S(2)}, u32[]{:S(2)}) collective-permute-start(f32[2,3,64,256]{3,2,1,0:T(8,128)} %get-tuple-element.21.v1_ref), channel_id=1, source_target_pairs={{0,1},{1,2},{2,3},{3,4},{4,5},{5,6},{6,7},{7,8},{8,9},{9,10},{10,1... | collective-permute-start | bytes 1179656 | tf_op jit(solution)/shard_map/ppermute | solution.py:487
  50.4 0.8 copy-start.1
  86.9 5.2 %copy-start.3 = (f32[30,256]{1,0:T(8,128)}, f32[30,256]{1,0:T(8,128)S(1)}, u32[]{:S(2)}) copy-start(f32[30,256]{1,0:T(8,128)S(1)} %reduce_sum.9.energy_ref) | copy-start | bytes 92164
  86.9 5.1 %collective-permute-start.5 = (f32[20,256]{1,0:T(8,128)S(1)}, f32[20,256]{1,0:T(8,128)S(1)}, u32[]{:S(2)}, u32[]{:S(2)}) collective-permute-start(f32[20,256]{1,0:T(8,128)S(1)} %slice.4), channel_id=1, source_target_pairs={{1,0},{2,1},{3,2},{4,3},{5,4},{6,5},{7,6},{8,7},{9,8},{10,9},{11,1... | collective-permute-start | bytes 61448 | tf_op jit(solution)/shard_map/ppermute | solution.py:487
  92.0 0.6 copy-start.4

commit v2 on v1

--- a/solution.py
+++ b/solution.py
@@ -21,7 +21,7 @@
 SHEAR = 1.0 / (2.0 * (1.0 + POISSON))
 KDIAG = (LAME + 4.0 * SHEAR) / 9.0
 F32 = jnp.float32
-VMEM_LIMIT = 56 * 1024 * 1024
+VMEM_LIMIT = 16 * 1024 * 1024
 PAIRS = ("ss", "sd", "ds", "dd")
 
 
@@ -265,6 +265,8 @@
     loads = [left_ref.at[0], load_ref.at[0], load_ref.at[1], right_ref.at[0], right_ref.at[1]]
     keeps = [keep_ref.at[0], keep_ref.at[1], right_ref.at[2]]
     zero = jnp.zeros((ROWS, NZ), F32)
+    has_right = 1.0 - end_flag()
+    scaled = lambda value, plane: value * has_right if plane > 2 else value
 
     def start(chunk, total):
         here = rows_at(chunk)
@@ -278,7 +280,7 @@
             if plane < 4:
                 inv_ref[plane, here] = inverse
             for comp in range(3):
-                load = loads[plane][comp, here]
+                load = scaled(loads[plane][comp, here], plane)
                 value = load * inverse
                 if plane < 3:
                     v0_ref[plane, comp, here] = value
@@ -295,8 +297,8 @@
         for plane, forces in apply_rows(zs, zd, 5, e_ref, 1, 1, carry, chunk):
             inverse = inv_ref[plane, here]
             for comp in range(3):
-                kept = keeps[plane - 1][comp, here] > 0.0
-                before = loads[plane][comp, here] * inverse
+                kept = scaled(keeps[plane - 1][comp, here], plane) > 0.0
+                before = scaled(loads[plane][comp, here], plane) * inverse
                 image, value = advance(forces[comp], kept, before, inverse)
                 if plane < 3:
                     v1_ref[plane - 1, comp, here] = value
@@ -451,7 +453,7 @@
     total = [
         part(energy_ref, 0),
         part(energy_ref, 1),
-        part(energy_ref, 2) + part(next_ref, 0),
+        part(energy_ref, 2) + (1.0 - end_flag()) * part(next_ref, 0),
         part(next_ref, 1),
     ]
     before = jnp.maximum(load - 1, 0)
@@ -483,8 +485,7 @@
 
 def shifted(array, axis, distance):
     size = lax.axis_size(axis)
-    route = [(i, i + distance) for i in range(size) if 0 <= i + distance < size]
-    return lax.ppermute(array, axis, route)
+    return lax.ppermute(array, axis, [(i, (i + distance) % size) for i in range(size)])
 
 
 def body(density, fixed_dofs, body_loads, point_nodes, point_forces):

time: 95 us -> 77.7 us (0.82)
  Pallas kernels: 21.2 us -> 11.5 us
  starting transfers between devices: 17 us -> 8.52 us
  waiting for transfers between devices: 7.41 us -> 12.4 us
  blocking collectives: 44.3 us -> 40.8 us
    ppermute x6, starting transfers between devices: 17 us -> 8.52 us  [shifted(): lax.ppermute(array, axis, [(i, (i + distance) % size) for i in range(size)])]
    ppermute x6, waiting for transfers between devices: 7.41 us -> 12.4 us  [shifted(): lax.ppermute(array, axis, [(i, (i + distance) % size) for i in range(size)])]
    all_to_all x1, blocking collectives: 19.2 us -> 15.9 us  [body(): lax.all_to_all(jnp.broadcast_to(dens[None], (n_load,) + dens.shape), 'loa...]
    pallas_call x1, Pallas kernels: 6.18 us -> 3.66 us  [body(): kernel_call(first_kernel, [(3,) + plane, (2,) + plane, plane, (6,) + padd...]
    pallas_call x1, Pallas kernels: 6.64 us -> 4.28 us  [body(): kernel_call(second_kernel, [(3,) + plane, (n_space, 8, 128)], 0, 8, [zed(...]
    pallas_call x1, Pallas kernels: 2.75 us -> 0.5 us  [body(): kernel_call(loads_kernel, [(2,) + plane, (2,) + plane, (2,) + plane, (3,)...]
    pallas_call x1, Pallas kernels: 3.88 us -> 2.32 us  [body(): kernel_call(energy_kernel, [(3, CX, NY, NZ), (CHUNKS, 3 * span, NZ)], 0,...]
    pallas_call x1, Pallas kernels: 1.77 us -> 0.74 us  [body(): kernel_call(filter_kernel, [(CX, ROWS, NZ)], 0, 3)(energy, following, dens)]
  transfers between devices with their start and end apart: 6 -> 6, of which waited for: 3 -> 4; matrix products, arithmetic and copies ran while one was open for 0% -> 0% of each run, Pallas kernels for 0% -> 0%
where the time goes in v2:
time: 77.7 us; the launch traced here: 77.4 us
  blocking collectives  40.8 us (53%)
  waiting for transfers between devices  12.4 us (16%)
  Pallas kernels  11.5 us (15%)
  starting transfers between devices  8.52 us (11%)
  local copies, waits for them, and re-layouts  3.36 us (4%)
    all_to_all x1, blocking collectives, body(): lax.all_to_all(jnp.broadcast_to(dens[None], (n_load,) + dens.shape), 'loa...  15.9 us
    all_to_all x1, blocking collectives, body(): mom = lax.all_to_all(mom, 'space', 0, 0)  13.6 us
    ppermute x6, waiting for transfers between devices, shifted(): lax.ppermute(array, axis, [(i, (i + distance) % size) for i in range(size)])  12.4 us
    all_to_all x1, blocking collectives, body(): energy = jnp.sum(lax.all_to_all(energy, 'load', 0, 0), axis=0)  11.3 us
    ppermute x6, starting transfers between devices, shifted(): lax.ppermute(array, axis, [(i, (i + distance) % size) for i in range(size)])  8.52 us
    pallas_call x1, Pallas kernels, body(): kernel_call(second_kernel, [(3,) + plane, (n_space, 8, 128)], 0, 8, [zed(...  4.28 us
    pallas_call x1, Pallas kernels, body(): kernel_call(first_kernel, [(3,) + plane, (2,) + plane, plane, (6,) + padd...  3.66 us
    unnamed x9, local copies, waits for them, and re-layouts  3.33 us
  transfers between devices with their start and end apart: 6, of which 4 were waited for; matrix products, arithmetic and copies ran while one was open for 0% of the time, Pallas kernels for 0%

profile of v2, /device:TPU:1, one launch (start us, length us, event | category | flops | bytes accessed | tf_op | source)
XLA Modules:
  0.0 77.4 jit_solution(683852238008614927)
XLA Ops:
  0.6 0.7 copy.9
  1.3 0.7 copy-done.2
  2.0 1.0 %copy-done = f32[1,3,2,64,256]{4,3,2,1,0:T(8,128)S(1)} copy-done((f32[1,3,2,64,256]{4,3,2,1,0:T(8,128)S(1)}, f32[1,3,2,64,256]{4,3,2,1,0:T(8,128)}, u32[]{:S(2)}) %copy-start) | copy-done | bytes 393240
  3.0 1.0 %copy-done.1 = s32[3,2,64,256]{3,2,1,0:T(8,128)S(1)} copy-done((s32[3,2,64,256]{3,2,1,0:T(8,128)S(1)}, s32[3,2,64,256]{3,2,1,0:T(8,128)}, u32[]{:S(2)}) %copy-start.1) | copy-done | bytes 393240
  4.0 0.5 shard_map.68
  4.5 1.5 %collective-permute-start.1 = (f32[3,3,64,256]{3,2,1,0:T(8,128)S(1)}, f32[3,3,64,256]{3,2,1,0:T(8,128)S(1)}, u32[]{:S(2)}, u32[]{:S(2)}) collective-permute-start(f32[3,3,64,256]{3,2,1,0:T(8,128)S(1)} %get-tuple-element.19), channel_id=1, source_target_pairs={{0,15},{1,0},{2,1},{3,2},{4,3},{5,4},{6,5},{7,6},{8,7},{9,8},{10,9... | collective-permute-start | bytes 1769480 | tf_op jit(solution)/shard_map/ppermute | solution.py:488
  6.0 1.3 %collective-permute-start.2 = (f32[2,8,256]{2,1,0:T(8,128)S(1)}, f32[2,8,256]{2,1,0:T(8,128)S(1)}, u32[]{:S(2)}, u32[]{:S(2)}) collective-permute-start(f32[2,8,256]{2,1,0:T(8,128)S(1)} %copy-done.3), channel_id=1, source_target_pairs={{0,1},{1,2},{2,3},{3,4},{4,5},{5,6},{6,7},{7,8},{8,9},{9,10},{10,1... | collective-permute-start | bytes 49160 | tf_op jit(solution)/shard_map/ppermute | solution.py:488
  7.3 2.3 %collective-permute-start.3 = (f32[2,8,256]{2,1,0:T(8,128)S(1)}, f32[2,8,256]{2,1,0:T(8,128)S(1)}, u32[]{:S(2)}, u32[]{:S(2)}) collective-permute-start(f32[2,8,256]{2,1,0:T(8,128)S(1)} %copy-done.3), channel_id=1, source_target_pairs={{0,15},{1,0},{2,1},{3,2},{4,3},{5,4},{6,5},{7,6},{8,7},{9,8},{10,9... | collective-permute-start | bytes 49160 | tf_op jit(solution)/shard_map/ppermute | solution.py:488
  9.6 0.0 collective-permute-start
  9.6 0.7 collective-permute-done.2
  10.3 4.6 %collective-permute-done.3 = f32[2,8,256]{2,1,0:T(8,128)S(1)} collective-permute-done((f32[2,8,256]{2,1,0:T(8,128)S(1)}, f32[2,8,256]{2,1,0:T(8,128)S(1)}, u32[]{:S(2)}, u32[]{:S(2)}) %collective-permute-start.3) | collective-permute-done | bytes 16416 | tf_op jit(solution)/shard_map/ppermute | solution.py:488
  14.9 15.9 %all_to_all.15.dens_ref = f32[8,6,8,256]{3,2,1,0:T(8,128)S(1)} all-to-all(f32[8,6,8,256]{3,2,1,0:T(8,128)S(1)} %broadcast_in_dim.4), channel_id=1, replica_groups=mesh['load'=8,'space'=16] {'load'}, dimensions={0} | all-to-all | bytes 786432 | tf_op jit(solution)/shard_map/all_to_all | solution.py:502
  30.8 0.0 collective-permute-done.left_ref.keep_left_ref
  30.8 0.0 collective-permute-done.1.right_ref
  30.8 3.7 %shard_map.69 = (f32[3,3,64,256]{3,2,1,0:T(8,128)S(1)}, f32[2,3,64,256]{3,2,1,0:T(8,128)S(1)}, f32[3,64,256]{2,1,0:T(8,128)S(1)}, f32[6,72,256]{2,1,0:T(8,128)S(...) custom-call(f32[2,3,64,256]{3,2,1,0:T(8,128)S(1)} %get-tuple-element.16.load_ref, ...), custom_call_target="tpu_custom_call" | custom-call | tf_op jit(solution)/shard_map/pallas_call | solution.py:507
  34.5 2.5 %collective-permute-start.4 = (f32[2,3,64,256]{3,2,1,0:T(8,128)S(1)}, f32[2,3,64,256]{3,2,1,0:T(8,128)S(1)}, u32[]{:S(2)}, u32[]{:S(2)}) collective-permute-start(f32[2,3,64,256]{3,2,1,0:T(8,128)S(1)} %get-tuple-element.21.v1_ref), channel_id=1, source_target_pairs={{0,1},{1,2},{2,3},{3,4},{4,5},{5,6},{6,7},{7,8},{8,9},{9,10},{10,1... | collective-permute-start | bytes 1179656 | tf_op jit(solution)/shard_map/ppermute | solution.py:488
  37.0 4.7 %collective-permute-done.4.v1_left_ref = f32[2,3,64,256]{3,2,1,0:T(8,128)S(1)} collective-permute-done((f32[2,3,64,256]{3,2,1,0:T(8,128)S(1)}, f32[2,3,64,256]{3,2,1,0:T(8,128)S(1)}, u32[]{:S(2)}, u32[]{:S(2)}) %collective-permute-start.4) | collective-permute-done | bytes 393248 | tf_op jit(solution)/shard_map/ppermute | solution.py:488
  41.7 4.3 %shard_map.70 = (f32[3,3,64,256]{3,2,1,0:T(8,128)S(1)}, f32[16,8,128]{2,1,0:T(8,128)S(1)}) custom-call(f32[2,3,64,256]{3,2,1,0:T(8,128)S(1)} %collective-permute-done.4.v1_left_ref, f32[2,3,64,256]{3,2,1,0:T(8,128)S(1)} %get-tuple-element.21.v1_ref, f32[3,64,256]{2,1,0:T(8,128)S(1)} %get-tuple-element.22.v1_far_ref, ...), custom_call_target="tpu_custom_call" | custom-call | tf_op jit(solution)/shard_map/pallas_call | solution.py:515
  46.0 13.6 %all_to_all.16.mom_ref = f32[16,8,128]{2,1,0:T(8,128)S(1)} all-to-all(f32[16,8,128]{2,1,0:T(8,128)S(1)} %get-tuple-element.27), channel_id=1, replica_groups=mesh['load'=8,'space'=16] {'space'}, dimensions={0} | all-to-all | bytes 131072 | tf_op jit(solution)/shard_map/all_to_all | solution.py:522
  59.6 2.3 %shard_map.71 = (f32[3,2,64,256]{3,2,1,0:T(8,128)}, f32[8,30,256]{2,1,0:T(8,128)S(1)}) custom-call(f32[3,3,64,256]{3,2,1,0:T(8,128)S(1)} %get-tuple-element.20.v0_ref, f32[2,3,64,256]{3,2,1,0:T(8,128)S(1)} %collective-permute-done.4.v1_left_ref, f32[2,3,64,256]{3,2,1,0:T(8,128)S(1)} %get-tuple-element.21.v1_ref, ...), custom_call_target="tpu_custom_call" | custom-call | tf_op jit(solution)/shard_map/pallas_call | solution.py:524
  61.9 11.3 %all_to_all.17 = f32[8,30,256]{2,1,0:T(8,128)S(1)} all-to-all(f32[8,30,256]{2,1,0:T(8,128)S(1)} %get-tuple-element.29), channel_id=1, replica_groups=mesh['load'=8,'space'=16] {'load'}, dimensions={0} | all-to-all | bytes 491520 | tf_op jit(solution)/shard_map/all_to_all | solution.py:531
  73.3 0.9 %collective-permute-start.5 = (f32[20,256]{1,0:T(8,128)S(1)}, f32[20,256]{1,0:T(8,128)S(1)}, u32[]{:S(2)}, u32[]{:S(2)}) collective-permute-start(f32[20,256]{1,0:T(8,128)S(1)} %slice.4), channel_id=1, source_target_pairs={{0,15},{1,0},{2,1},{3,2},{4,3},{5,4},{6,5},{7,6},{8,7},{9,8},{10,9... | collective-permute-start | bytes 61448 | tf_op jit(solution)/shard_map/ppermute | solution.py:488
  74.2 2.4 %collective-permute-done.5.next_ref = f32[20,256]{1,0:T(8,128)S(1)} collective-permute-done((f32[20,256]{1,0:T(8,128)S(1)}, f32[20,256]{1,0:T(8,128)S(1)}, u32[]{:S(2)}, u32[]{:S(2)}) %collective-permute-start.5) | collective-permute-done | bytes 20512 | tf_op jit(solution)/shard_map/ppermute | solution.py:488
  76.6 0.7 shard_map.72
  (9 shorter events, 0.1 us)
Async XLA Ops:
  1.3 0.7 copy-start.2
  2.0 1.0 %copy-start = (f32[1,3,2,64,256]{4,3,2,1,0:T(8,128)S(1)}, f32[1,3,2,64,256]{4,3,2,1,0:T(8,128)}, u32[]{:S(2)}) copy-start(f32[1,3,2,64,256]{4,3,2,1,0:T(8,128)} %param.7) | copy-start | bytes 1179652
  3.0 1.0 %copy-start.1 = (s32[3,2,64,256]{3,2,1,0:T(8,128)S(1)}, s32[3,2,64,256]{3,2,1,0:T(8,128)}, u32[]{:S(2)}) copy-start(s32[3,2,64,256]{3,2,1,0:T(8,128)} %fixed_ref.1) | copy-start | bytes 1179652
  4.0 2.0 %copy-start.3 = (f32[2,8,256]{2,1,0:T(8,128)S(1)}, f32[2,8,256]{2,1,0:T(8,128)}, u32[]{:S(2)}) copy-start(f32[2,8,256]{2,1,0:T(8,128)} %param.5) | copy-start | bytes 49156
  4.5 26.3 %collective-permute-start.1 = (f32[3,3,64,256]{3,2,1,0:T(8,128)S(1)}, f32[3,3,64,256]{3,2,1,0:T(8,128)S(1)}, u32[]{:S(2)}, u32[]{:S(2)}) collective-permute-start(f32[3,3,64,256]{3,2,1,0:T(8,128)S(1)} %get-tuple-element.19), channel_id=1, source_target_pairs={{0,15},{1,0},{2,1},{3,2},{4,3},{5,4},{6,5},{7,6},{8,7},{9,8},{10,9... | collective-permute-start | bytes 1769480 | tf_op jit(solution)/shard_map/ppermute | solution.py:488
  6.0 4.3 %collective-permute-start.2 = (f32[2,8,256]{2,1,0:T(8,128)S(1)}, f32[2,8,256]{2,1,0:T(8,128)S(1)}, u32[]{:S(2)}, u32[]{:S(2)}) collective-permute-start(f32[2,8,256]{2,1,0:T(8,128)S(1)} %copy-done.3), channel_id=1, source_target_pairs={{0,1},{1,2},{2,3},{3,4},{4,5},{5,6},{6,7},{7,8},{8,9},{9,10},{10,1... | collective-permute-start | bytes 49160 | tf_op jit(solution)/shard_map/ppermute | solution.py:488
  7.3 7.6 %collective-permute-start.3 = (f32[2,8,256]{2,1,0:T(8,128)S(1)}, f32[2,8,256]{2,1,0:T(8,128)S(1)}, u32[]{:S(2)}, u32[]{:S(2)}) collective-permute-start(f32[2,8,256]{2,1,0:T(8,128)S(1)} %copy-done.3), channel_id=1, source_target_pairs={{0,15},{1,0},{2,1},{3,2},{4,3},{5,4},{6,5},{7,6},{8,7},{9,8},{10,9... | collective-permute-start | bytes 49160 | tf_op jit(solution)/shard_map/ppermute | solution.py:488
  9.6 21.2 %collective-permute-start = (f32[2,3,64,256]{3,2,1,0:T(8,128)S(1)}, f32[2,3,64,256]{3,2,1,0:T(8,128)S(1)}, u32[]{:S(2)}, u32[]{:S(2)}) collective-permute-start(f32[2,3,64,256]{3,2,1,0:T(8,128)S(1)} %get-tuple-element.18), channel_id=1, source_target_pairs={{0,1},{1,2},{2,3},{3,4},{4,5},{5,6},{6,7},{7,8},{8,9},{9,10},{10,1... | collective-permute-start | bytes 1179656 | tf_op jit(solution)/shard_map/ppermute | solution.py:488
  34.5 7.2 %collective-permute-start.4 = (f32[2,3,64,256]{3,2,1,0:T(8,128)S(1)}, f32[2,3,64,256]{3,2,1,0:T(8,128)S(1)}, u32[]{:S(2)}, u32[]{:S(2)}) collective-permute-start(f32[2,3,64,256]{3,2,1,0:T(8,128)S(1)} %get-tuple-element.21.v1_ref), channel_id=1, source_target_pairs={{0,1},{1,2},{2,3},{3,4},{4,5},{5,6},{6,7},{7,8},{8,9},{9,10},{10,1... | collective-permute-start | bytes 1179656 | tf_op jit(solution)/shard_map/ppermute | solution.py:488
  73.3 3.3 %collective-permute-start.5 = (f32[20,256]{1,0:T(8,128)S(1)}, f32[20,256]{1,0:T(8,128)S(1)}, u32[]{:S(2)}, u32[]{:S(2)}) collective-permute-start(f32[20,256]{1,0:T(8,128)S(1)} %slice.4), channel_id=1, source_target_pairs={{0,15},{1,0},{2,1},{3,2},{4,3},{5,4},{6,5},{7,6},{8,7},{9,8},{10,9... | collective-permute-start | bytes 61448 | tf_op jit(solution)/shard_map/ppermute | solution.py:488

commit v3 on v2

--- a/solution.py
+++ b/solution.py
@@ -220,6 +220,14 @@
             else:
                 right_ref[0, comp] = load
                 right_ref[1, comp] = keep
+
+
+def pack_kernel(before_ref, own_ref, after_ref, pack_ref):
+    for block in range(pack_ref.shape[0]):
+        for plane in range(CX):
+            pack_ref[block, plane] = before_ref[plane]
+            pack_ref[block, CX + plane] = own_ref[plane]
+            pack_ref[block, 2 * CX + plane] = after_ref[plane]
 
 
 def clear_tails(refs):
@@ -490,16 +498,19 @@
 
 def body(density, fixed_dofs, body_loads, point_nodes, point_forces):
     n_load, n_space = lax.axis_size("load"), lax.axis_size("space")
-    dens = jnp.concatenate(
-        [shifted(density, "space", 1), density, shifted(density, "space", -1)], axis=0
-    )
+    dens_left = shifted(density, "space", 1)
+    dens_right = shifted(density, "space", -1)
     plane = (3, NY, NZ)
     load, keep, to_right, to_left = kernel_call(
         loads_kernel, [(2,) + plane, (2,) + plane, (2,) + plane, (3,) + plane], 0, 4
     )(body_loads[0], fixed_dofs, point_nodes, point_forces[0])
+    (dens,) = kernel_call(pack_kernel, [(n_load, 3 * CX, ROWS, NZ)], 0, 3)(
+        dens_left, density, dens_right
+    )
+    dens, to_right, to_left = lax.optimization_barrier((dens, to_right, to_left))
     left = shifted(to_right, "space", 1)
     right = shifted(to_left, "space", -1)
-    dens = lax.all_to_all(jnp.broadcast_to(dens[None], (n_load,) + dens.shape), "load", 0, 0)
+    dens = lax.all_to_all(dens, "load", 0, 0)
 
     padded = (NY + ROWS, NZ)
     zed = lambda planes: pltpu.VMEM((planes, 3) + padded, F32)

time: 77.7 us -> 73.2 us (0.942)
  waiting for transfers between devices: 12.4 us -> 6.43 us
  blocking collectives: 40.8 us -> 42.6 us
    ppermute x6, waiting for transfers between devices: 12.4 us -> 6.43 us  [shifted(): lax.ppermute(array, axis, [(i, (i + distance) % size) for i in range(size)])]
    all_to_all x1, blocking collectives: 15.9 us -> 17.8 us  [body(): dens = lax.all_to_all(dens, 'load', 0, 0)]
    all_to_all x1, blocking collectives: 13.6 us -> 12.8 us  [body(): mom = lax.all_to_all(mom, 'space', 0, 0)]
  transfers between devices with their start and end apart: 6 -> 6, of which waited for: 4 -> 2; matrix products, arithmetic and copies ran while one was open for 0% -> 1% of each run, Pallas kernels for 0% -> 1%
where the time goes in v3:
time: 73.2 us; the launch traced here: 72.9 us
  blocking collectives  42.6 us (58%)
  Pallas kernels  11.5 us (16%)
  starting transfers between devices  8.06 us (11%)
  waiting for transfers between devices  6.43 us (9%)
  local copies, waits for them, and re-layouts  3.52 us (5%)
    all_to_all x1, blocking collectives, body(): dens = lax.all_to_all(dens, 'load', 0, 0)  17.8 us
    all_to_all x1, blocking collectives, body(): mom = lax.all_to_all(mom, 'space', 0, 0)  12.8 us
    all_to_all x1, blocking collectives, body(): energy = jnp.sum(lax.all_to_all(energy, 'load', 0, 0), axis=0)  12 us
    ppermute x6, starting transfers between devices, shifted(): lax.ppermute(array, axis, [(i, (i + distance) % size) for i in range(size)])  8.06 us
    ppermute x6, waiting for transfers between devices, shifted(): lax.ppermute(array, axis, [(i, (i + distance) % size) for i in range(size)])  6.43 us
    pallas_call x1, Pallas kernels, body(): kernel_call(second_kernel, [(3,) + plane, (n_space, 8, 128)], 0, 8, [zed(...  4.28 us
    pallas_call x1, Pallas kernels, body(): kernel_call(first_kernel, [(3,) + plane, (2,) + plane, plane, (6,) + padd...  3.66 us
    unnamed x9, local copies, waits for them, and re-layouts  3.51 us
  transfers between devices with their start and end apart: 6, of which 2 were waited for; matrix products, arithmetic and copies ran while one was open for 1% of the time, Pallas kernels for 1%

profile of v3, /device:TPU:1, one launch (start us, length us, event | category | flops | bytes accessed | tf_op | source)
XLA Modules:
  0.0 72.9 jit_solution(1994041370656487364)
XLA Ops:
  0.6 2.7 %collective-permute-start = (f32[2,8,256]{2,1,0:T(8,128)}, f32[2,8,256]{2,1,0:T(8,128)S(1)}, u32[]{:S(2)}, u32[]{:S(2)}) collective-permute-start(f32[2,8,256]{2,1,0:T(8,128)} %own_ref.1), channel_id=1, source_target_pairs={{0,1},{1,2},{2,3},{3,4},{4,5},{5,6},{6,7},{7,8},{8,9},{9,10},{10,1... | collective-permute-start | bytes 49160 | tf_op jit(solution)/shard_map/ppermute | solution.py:496
  3.3 0.0 collective-permute-start.1
  3.3 0.7 copy.9
  4.0 0.7 copy-done.3
  4.6 1.0 %copy-done = f32[1,3,2,64,256]{4,3,2,1,0:T(8,128)S(1)} copy-done((f32[1,3,2,64,256]{4,3,2,1,0:T(8,128)S(1)}, f32[1,3,2,64,256]{4,3,2,1,0:T(8,128)}, u32[]{:S(2)}) %copy-start) | copy-done | bytes 393240
  5.6 1.0 %copy-done.1 = s32[3,2,64,256]{3,2,1,0:T(8,128)S(1)} copy-done((s32[3,2,64,256]{3,2,1,0:T(8,128)S(1)}, s32[3,2,64,256]{3,2,1,0:T(8,128)}, u32[]{:S(2)}) %copy-start.1) | copy-done | bytes 393240
  6.6 0.5 shard_map.68
  7.1 0.0 collective-permute-done.before_ref
  7.2 0.0 collective-permute-done.1.after_ref
  7.2 0.2 copy-done.2
  7.4 2.7 %collective-permute-start.3 = (f32[3,3,64,256]{3,2,1,0:T(8,128)S(1)}, f32[3,3,64,256]{3,2,1,0:T(8,128)S(1)}, u32[]{:S(2)}, u32[]{:S(2)}) collective-permute-start(f32[3,3,64,256]{3,2,1,0:T(8,128)S(1)} %get-tuple-element.24), channel_id=1, source_target_pairs={{0,15},{1,0},{2,1},{3,2},{4,3},{5,4},{6,5},{7,6},{8,7},{9,8},{10,9... | collective-permute-start | bytes 1769480 | tf_op jit(solution)/shard_map/ppermute | solution.py:496
  10.1 0.0 collective-permute-start.2
  10.1 17.8 %all_to_all.15.dens_ref = f32[8,6,8,256]{3,2,1,0:T(8,128)S(1)} all-to-all(f32[8,6,8,256]{3,2,1,0:T(8,128)S(1)} %shard_map.69), channel_id=1, replica_groups=mesh['load'=8,'space'=16] {'load'}, dimensions={0} | all-to-all | bytes 786432 | tf_op jit(solution)/shard_map/all_to_all | solution.py:513
  27.9 0.0 collective-permute-done.3.right_ref
  27.9 3.7 %shard_map.70 = (f32[3,3,64,256]{3,2,1,0:T(8,128)S(1)}, f32[2,3,64,256]{3,2,1,0:T(8,128)S(1)}, f32[3,64,256]{2,1,0:T(8,128)S(1)}, f32[6,72,256]{2,1,0:T(8,128)S(...) custom-call(f32[2,3,64,256]{3,2,1,0:T(8,128)S(1)} %get-tuple-element.19.load_ref, ...), custom_call_target="tpu_custom_call" | custom-call | tf_op jit(solution)/shard_map/pallas_call | solution.py:518
  31.6 0.9 %collective-permute-start.4 = (f32[2,3,64,256]{3,2,1,0:T(8,128)S(1)}, f32[2,3,64,256]{3,2,1,0:T(8,128)S(1)}, u32[]{:S(2)}, u32[]{:S(2)}) collective-permute-start(f32[2,3,64,256]{3,2,1,0:T(8,128)S(1)} %get-tuple-element.27.v1_ref), channel_id=1, source_target_pairs={{0,1},{1,2},{2,3},{3,4},{4,5},{5,6},{6,7},{7,8},{8,9},{9,10},{10,1... | collective-permute-start | bytes 1179656 | tf_op jit(solution)/shard_map/ppermute | solution.py:496
  32.5 4.7 %collective-permute-done.4.v1_left_ref = f32[2,3,64,256]{3,2,1,0:T(8,128)S(1)} collective-permute-done((f32[2,3,64,256]{3,2,1,0:T(8,128)S(1)}, f32[2,3,64,256]{3,2,1,0:T(8,128)S(1)}, u32[]{:S(2)}, u32[]{:S(2)}) %collective-permute-start.4) | collective-permute-done | bytes 393248 | tf_op jit(solution)/shard_map/ppermute | solution.py:496
  37.3 4.3 %shard_map.71 = (f32[3,3,64,256]{3,2,1,0:T(8,128)S(1)}, f32[16,8,128]{2,1,0:T(8,128)S(1)}) custom-call(f32[2,3,64,256]{3,2,1,0:T(8,128)S(1)} %collective-permute-done.4.v1_left_ref, f32[2,3,64,256]{3,2,1,0:T(8,128)S(1)} %get-tuple-element.27.v1_ref, f32[3,64,256]{2,1,0:T(8,128)S(1)} %get-tuple-element.28.v1_far_ref, ...), custom_call_target="tpu_custom_call" | custom-call | tf_op jit(solution)/shard_map/pallas_call | solution.py:526
  41.6 12.8 %all_to_all.16.mom_ref = f32[16,8,128]{2,1,0:T(8,128)S(1)} all-to-all(f32[16,8,128]{2,1,0:T(8,128)S(1)} %get-tuple-element.33), channel_id=1, replica_groups=mesh['load'=8,'space'=16] {'space'}, dimensions={0} | all-to-all | bytes 131072 | tf_op jit(solution)/shard_map/all_to_all | solution.py:533
  54.3 2.3 %shard_map.72 = (f32[3,2,64,256]{3,2,1,0:T(8,128)}, f32[8,30,256]{2,1,0:T(8,128)S(1)}) custom-call(f32[3,3,64,256]{3,2,1,0:T(8,128)S(1)} %get-tuple-element.26.v0_ref, f32[2,3,64,256]{3,2,1,0:T(8,128)S(1)} %collective-permute-done.4.v1_left_ref, f32[2,3,64,256]{3,2,1,0:T(8,128)S(1)} %get-tuple-element.27.v1_ref, ...), custom_call_target="tpu_custom_call" | custom-call | tf_op jit(solution)/shard_map/pallas_call | solution.py:535
  56.7 12.0 %all_to_all.17 = f32[8,30,256]{2,1,0:T(8,128)S(1)} all-to-all(f32[8,30,256]{2,1,0:T(8,128)S(1)} %get-tuple-element.35), channel_id=1, replica_groups=mesh['load'=8,'space'=16] {'load'}, dimensions={0} | all-to-all | bytes 491520 | tf_op jit(solution)/shard_map/all_to_all | solution.py:542
  68.7 1.7 %collective-permute-start.5 = (f32[20,256]{1,0:T(8,128)S(1)}, f32[20,256]{1,0:T(8,128)S(1)}, u32[]{:S(2)}, u32[]{:S(2)}) collective-permute-start(f32[20,256]{1,0:T(8,128)S(1)} %slice.4), channel_id=1, source_target_pairs={{0,15},{1,0},{2,1},{3,2},{4,3},{5,4},{6,5},{7,6},{8,7},{9,8},{10,9... | collective-permute-start | bytes 61448 | tf_op jit(solution)/shard_map/ppermute | solution.py:496
  70.4 1.7 %collective-permute-done.5.next_ref = f32[20,256]{1,0:T(8,128)S(1)} collective-permute-done((f32[20,256]{1,0:T(8,128)S(1)}, f32[20,256]{1,0:T(8,128)S(1)}, u32[]{:S(2)}, u32[]{:S(2)}) %collective-permute-start.5) | collective-permute-done | bytes 20512 | tf_op jit(solution)/shard_map/ppermute | solution.py:496
  72.1 0.7 %shard_map.73 = f32[2,8,256]{2,1,0:T(8,128)} custom-call(f32[30,256]{1,0:T(8,128)S(1)} %reduce_sum.9.energy_ref, f32[20,256]{1,0:T(8,128)S(1)} %collective-permute-done.5.next_ref, f32[8,6,8,256]{3,2,1,0:T(8,128)S(1)} %all_to_all.15.dens_ref), custom_call_target="tpu_custom_call" | custom-call | tf_op jit(solution)/shard_map/pallas_call | solution.py:544
  (8 shorter events, 0.1 us)
Async XLA Ops:
  0.6 6.5 %collective-permute-start = (f32[2,8,256]{2,1,0:T(8,128)}, f32[2,8,256]{2,1,0:T(8,128)S(1)}, u32[]{:S(2)}, u32[]{:S(2)}) collective-permute-start(f32[2,8,256]{2,1,0:T(8,128)} %own_ref.1), channel_id=1, source_target_pairs={{0,1},{1,2},{2,3},{3,4},{4,5},{5,6},{6,7},{7,8},{8,9},{9,10},{10,1... | collective-permute-start | bytes 49160 | tf_op jit(solution)/shard_map/ppermute | solution.py:496
  3.3 3.9 %collective-permute-start.1 = (f32[2,8,256]{2,1,0:T(8,128)}, f32[2,8,256]{2,1,0:T(8,128)S(1)}, u32[]{:S(2)}, u32[]{:S(2)}) collective-permute-start(f32[2,8,256]{2,1,0:T(8,128)} %own_ref.1), channel_id=1, source_target_pairs={{0,15},{1,0},{2,1},{3,2},{4,3},{5,4},{6,5},{7,6},{8,7},{9,8},{10,9... | collective-permute-start | bytes 49160 | tf_op jit(solution)/shard_map/ppermute | solution.py:496
  4.0 0.7 copy-start.3
  4.6 1.0 %copy-start = (f32[1,3,2,64,256]{4,3,2,1,0:T(8,128)S(1)}, f32[1,3,2,64,256]{4,3,2,1,0:T(8,128)}, u32[]{:S(2)}) copy-start(f32[1,3,2,64,256]{4,3,2,1,0:T(8,128)} %param.7) | copy-start | bytes 1179652
  5.6 1.0 %copy-start.1 = (s32[3,2,64,256]{3,2,1,0:T(8,128)S(1)}, s32[3,2,64,256]{3,2,1,0:T(8,128)}, u32[]{:S(2)}) copy-start(s32[3,2,64,256]{3,2,1,0:T(8,128)} %fixed_ref.1) | copy-start | bytes 1179652
  6.6 0.7 copy-start.2
  7.4 20.5 %collective-permute-start.3 = (f32[3,3,64,256]{3,2,1,0:T(8,128)S(1)}, f32[3,3,64,256]{3,2,1,0:T(8,128)S(1)}, u32[]{:S(2)}, u32[]{:S(2)}) collective-permute-start(f32[3,3,64,256]{3,2,1,0:T(8,128)S(1)} %get-tuple-element.24), channel_id=1, source_target_pairs={{0,15},{1,0},{2,1},{3,2},{4,3},{5,4},{6,5},{7,6},{8,7},{9,8},{10,9... | collective-permute-start | bytes 1769480 | tf_op jit(solution)/shard_map/ppermute | solution.py:496
  10.1 17.8 %collective-permute-start.2 = (f32[2,3,64,256]{3,2,1,0:T(8,128)S(1)}, f32[2,3,64,256]{3,2,1,0:T(8,128)S(1)}, u32[]{:S(2)}, u32[]{:S(2)}) collective-permute-start(f32[2,3,64,256]{3,2,1,0:T(8,128)S(1)} %get-tuple-element.23), channel_id=1, source_target_pairs={{0,1},{1,2},{2,3},{3,4},{4,5},{5,6},{6,7},{7,8},{8,9},{9,10},{10,1... | collective-permute-start | bytes 1179656 | tf_op jit(solution)/shard_map/ppermute | solution.py:496
  31.6 5.7 %collective-permute-start.4 = (f32[2,3,64,256]{3,2,1,0:T(8,128)S(1)}, f32[2,3,64,256]{3,2,1,0:T(8,128)S(1)}, u32[]{:S(2)}, u32[]{:S(2)}) collective-permute-start(f32[2,3,64,256]{3,2,1,0:T(8,128)S(1)} %get-tuple-element.27.v1_ref), channel_id=1, source_target_pairs={{0,1},{1,2},{2,3},{3,4},{4,5},{5,6},{6,7},{7,8},{8,9},{9,10},{10,1... | collective-permute-start | bytes 1179656 | tf_op jit(solution)/shard_map/ppermute | solution.py:496
  68.7 3.4 %collective-permute-start.5 = (f32[20,256]{1,0:T(8,128)S(1)}, f32[20,256]{1,0:T(8,128)S(1)}, u32[]{:S(2)}, u32[]{:S(2)}) collective-permute-start(f32[20,256]{1,0:T(8,128)S(1)} %slice.4), channel_id=1, source_target_pairs={{0,15},{1,0},{2,1},{3,2},{4,3},{5,4},{6,5},{7,6},{8,7},{9,8},{10,9... | collective-permute-start | bytes 61448 | tf_op jit(solution)/shard_map/ppermute | solution.py:496

commit v4 on v3

--- a/solution.py
+++ b/solution.py
@@ -169,22 +169,32 @@
     return low + pltpu.roll(jnp.where(last, prev, high), 1, 0), high
 
 
-def apply_rows(zs_ref, zd_ref, planes, e_ref, e_first, e_pad, carry_ref, chunk):
-    low = plane_modes(zs_ref, zd_ref, 0, chunk)
+def apply_rows(planes, moduli, carry_ref, chunk, first_edge=False, last_edge=False):
+    slot = 0
+
+    def finish(acc):
+        nonlocal slot
+        forces = []
+        for comp in range(3):
+            force, carry = node_force(acc[comp], carry_ref[slot, comp])
+            carry_ref[slot, comp] = carry
+            forces.append(force)
+        slot += 1
+        return forces
+
+    low = plane_modes(*planes[0], chunk)
     partial = None
-    for plane in range(planes - 1):
-        high = plane_modes(zs_ref, zd_ref, plane + 1, chunk)
-        modulus = e_ref[e_first + plane, rows_at(chunk + e_pad)]
+    for index, modulus in enumerate(moduli):
+        high = plane_modes(*planes[index + 1], chunk)
         to_low, to_high = split_x(element_response(element_modes(low, high), modulus))
         if partial is not None:
-            forces = []
-            for comp in range(3):
-                acc = {pair: partial[comp][pair] + to_low[comp][pair] for pair in PAIRS}
-                force, carry = node_force(acc, carry_ref[plane - 1, comp])
-                carry_ref[plane - 1, comp] = carry
-                forces.append(force)
-            yield plane, forces
+            acc = [{p: partial[c][p] + to_low[c][p] for p in PAIRS} for c in range(3)]
+            yield index, finish(acc)
+        elif first_edge:
+            yield index, finish(to_low)
         partial, low = to_high, high
+    if last_edge:
+        yield len(moduli), finish(partial)
 
 
 def loads_kernel(
@@ -253,10 +263,23 @@
     return image, jnp.where(kept, forces * inverse, before)
 
 
+def modulus_rows(e_ref, plane, chunk):
+    return e_ref[plane, rows_at(chunk + 1)]
+
+
+def inverse_diagonal(e_ref, plane, chunk):
+    last = row_ids((ROWS, NZ)) == ROWS - 1
+    cur = modulus_rows(e_ref, plane, chunk) + modulus_rows(e_ref, plane + 1, chunk)
+    before = modulus_rows(e_ref, plane, chunk - 1) + modulus_rows(e_ref, plane + 1, chunk - 1)
+    cur = cur + pltpu.roll(jnp.where(last, before, cur), 1, 0)
+    diag = KDIAG * (cur + from_below(cur))
+    return 1.0 / jnp.where(diag > 0.0, diag, 1.0)
+
+
 def first_kernel(
     load_ref, keep_ref, left_ref, right_ref, dens_ref,
-    v0_ref, v1_ref, v1_far_ref, e_ref, inv_ref, mom_ref,
-    zs, zd, carry,
+    v1_ref, v0_ref, e_ref, inv_ref, zs, zd, mom_ref,
+    carry,
 ):
     first_x = lax.axis_index("space") * CX
     limit = lax.axis_size("space") * CX
@@ -270,25 +293,19 @@
             e_ref[plane, rows] = scale * (EMIN + (1.0 - EMIN) * (dens * dens * dens))
     clear_tails([zs, zd])
     clear_carry(carry)
-    loads = [left_ref.at[0], load_ref.at[0], load_ref.at[1], right_ref.at[0], right_ref.at[1]]
-    keeps = [keep_ref.at[0], keep_ref.at[1], right_ref.at[2]]
+    loads = [left_ref.at[0], load_ref.at[0], load_ref.at[1], right_ref.at[0]]
+    has_right = 1.0 - end_flag()
     zero = jnp.zeros((ROWS, NZ), F32)
-    has_right = 1.0 - end_flag()
-    scaled = lambda value, plane: value * has_right if plane > 2 else value
 
     def start(chunk, total):
         here = rows_at(chunk)
-        last = row_ids((ROWS, NZ)) == ROWS - 1
-        for plane in range(5):
-            cur = e_ref[plane, rows_at(chunk + 1)] + e_ref[plane + 1, rows_at(chunk + 1)]
-            before = e_ref[plane, rows_at(chunk)] + e_ref[plane + 1, rows_at(chunk)]
-            cur = cur + pltpu.roll(jnp.where(last, before, cur), 1, 0)
-            diag = KDIAG * (cur + from_below(cur))
-            inverse = 1.0 / jnp.where(diag > 0.0, diag, 1.0)
-            if plane < 4:
-                inv_ref[plane, here] = inverse
-            for comp in range(3):
-                load = scaled(loads[plane][comp, here], plane)
+        for plane in range(4):
+            inverse = inverse_diagonal(e_ref, plane, chunk)
+            inv_ref[plane, here] = inverse
+            for comp in range(3):
+                load = loads[plane][comp, here]
+                if plane == 3:
+                    load = load * has_right
                 value = load * inverse
                 if plane < 3:
                     v0_ref[plane, comp, here] = value
@@ -302,40 +319,106 @@
     def apply(chunk, totals):
         here = rows_at(chunk)
         odd, even = totals
-        for plane, forces in apply_rows(zs, zd, 5, e_ref, 1, 1, carry, chunk):
+        moduli = [modulus_rows(e_ref, plane, chunk) for plane in (1, 2, 3)]
+        for plane, forces in apply_rows([(zs, zd, k) for k in range(4)], moduli, carry, chunk):
             inverse = inv_ref[plane, here]
             for comp in range(3):
-                kept = scaled(keeps[plane - 1][comp, here], plane) > 0.0
-                before = scaled(loads[plane][comp, here], plane) * inverse
+                kept = keep_ref[plane - 1, comp, here] > 0.0
+                before = v0_ref[plane, comp, here]
                 image, value = advance(forces[comp], kept, before, inverse)
-                if plane < 3:
-                    v1_ref[plane - 1, comp, here] = value
-                    odd = odd + before * image
-                    even = even + value * image
-                else:
-                    v1_far_ref[comp, here] = value
+                v1_ref[plane - 1, comp, here] = value
+                odd = odd + before * image
+                even = even + value * image
         return odd, even
 
     mom1, mom2 = lax.fori_loop(0, CHUNKS, apply, (zero, zero))
     mom_ref[...] = folded([mom0, mom1, mom2] + [zero] * 5)
 
 
+def middle_kernel(
+    v1_ref, zs0, zd0, e_ref, inv_ref, right_ref, keep_ref, sofar_ref,
+    v2_ref, zs1, zd1, zs2, zd2, force_ref, mom_ref,
+    zs, zd, zs_far, zd_far, carry,
+):
+    clear_tails([zs, zd, zs1, zd1, zs2, zd2, zs_far, zd_far])
+    clear_carry(carry)
+    has_right = 1.0 - end_flag()
+    zero = jnp.zeros((ROWS, NZ), F32)
+
+    def start(chunk, done):
+        here = rows_at(chunk)
+        inverse = inverse_diagonal(e_ref, 4, chunk)
+        for comp in range(3):
+            store_z_modes(zs, zd, 0, comp, here, right_ref[1, comp, here] * has_right * inverse)
+            store_z_modes(zs1, zd1, 0, comp, here, v1_ref[0, comp, here])
+            store_z_modes(zs_far, zd_far, 0, comp, here, v1_ref[1, comp, here])
+        return done
+
+    lax.fori_loop(0, CHUNKS, start, 0)
+
+    def outer(chunk, done):
+        here = rows_at(chunk)
+        moduli = [modulus_rows(e_ref, plane, chunk) for plane in (3, 4)]
+        planes = [(zs0, zd0, 2), (zs0, zd0, 3), (zs, zd, 0)]
+        for _, forces in apply_rows(planes, moduli, carry.at[0:1], chunk):
+            inverse = inv_ref[3, here]
+            for comp in range(3):
+                kept = right_ref[2, comp, here] * has_right > 0.0
+                before = right_ref[0, comp, here] * has_right * inverse
+                _, value = advance(forces[comp], kept, before, inverse)
+                store_z_modes(zs_far, zd_far, 1, comp, here, value)
+        return done
+
+    lax.fori_loop(0, CHUNKS, outer, 0)
+
+    def apply(chunk, totals):
+        here = rows_at(chunk)
+        odd, even = totals
+        moduli = [modulus_rows(e_ref, plane, chunk) for plane in (2, 3)]
+        planes = [(zs1, zd1, 0), (zs_far, zd_far, 0), (zs_far, zd_far, 1)]
+        for plane, forces in apply_rows(planes, moduli, carry.at[1:3], chunk, first_edge=True):
+            if plane == 0:
+                for comp in range(3):
+                    force_ref[comp, here] = forces[comp]
+                continue
+            inverse = inv_ref[2, here]
+            for comp in range(3):
+                kept = keep_ref[1, comp, here] > 0.0
+                before = v1_ref[1, comp, here]
+                image, value = advance(forces[comp], kept, before, inverse)
+                v2_ref[comp, here] = value
+                store_z_modes(zs2, zd2, 0, comp, here, value)
+                odd = odd + before * image
+                even = even + value * image
+        return odd, even
+
+    mom3, mom4 = lax.fori_loop(0, CHUNKS, apply, (zero, zero))
+    at_end = end_flag()
+
+    def last(chunk, total):
+        modes = plane_modes(zs2, zd2, 0, chunk)
+        energy = element_energy(element_modes(modes, zero_modes()))
+        return total + modulus_rows(e_ref, 3, chunk) * energy
+
+    mom5 = at_end * lax.fori_loop(0, CHUNKS, last, zero)
+    mom_ref[...] = sofar_ref[...] + folded([zero] * 3 + [mom3, mom4, mom5] + [zero] * 2)
+
+
 def second_kernel(
-    v1_left_ref, v1_ref, v1_far_ref, keep_left_ref, keep_ref, e_ref, inv_ref, sofar_ref,
+    v1_left_ref, v1_ref, keep_left_ref, keep_ref, e_ref, inv_ref,
+    zs1, zd1, zs2_far, zd2_far, force_ref, sofar_ref,
     v2_ref, mom_ref,
     zs, zd, zs2, zd2, carry,
 ):
-    v1_planes = [v1_left_ref.at[0], v1_left_ref.at[1], v1_ref.at[0], v1_ref.at[1], v1_far_ref]
-    keeps = [keep_left_ref.at[1], keep_ref.at[0], keep_ref.at[1]]
     clear_tails([zs, zd, zs2, zd2])
     clear_carry(carry)
     zero = jnp.zeros((ROWS, NZ), F32)
 
     def start(chunk, done):
         here = rows_at(chunk)
-        for plane in range(5):
-            for comp in range(3):
-                store_z_modes(zs, zd, plane, comp, here, v1_planes[plane][comp, here])
+        for plane in range(2):
+            for comp in range(3):
+                store_z_modes(zs, zd, plane, comp, here, v1_left_ref[plane, comp, here])
         return done
 
     lax.fori_loop(0, CHUNKS, start, 0)
@@ -343,25 +426,34 @@
     def apply(chunk, totals):
         here = rows_at(chunk)
         odd, even = totals
-        for plane, forces in apply_rows(zs, zd, 5, e_ref, 0, 1, carry, chunk):
+        moduli = [modulus_rows(e_ref, plane, chunk) for plane in (0, 1)]
+        planes = [(zs, zd, 0), (zs, zd, 1), (zs1, zd1, 0)]
+        for plane, forces in apply_rows(planes, moduli, carry, chunk, last_edge=True):
             inverse = inv_ref[plane - 1, here]
             for comp in range(3):
-                kept = keeps[plane - 1][comp, here] > 0.0
-                before = v1_planes[plane][comp, here]
-                image, value = advance(forces[comp], kept, before, inverse)
+                if plane == 1:
+                    kept, before = keep_left_ref[1, comp, here] > 0.0, v1_left_ref[1, comp, here]
+                    force = forces[comp]
+                else:
+                    kept, before = keep_ref[0, comp, here] > 0.0, v1_ref[0, comp, here]
+                    force = forces[comp] + force_ref[comp, here]
+                image, value = advance(force, kept, before, inverse)
                 v2_ref[plane - 1, comp, here] = value
                 store_z_modes(zs2, zd2, plane - 1, comp, here, value)
-                if plane > 1:
+                if plane == 2:
                     odd = odd + before * image
                     even = even + value * image
         return odd, even
 
     mom3, mom4 = lax.fori_loop(0, CHUNKS, apply, (zero, zero))
-    at_end = end_flag()
 
     def last(chunk, total):
-        for plane, energy in enumerate(energies(zs2, zd2, chunk)):
-            total = total + (e_ref[1 + plane, rows_at(chunk + 1)] * energy) * (at_end if plane == 2 else 1.0)
+        low = plane_modes(zs2, zd2, 0, chunk)
+        for plane, where in enumerate(((zs2, zd2, 1), (zs2_far, zd2_far, 0))):
+            high = plane_modes(*where, chunk)
+            energy = element_energy(element_modes(low, high))
+            total = total + modulus_rows(e_ref, 1 + plane, chunk) * energy
+            low = high
         return total
 
     mom5 = lax.fori_loop(0, CHUNKS, last, zero)
@@ -370,6 +462,10 @@
         mom_ref[device] = total
 
 
+def zero_modes():
+    return [{pair: jnp.zeros((ROWS, NZ), F32) for pair in PAIRS}] * 3
+
+
 def end_flag():
     at_end = lax.axis_index("space") == lax.axis_size("space") - 1
     return jnp.where(at_end, 1.0, 0.0).astype(F32)
@@ -377,13 +473,12 @@
 
 def energies(zs, zd, chunk):
     planes = [plane_modes(zs, zd, plane, chunk) for plane in range(3)]
-    zero = {pair: jnp.zeros((ROWS, NZ), F32) for pair in PAIRS}
-    planes.append([zero] * 3)
+    planes.append(zero_modes())
     for low, high in zip(planes[:-1], planes[1:]):
         yield element_energy(element_modes(low, high))
 
 
-def energy_kernel(v0_ref, v1_left_ref, v1_ref, v2_ref, mom_ref, u_ref, out_ref, zs, zd, e_ref):
+def energy_kernel(v0_ref, v1_left_ref, v1_ref, v2_ref, v2_far_ref, mom_ref, u_ref, out_ref, zs, zd, e_ref):
     total = mom_ref[0]
     for device in range(1, mom_ref.shape[0]):
         total = total + mom_ref[device]
@@ -410,13 +505,14 @@
         e_ref[plane, 0:ROWS] = jnp.zeros((ROWS, NZ), F32)
         e_ref[plane, NY + ROWS : NY + 2 * ROWS] = jnp.zeros((ROWS, NZ), F32)
     v1_planes = [v1_left_ref.at[1], v1_ref.at[0], v1_ref.at[1]]
+    v2_planes = [v2_ref.at[0], v2_ref.at[1], v2_far_ref]
 
     def combine(chunk, done):
         here = rows_at(chunk)
         for plane in range(3):
             for comp in range(3):
                 value = c0 * v0_ref[plane, comp, here] + c1 * v1_planes[plane][comp, here]
-                value = value + c2 * v2_ref[plane, comp, here]
+                value = value + c2 * v2_planes[plane][comp, here]
                 if plane > 0:
                     u_ref[comp, plane - 1, here] = value
                 store_z_modes(zs, zd, plane, comp, here, value)
@@ -513,32 +609,40 @@
     dens = lax.all_to_all(dens, "load", 0, 0)
 
     padded = (NY + ROWS, NZ)
-    zed = lambda planes: pltpu.VMEM((planes, 3) + padded, F32)
-    carry = pltpu.VMEM((3, 3, ROWS, NZ), F32)
-    v0, v1, v1_far, modulus, inverse, mom = kernel_call(
+    modes = lambda planes: (planes, 3) + padded
+    zed = lambda planes: pltpu.VMEM(modes(planes), F32)
+    carried = lambda slots: pltpu.VMEM((slots, 3, ROWS, NZ), F32)
+    v1, v0, modulus, inverse, zs0, zd0, mom = kernel_call(
         first_kernel,
-        [(3,) + plane, (2,) + plane, plane, (6,) + padded, (4, NY, NZ), (8, 128)],
+        [(2,) + plane, (3,) + plane, (6,) + padded, (4, NY, NZ), modes(4), modes(4), (8, 128)],
         0,
         5,
-        [zed(5), zed(5), carry],
+        [carried(2)],
     )(load, keep, left, right, dens)
     v1_left = shifted(v1, "space", 1)
+    v2_far, zs1, zd1, zs2, zd2, force, mom = kernel_call(
+        middle_kernel,
+        [plane, modes(1), modes(1), modes(1), modes(1), plane, (8, 128)],
+        0,
+        8,
+        [zed(1), zed(1), zed(2), zed(2), carried(3)],
+    )(v1, zs0, zd0, modulus, inverse, right, keep, mom)
     v2, mom = kernel_call(
         second_kernel,
-        [(3,) + plane, (n_space, 8, 128)],
+        [(2,) + plane, (n_space, 8, 128)],
         0,
-        8,
-        [zed(5), zed(5), zed(3), zed(3), carry],
-    )(v1_left, v1, v1_far, left, keep, modulus, inverse, mom)
+        12,
+        [zed(2), zed(2), zed(2), zed(2), carried(2)],
+    )(v1_left, v1, left, keep, modulus, inverse, zs1, zd1, zs2, zd2, force, mom)
     mom = lax.all_to_all(mom, "space", 0, 0)
     span = ROWS + 2
     moved, energy = kernel_call(
         energy_kernel,
         [(3, CX, NY, NZ), (CHUNKS, 3 * span, NZ)],
         0,
-        5,
+        6,
         [zed(3), zed(3), pltpu.VMEM((3, NY + 2 * ROWS, NZ), F32)],
-    )(v0, v1_left, v1, v2, mom)
+    )(v0, v1_left, v1, v2, v2_far, mom)
     energy = jnp.sum(lax.all_to_all(energy, "load", 0, 0), axis=0)
     following = shifted(energy[: 2 * span], "space", -1)
     (filtered,) = kernel_call(filter_kernel, [(CX, ROWS, NZ)], 0, 3)(energy, following, dens)

time: 73.2 us -> 71.8 us (0.981)
  waiting for transfers between devices: 6.43 us -> 1.71 us
  Pallas kernels: 11.5 us -> 15.5 us
    ppermute x6, waiting for transfers between devices: 6.43 us -> 1.71 us  [shifted(): lax.ppermute(array, axis, [(i, (i + distance) % size) for i in range(size)])]
    pallas_call x2 -> x3, Pallas kernels: 7.94 us -> 11.9 us  [the longest x1 5.44 us: body(): kernel_call(middle_kernel, [plane, modes(1), modes(1), modes(1), modes(1)...]
    all_to_all x1, blocking collectives: 12.8 us -> 12.1 us  [body(): mom = lax.all_to_all(mom, 'space', 0, 0)]
  transfers between devices with their start and end apart: 6 -> 6, of which waited for: 2 -> 1; matrix products, arithmetic and copies ran while one was open for 1% -> 1% of each run, Pallas kernels for 1% -> 8%
where the time goes in v4:
time: 71.8 us; the launch traced here: 71.4 us
  blocking collectives  41.9 us (58%)
  Pallas kernels  15.5 us (22%)
  starting transfers between devices  8.06 us (11%)
  local copies, waits for them, and re-layouts  3.52 us (5%)
  waiting for transfers between devices  1.71 us (2%)
    all_to_all x1, blocking collectives, body(): dens = lax.all_to_all(dens, 'load', 0, 0)  17.8 us
    all_to_all x1, blocking collectives, body(): mom = lax.all_to_all(mom, 'space', 0, 0)  12.1 us
    all_to_all x1, blocking collectives, body(): energy = jnp.sum(lax.all_to_all(energy, 'load', 0, 0), axis=0)  12 us
    ppermute x6, starting transfers between devices, shifted(): lax.ppermute(array, axis, [(i, (i + distance) % size) for i in range(size)])  8.06 us
    pallas_call x1, Pallas kernels, body(): kernel_call(middle_kernel, [plane, modes(1), modes(1), modes(1), modes(1)...  5.44 us
    unnamed x9, local copies, waits for them, and re-layouts  3.51 us
    pallas_call x1, Pallas kernels, body(): kernel_call(second_kernel, [(2,) + plane, (n_space, 8, 128)], 0, 12, [zed...  3.27 us
    pallas_call x1, Pallas kernels, body(): kernel_call(first_kernel, [(2,) + plane, (3,) + plane, (6,) + padded, (4,...  3.24 us
  transfers between devices with their start and end apart: 6, of which 1 were waited for; matrix products, arithmetic and copies ran while one was open for 1% of the time, Pallas kernels for 8%

profile of v4, /device:TPU:1, one launch (start us, length us, event | category | flops | bytes accessed | tf_op | source)
XLA Modules:
  0.0 71.4 jit_solution(10378676115203982765)
XLA Ops:
  0.6 2.7 %collective-permute-start = (f32[2,8,256]{2,1,0:T(8,128)}, f32[2,8,256]{2,1,0:T(8,128)S(1)}, u32[]{:S(2)}, u32[]{:S(2)}) collective-permute-start(f32[2,8,256]{2,1,0:T(8,128)} %own_ref.1), channel_id=1, source_target_pairs={{0,1},{1,2},{2,3},{3,4},{4,5},{5,6},{6,7},{7,8},{8,9},{9,10},{10,1... | collective-permute-start | bytes 49160 | tf_op jit(solution)/shard_map/ppermute | solution.py:592
  3.3 0.0 collective-permute-start.1
  3.3 0.7 copy.9
  4.0 0.7 copy-done.3
  4.6 1.0 %copy-done = f32[1,3,2,64,256]{4,3,2,1,0:T(8,128)S(1)} copy-done((f32[1,3,2,64,256]{4,3,2,1,0:T(8,128)S(1)}, f32[1,3,2,64,256]{4,3,2,1,0:T(8,128)}, u32[]{:S(2)}) %copy-start) | copy-done | bytes 393240
  5.6 1.0 %copy-done.1 = s32[3,2,64,256]{3,2,1,0:T(8,128)S(1)} copy-done((s32[3,2,64,256]{3,2,1,0:T(8,128)S(1)}, s32[3,2,64,256]{3,2,1,0:T(8,128)}, u32[]{:S(2)}) %copy-start.1) | copy-done | bytes 393240
  6.6 0.5 shard_map.68
  7.1 0.0 collective-permute-done.before_ref
  7.2 0.0 collective-permute-done.1.after_ref
  7.2 0.2 copy-done.2
  7.4 2.7 %collective-permute-start.3 = (f32[3,3,64,256]{3,2,1,0:T(8,128)S(1)}, f32[3,3,64,256]{3,2,1,0:T(8,128)S(1)}, u32[]{:S(2)}, u32[]{:S(2)}) collective-permute-start(f32[3,3,64,256]{3,2,1,0:T(8,128)S(1)} %get-tuple-element.32), channel_id=1, source_target_pairs={{0,15},{1,0},{2,1},{3,2},{4,3},{5,4},{6,5},{7,6},{8,7},{9,8},{10,9... | collective-permute-start | bytes 1769480 | tf_op jit(solution)/shard_map/ppermute | solution.py:592
  10.1 17.8 %all_to_all.15.dens_ref = f32[8,6,8,256]{3,2,1,0:T(8,128)S(1)} all-to-all(f32[8,6,8,256]{3,2,1,0:T(8,128)S(1)} %shard_map.69), channel_id=1, replica_groups=mesh['load'=8,'space'=16] {'load'}, dimensions={0} | all-to-all | bytes 786432 | tf_op jit(solution)/shard_map/all_to_all | solution.py:609
  27.9 0.0 collective-permute-done.3.right_ref
  27.9 3.2 %shard_map.70 = (f32[2,3,64,256]{3,2,1,0:T(8,128)S(1)}, f32[3,3,64,256]{3,2,1,0:T(8,128)S(1)}, f32[6,72,256]{2,1,0:T(8,128)S(1)}, f32[4,64,256]{2,1,0:T(8,128)S(...) custom-call(f32[2,3,64,256]{3,2,1,0:T(8,128)S(1)} %get-tuple-element.27.load_ref, ...), custom_call_target="tpu_custom_call" | custom-call | tf_op jit(solution)/shard_map/pallas_call | solution.py:615
  31.2 0.9 %collective-permute-start.4 = (f32[2,3,64,256]{3,2,1,0:T(8,128)S(1)}, f32[2,3,64,256]{3,2,1,0:T(8,128)S(1)}, u32[]{:S(2)}, u32[]{:S(2)}) collective-permute-start(f32[2,3,64,256]{3,2,1,0:T(8,128)S(1)} %get-tuple-element.35.v1_ref), channel_id=1, source_target_pairs={{0,1},{1,2},{2,3},{3,4},{4,5},{5,6},{6,7},{7,8},{8,9},{9,10},{10,1... | collective-permute-start | bytes 1179656 | tf_op jit(solution)/shard_map/ppermute | solution.py:592
  32.1 5.4 %shard_map.71 = (f32[3,64,256]{2,1,0:T(8,128)S(1)}, f32[1,3,72,256]{3,2,1,0:T(8,128)S(1)}, f32[1,3,72,256]{3,2,1,0:T(8,128)S(1)}, f32[1,3,72,256]{3,2,1,0:T(8,12...) custom-call(f32[2,3,64,256]{3,2,1,0:T(8,128)S(1)} %get-tuple-element.35.v1_ref, ...), custom_call_target="tpu_custom_call" | custom-call | tf_op jit(solution)/shard_map/pallas_call | solution.py:623
  37.6 0.0 collective-permute-done.4.v1_left_ref
  37.6 3.3 %shard_map.72 = (f32[2,3,64,256]{3,2,1,0:T(8,128)S(1)}, f32[16,8,128]{2,1,0:T(8,128)S(1)}) custom-call(f32[2,3,64,256]{3,2,1,0:T(8,128)S(1)} %collective-permute-done.4.v1_left_ref, f32[2,3,64,256]{3,2,1,0:T(8,128)S(1)} %get-tuple-element.35.v1_ref, f32[2,3,64,256]{3,2,1,0:T(8,128)S(1)} %collective-permute-done.2.left_ref.keep_left_ref, ...), custom_call_target="tpu_custom_call" | custom-call | tf_op jit(solution)/shard_map/pallas_call | solution.py:630
  40.9 12.1 %all_to_all.16.mom_ref = f32[16,8,128]{2,1,0:T(8,128)S(1)} all-to-all(f32[16,8,128]{2,1,0:T(8,128)S(1)} %get-tuple-element.49), channel_id=1, replica_groups=mesh['load'=8,'space'=16] {'space'}, dimensions={0} | all-to-all | bytes 131072 | tf_op jit(solution)/shard_map/all_to_all | solution.py:637
  52.9 2.3 %shard_map.73 = (f32[3,2,64,256]{3,2,1,0:T(8,128)}, f32[8,30,256]{2,1,0:T(8,128)S(1)}) custom-call(f32[3,3,64,256]{3,2,1,0:T(8,128)S(1)} %get-tuple-element.34.v0_ref, f32[2,3,64,256]{3,2,1,0:T(8,128)S(1)} %collective-permute-done.4.v1_left_ref, f32[2,3,64,256]{3,2,1,0:T(8,128)S(1)} %get-tuple-element.35.v1_ref, ...), custom_call_target="tpu_custom_call" | custom-call | tf_op jit(solution)/shard_map/pallas_call | solution.py:639
  55.2 12.0 %all_to_all.17 = f32[8,30,256]{2,1,0:T(8,128)S(1)} all-to-all(f32[8,30,256]{2,1,0:T(8,128)S(1)} %get-tuple-element.51), channel_id=1, replica_groups=mesh['load'=8,'space'=16] {'load'}, dimensions={0} | all-to-all | bytes 491520 | tf_op jit(solution)/shard_map/all_to_all | solution.py:646
  67.3 1.7 %collective-permute-start.5 = (f32[20,256]{1,0:T(8,128)S(1)}, f32[20,256]{1,0:T(8,128)S(1)}, u32[]{:S(2)}, u32[]{:S(2)}) collective-permute-start(f32[20,256]{1,0:T(8,128)S(1)} %slice.4), channel_id=1, source_target_pairs={{0,15},{1,0},{2,1},{3,2},{4,3},{5,4},{6,5},{7,6},{8,7},{9,8},{10,9... | collective-permute-start | bytes 61448 | tf_op jit(solution)/shard_map/ppermute | solution.py:592
  69.0 1.7 %collective-permute-done.5.next_ref = f32[20,256]{1,0:T(8,128)S(1)} collective-permute-done((f32[20,256]{1,0:T(8,128)S(1)}, f32[20,256]{1,0:T(8,128)S(1)}, u32[]{:S(2)}, u32[]{:S(2)}) %collective-permute-start.5) | collective-permute-done | bytes 20512 | tf_op jit(solution)/shard_map/ppermute | solution.py:592
  70.7 0.7 %shard_map.74 = f32[2,8,256]{2,1,0:T(8,128)} custom-call(f32[30,256]{1,0:T(8,128)S(1)} %reduce_sum.9.energy_ref, f32[20,256]{1,0:T(8,128)S(1)} %collective-permute-done.5.next_ref, f32[8,6,8,256]{3,2,1,0:T(8,128)S(1)} %all_to_all.15.dens_ref), custom_call_target="tpu_custom_call" | custom-call | tf_op jit(solution)/shard_map/pallas_call | solution.py:648
  (9 shorter events, 0.1 us)
Async XLA Ops:
  0.6 6.5 %collective-permute-start = (f32[2,8,256]{2,1,0:T(8,128)}, f32[2,8,256]{2,1,0:T(8,128)S(1)}, u32[]{:S(2)}, u32[]{:S(2)}) collective-permute-start(f32[2,8,256]{2,1,0:T(8,128)} %own_ref.1), channel_id=1, source_target_pairs={{0,1},{1,2},{2,3},{3,4},{4,5},{5,6},{6,7},{7,8},{8,9},{9,10},{10,1... | collective-permute-start | bytes 49160 | tf_op jit(solution)/shard_map/ppermute | solution.py:592
  3.3 3.9 %collective-permute-start.1 = (f32[2,8,256]{2,1,0:T(8,128)}, f32[2,8,256]{2,1,0:T(8,128)S(1)}, u32[]{:S(2)}, u32[]{:S(2)}) collective-permute-start(f32[2,8,256]{2,1,0:T(8,128)} %own_ref.1), channel_id=1, source_target_pairs={{0,15},{1,0},{2,1},{3,2},{4,3},{5,4},{6,5},{7,6},{8,7},{9,8},{10,9... | collective-permute-start | bytes 49160 | tf_op jit(solution)/shard_map/ppermute | solution.py:592
  4.0 0.7 copy-start.3
  4.6 1.0 %copy-start = (f32[1,3,2,64,256]{4,3,2,1,0:T(8,128)S(1)}, f32[1,3,2,64,256]{4,3,2,1,0:T(8,128)}, u32[]{:S(2)}) copy-start(f32[1,3,2,64,256]{4,3,2,1,0:T(8,128)} %param.7) | copy-start | bytes 1179652
  5.6 1.0 %copy-start.1 = (s32[3,2,64,256]{3,2,1,0:T(8,128)S(1)}, s32[3,2,64,256]{3,2,1,0:T(8,128)}, u32[]{:S(2)}) copy-start(s32[3,2,64,256]{3,2,1,0:T(8,128)} %fixed_ref.1) | copy-start | bytes 1179652
  6.6 0.7 %copy-start.2 = (f32[2,8,256]{2,1,0:T(8,128)S(1)}, f32[2,8,256]{2,1,0:T(8,128)}, u32[]{:S(2)}) copy-start(f32[2,8,256]{2,1,0:T(8,128)} %own_ref.1) | copy-start | bytes 49156
  7.4 20.5 %collective-permute-start.3 = (f32[3,3,64,256]{3,2,1,0:T(8,128)S(1)}, f32[3,3,64,256]{3,2,1,0:T(8,128)S(1)}, u32[]{:S(2)}, u32[]{:S(2)}) collective-permute-start(f32[3,3,64,256]{3,2,1,0:T(8,128)S(1)} %get-tuple-element.32), channel_id=1, source_target_pairs={{0,15},{1,0},{2,1},{3,2},{4,3},{5,4},{6,5},{7,6},{8,7},{9,8},{10,9... | collective-permute-start | bytes 1769480 | tf_op jit(solution)/shard_map/ppermute | solution.py:592
  10.1 17.8 %collective-permute-start.2 = (f32[2,3,64,256]{3,2,1,0:T(8,128)S(1)}, f32[2,3,64,256]{3,2,1,0:T(8,128)S(1)}, u32[]{:S(2)}, u32[]{:S(2)}) collective-permute-start(f32[2,3,64,256]{3,2,1,0:T(8,128)S(1)} %get-tuple-element.31), channel_id=1, source_target_pairs={{0,1},{1,2},{2,3},{3,4},{4,5},{5,6},{6,7},{7,8},{8,9},{9,10},{10,1... | collective-permute-start | bytes 1179656 | tf_op jit(solution)/shard_map/ppermute | solution.py:592
  31.2 6.4 %collective-permute-start.4 = (f32[2,3,64,256]{3,2,1,0:T(8,128)S(1)}, f32[2,3,64,256]{3,2,1,0:T(8,128)S(1)}, u32[]{:S(2)}, u32[]{:S(2)}) collective-permute-start(f32[2,3,64,256]{3,2,1,0:T(8,128)S(1)} %get-tuple-element.35.v1_ref), channel_id=1, source_target_pairs={{0,1},{1,2},{2,3},{3,4},{4,5},{5,6},{6,7},{7,8},{8,9},{9,10},{10,1... | collective-permute-start | bytes 1179656 | tf_op jit(solution)/shard_map/ppermute | solution.py:592
  67.3 3.4 %collective-permute-start.5 = (f32[20,256]{1,0:T(8,128)S(1)}, f32[20,256]{1,0:T(8,128)S(1)}, u32[]{:S(2)}, u32[]{:S(2)}) collective-permute-start(f32[20,256]{1,0:T(8,128)S(1)} %slice.4), channel_id=1, source_target_pairs={{0,15},{1,0},{2,1},{3,2},{4,3},{5,4},{6,5},{7,6},{8,7},{9,8},{10,9... | collective-permute-start | bytes 61448 | tf_op jit(solution)/shard_map/ppermute | solution.py:592

commit v5 on v4

--- a/solution.py
+++ b/solution.py
@@ -25,13 +25,13 @@
 PAIRS = ("ss", "sd", "ds", "dd")
 
 
-def kernel_call(fn, outs, n_smem, n_in, scratch=()):
+def kernel_call(fn, outs, n_hbm, n_in, scratch=()):
     vmem = pl.BlockSpec(memory_space=pltpu.VMEM)
-    smem = pl.BlockSpec(memory_space=pltpu.SMEM)
+    hbm = pl.BlockSpec(memory_space=pltpu.HBM)
     return pl.pallas_call(
         fn,
         out_shape=[jax.ShapeDtypeStruct(shape, F32) for shape in outs],
-        in_specs=[smem] * n_smem + [vmem] * n_in,
+        in_specs=[hbm] * n_hbm + [vmem] * n_in,
         out_specs=[vmem] * len(outs),
         scratch_shapes=list(scratch),
         compiler_params=pltpu.CompilerParams(vmem_limit_bytes=VMEM_LIMIT),
@@ -198,8 +198,15 @@
 
 
 def loads_kernel(
-    body_ref, fixed_ref, node_ref, force_ref, load_ref, keep_ref, right_ref, left_ref
+    body_hbm, fixed_hbm, node_hbm, force_hbm, load_ref, keep_ref, right_ref, left_ref,
+    body_ref, fixed_ref, node_ref, force_ref, sems,
 ):
+    pairs = ((node_hbm, node_ref), (force_hbm, force_ref), (body_hbm, body_ref), (fixed_hbm, fixed_ref))
+    copies = [pltpu.make_async_copy(src, dst, sems.at[k]) for k, (src, dst) in enumerate(pairs)]
+    for copy in copies:
+        copy.start()
+    copies[0].wait()
+    copies[1].wait()
     cells = CX * NY * NZ
     local = node_ref[...] - lax.axis_index("space") * cells
     valid = (local >= 0) & (local < cells)
@@ -208,7 +215,7 @@
     depth = lax.bitwise_and(local, NZ - 1)
     points = local.shape[1]
     on_line = row_ids((CX * NY, points)) == line
-    lines = [jnp.where(on_line, force_ref[comp : comp + 1, :], 0.0) for comp in range(3)]
+    lines = [jnp.where(on_line, force_ref[comp], 0.0) for comp in range(3)]
     at_depth = jnp.where(row_ids((NZ, points)) == depth, 1.0, 0.0)
     added = lax.dot_general(
         jnp.concatenate(lines, axis=0),
@@ -217,11 +224,13 @@
         precision=lax.Precision.HIGHEST,
         preferred_element_type=F32,
     )
+    copies[2].wait()
+    copies[3].wait()
     for plane in range(CX):
         for comp in range(3):
             keep = 1.0 - fixed_ref[comp, plane].astype(F32)
             first = (comp * CX + plane) * NY
-            load = keep * (body_ref[comp, plane] + added[first : first + NY])
+            load = keep * (body_ref[0, comp, plane] + added[first : first + NY])
             load_ref[plane, comp] = load
             keep_ref[plane, comp] = keep
             left_ref[plane, comp] = load
@@ -314,7 +323,7 @@
                 store_z_modes(zs, zd, plane, comp, here, value)
         return total
 
-    mom0 = lax.fori_loop(0, CHUNKS, start, zero)
+    mom0 = lax.fori_loop(0, CHUNKS, start, zero, unroll=CHUNKS // 2)
 
     def apply(chunk, totals):
         here = rows_at(chunk)
@@ -331,7 +340,7 @@
                 even = even + value * image
         return odd, even
 
-    mom1, mom2 = lax.fori_loop(0, CHUNKS, apply, (zero, zero))
+    mom1, mom2 = lax.fori_loop(0, CHUNKS, apply, (zero, zero), unroll=CHUNKS // 2)
     mom_ref[...] = folded([mom0, mom1, mom2] + [zero] * 5)
 
 
@@ -354,7 +363,7 @@
             store_z_modes(zs_far, zd_far, 0, comp, here, v1_ref[1, comp, here])
         return done
 
-    lax.fori_loop(0, CHUNKS, start, 0)
+    lax.fori_loop(0, CHUNKS, start, 0, unroll=CHUNKS)
 
     def outer(chunk, done):
         here = rows_at(chunk)
@@ -369,7 +378,7 @@
                 store_z_modes(zs_far, zd_far, 1, comp, here, value)
         return done
 
-    lax.fori_loop(0, CHUNKS, outer, 0)
+    lax.fori_loop(0, CHUNKS, outer, 0, unroll=CHUNKS)
 
     def apply(chunk, totals):
         here = rows_at(chunk)
@@ -392,7 +401,7 @@
                 even = even + value * image
         return odd, even
 
-    mom3, mom4 = lax.fori_loop(0, CHUNKS, apply, (zero, zero))
+    mom3, mom4 = lax.fori_loop(0, CHUNKS, apply, (zero, zero), unroll=CHUNKS)
     at_end = end_flag()
 
     def last(chunk, total):
@@ -400,7 +409,7 @@
         energy = element_energy(element_modes(modes, zero_modes()))
         return total + modulus_rows(e_ref, 3, chunk) * energy
 
-    mom5 = at_end * lax.fori_loop(0, CHUNKS, last, zero)
+    mom5 = at_end * lax.fori_loop(0, CHUNKS, last, zero, unroll=CHUNKS)
     mom_ref[...] = sofar_ref[...] + folded([zero] * 3 + [mom3, mom4, mom5] + [zero] * 2)
 
 
@@ -421,7 +430,7 @@
                 store_z_modes(zs, zd, plane, comp, here, v1_left_ref[plane, comp, here])
         return done
 
-    lax.fori_loop(0, CHUNKS, start, 0)
+    lax.fori_loop(0, CHUNKS, start, 0, unroll=CHUNKS)
 
     def apply(chunk, totals):
         here = rows_at(chunk)
@@ -445,7 +454,7 @@
                     even = even + value * image
         return odd, even
 
-    mom3, mom4 = lax.fori_loop(0, CHUNKS, apply, (zero, zero))
+    mom3, mom4 = lax.fori_loop(0, CHUNKS, apply, (zero, zero), unroll=CHUNKS)
 
     def last(chunk, total):
         low = plane_modes(zs2, zd2, 0, chunk)
@@ -456,7 +465,7 @@
             low = high
         return total
 
-    mom5 = lax.fori_loop(0, CHUNKS, last, zero)
+    mom5 = lax.fori_loop(0, CHUNKS, last, zero, unroll=CHUNKS)
     total = sofar_ref[...] + folded([zero] * 3 + [mom3, mom4, mom5] + [zero] * 2)
     for device in range(mom_ref.shape[0]):
         mom_ref[device] = total
@@ -518,7 +527,7 @@
                 store_z_modes(zs, zd, plane, comp, here, value)
         return done
 
-    lax.fori_loop(0, CHUNKS, combine, 0)
+    lax.fori_loop(0, CHUNKS, combine, 0, unroll=CHUNKS)
     at_end = end_flag()
 
     def measure(chunk, done):
@@ -526,7 +535,7 @@
             e_ref[plane, rows_at(chunk + 1)] = energy * (at_end if plane == 2 else 1.0)
         return done
 
-    lax.fori_loop(0, CHUNKS, measure, 0)
+    lax.fori_loop(0, CHUNKS, measure, 0, unroll=CHUNKS)
     span = ROWS + 2
     for block in range(CHUNKS):
         for plane in range(3):
@@ -597,9 +606,20 @@
     dens_left = shifted(density, "space", 1)
     dens_right = shifted(density, "space", -1)
     plane = (3, NY, NZ)
+    by_component = jnp.swapaxes(point_forces, 0, 1)
     load, keep, to_right, to_left = kernel_call(
-        loads_kernel, [(2,) + plane, (2,) + plane, (2,) + plane, (3,) + plane], 0, 4
-    )(body_loads[0], fixed_dofs, point_nodes, point_forces[0])
+        loads_kernel,
+        [(2,) + plane, (2,) + plane, (2,) + plane, (3,) + plane],
+        4,
+        0,
+        [
+            pltpu.VMEM(body_loads.shape, F32),
+            pltpu.VMEM(fixed_dofs.shape, jnp.int32),
+            pltpu.VMEM(point_nodes.shape, jnp.int32),
+            pltpu.VMEM(by_component.shape, F32),
+            pltpu.SemaphoreType.DMA((4,)),
+        ],
+    )(*[pltpu.with_memory_space_constraint(x, pltpu.HBM) for x in (body_loads, fixed_dofs, point_nodes, by_component)])
     (dens,) = kernel_call(pack_kernel, [(n_load, 3 * CX, ROWS, NZ)], 0, 3)(
         dens_left, density, dens_right
     )

time: 71.8 us -> 67.8 us (0.944)
  Pallas kernels: 15.5 us -> 9.42 us
  waiting for transfers between devices: 1.71 us -> 6.43 us
  local copies, waits for them, and re-layouts: 3.52 us -> 0.01 us
  blocking collectives: 41.9 us -> 44.8 us
  starting transfers between devices: 8.06 us -> 6.26 us
    ppermute x6, waiting for transfers between devices: 1.71 us -> 6.43 us  [shifted(): lax.ppermute(array, axis, [(i, (i + distance) % size) for i in range(size)])]
    unnamed x9 -> x2, local copies, waits for them, and re-layouts: 3.51 us -> 0.01 us
    pallas_call x1, Pallas kernels: 5.44 us -> 2.29 us  [body(): kernel_call(middle_kernel, [plane, modes(1), modes(1), modes(1), modes(1)...]
    ppermute x6, starting transfers between devices: 8.06 us -> 6.26 us  [shifted(): lax.ppermute(array, axis, [(i, (i + distance) % size) for i in range(size)])]
    all_to_all x1, blocking collectives: 12.1 us -> 13.7 us  [body(): mom = lax.all_to_all(mom, 'space', 0, 0)]
    pallas_call x1, Pallas kernels: 3.27 us -> 1.78 us  [body(): kernel_call(second_kernel, [(2,) + plane, (n_space, 8, 128)], 0, 12, [zed...]
    pallas_call x1, Pallas kernels: 3.24 us -> 1.91 us  [body(): kernel_call(first_kernel, [(2,) + plane, (3,) + plane, (6,) + padded, (4,...]
    all_to_all x1, blocking collectives: 17.8 us -> 19.1 us  [body(): dens = lax.all_to_all(dens, 'load', 0, 0)]
  transfers between devices with their start and end apart: 6 -> 6, of which waited for: 1 -> 3; matrix products, arithmetic and copies ran while one was open for 1% -> 0% of each run, Pallas kernels for 8% -> 5%
where the time goes in v5:
time: 67.8 us; the launch traced here: 67.6 us
  blocking collectives  44.8 us (66%)
  Pallas kernels  9.42 us (14%)
  waiting for transfers between devices  6.43 us (9%)
  starting transfers between devices  6.26 us (9%)
  between operations  0.7 us (1%)
    all_to_all x1, blocking collectives, body(): dens = lax.all_to_all(dens, 'load', 0, 0)  19.1 us
    all_to_all x1, blocking collectives, body(): mom = lax.all_to_all(mom, 'space', 0, 0)  13.7 us
    all_to_all x1, blocking collectives, body(): energy = jnp.sum(lax.all_to_all(energy, 'load', 0, 0), axis=0)  12 us
    ppermute x6, waiting for transfers between devices, shifted(): lax.ppermute(array, axis, [(i, (i + distance) % size) for i in range(size)])  6.43 us
    ppermute x6, starting transfers between devices, shifted(): lax.ppermute(array, axis, [(i, (i + distance) % size) for i in range(size)])  6.26 us
    pallas_call x1, Pallas kernels, body(): kernel_call(middle_kernel, [plane, modes(1), modes(1), modes(1), modes(1)...  2.29 us
    pallas_call x1, Pallas kernels, body(): kernel_call(first_kernel, [(2,) + plane, (3,) + plane, (6,) + padded, (4,...  1.91 us
    pallas_call x1, Pallas kernels, body(): kernel_call(second_kernel, [(2,) + plane, (n_space, 8, 128)], 0, 12, [zed...  1.78 us
  transfers between devices with their start and end apart: 6, of which 3 were waited for; matrix products, arithmetic and copies ran while one was open for 0% of the time, Pallas kernels for 5%

profile of v5, /device:TPU:1, one launch (start us, length us, event | category | flops | bytes accessed | tf_op | source)
XLA Modules:
  0.0 67.6 jit_solution(11896368148125898924)
XLA Ops:
  0.6 2.7 %collective-permute-start = (f32[2,8,256]{2,1,0:T(8,128)}, f32[2,8,256]{2,1,0:T(8,128)S(1)}, u32[]{:S(2)}, u32[]{:S(2)}) collective-permute-start(f32[2,8,256]{2,1,0:T(8,128)} %own_ref.1), channel_id=1, source_target_pairs={{0,1},{1,2},{2,3},{3,4},{4,5},{5,6},{6,7},{7,8},{8,9},{9,10},{10,1... | collective-permute-start | bytes 49160 | tf_op jit(solution)/shard_map/ppermute | solution.py:601
  3.3 0.0 collective-permute-start.1
  3.3 0.0 copy-start
  3.3 1.3 %shard_map.68 = (f32[2,3,64,256]{3,2,1,0:T(8,128)S(1)}, f32[2,3,64,256]{3,2,1,0:T(8,128)S(1)}, f32[2,3,64,256]{3,2,1,0:T(8,128)S(1)}, f32[3,3,64,256]{3,2,1,0:T(8,128)S(1)}) custom-call(f32[1,3,2,64,256]{4,3,2,1,0:T(8,128)} %body_hbm.1, s32[3,2,64,256]{3,2,1,0:T(8,128)} %fixed_hbm.1, s32[1,128]{1,0:T(1,128)} %node_hbm.1, f32[3,1,128]{2,1,0:T(1,128)} %bitcast.2), custom_call_target="tpu_custom_call" | custom-call | tf_op jit(solution)/shard_map/pallas_call | solution.py:610
  4.7 0.0 collective-permute-done.before_ref
  4.7 2.3 %collective-permute-done.1.after_ref = f32[2,8,256]{2,1,0:T(8,128)S(1)} collective-permute-done((f32[2,8,256]{2,1,0:T(8,128)}, f32[2,8,256]{2,1,0:T(8,128)S(1)}, u32[]{:S(2)}, u32[]{:S(2)}) %collective-permute-start.1) | collective-permute-done | bytes 16416 | tf_op jit(solution)/shard_map/ppermute | solution.py:601
  7.0 0.0 copy-done
  7.0 0.7 %collective-permute-start.3 = (f32[3,3,64,256]{3,2,1,0:T(8,128)S(1)}, f32[3,3,64,256]{3,2,1,0:T(8,128)S(1)}, u32[]{:S(2)}, u32[]{:S(2)}) collective-permute-start(f32[3,3,64,256]{3,2,1,0:T(8,128)S(1)} %get-tuple-element.32), channel_id=1, source_target_pairs={{0,15},{1,0},{2,1},{3,2},{4,3},{5,4},{6,5},{7,6},{8,7},{9,8},{10,9... | collective-permute-start | bytes 1769480 | tf_op jit(solution)/shard_map/ppermute | solution.py:601
  7.7 1.1 %collective-permute-start.2 = (f32[2,3,64,256]{3,2,1,0:T(8,128)S(1)}, f32[2,3,64,256]{3,2,1,0:T(8,128)S(1)}, u32[]{:S(2)}, u32[]{:S(2)}) collective-permute-start(f32[2,3,64,256]{3,2,1,0:T(8,128)S(1)} %get-tuple-element.31), channel_id=1, source_target_pairs={{0,1},{1,2},{2,3},{3,4},{4,5},{5,6},{6,7},{7,8},{8,9},{9,10},{10,1... | collective-permute-start | bytes 1179656 | tf_op jit(solution)/shard_map/ppermute | solution.py:601
  8.8 19.1 %all_to_all.15.dens_ref = f32[8,6,8,256]{3,2,1,0:T(8,128)S(1)} all-to-all(f32[8,6,8,256]{3,2,1,0:T(8,128)S(1)} %shard_map.69), channel_id=1, replica_groups=mesh['load'=8,'space'=16] {'load'}, dimensions={0} | all-to-all | bytes 786432 | tf_op jit(solution)/shard_map/all_to_all | solution.py:629
  27.9 0.0 collective-permute-done.2.left_ref.keep_left_ref
  27.9 0.0 collective-permute-done.3.right_ref
  27.9 1.9 %shard_map.70 = (f32[2,3,64,256]{3,2,1,0:T(8,128)S(1)}, f32[3,3,64,256]{3,2,1,0:T(8,128)S(1)}, f32[6,72,256]{2,1,0:T(8,128)S(1)}, f32[4,64,256]{2,1,0:T(8,128)S(...) custom-call(f32[2,3,64,256]{3,2,1,0:T(8,128)S(1)} %get-tuple-element.27.load_ref, ...), custom_call_target="tpu_custom_call" | custom-call | tf_op jit(solution)/shard_map/pallas_call | solution.py:635
  29.9 0.1 collective-permute-start.4
  29.9 2.3 %shard_map.71 = (f32[3,64,256]{2,1,0:T(8,128)S(1)}, f32[1,3,72,256]{3,2,1,0:T(8,128)S(1)}, f32[1,3,72,256]{3,2,1,0:T(8,128)S(1)}, f32[1,3,72,256]{3,2,1,0:T(8,12...) custom-call(f32[2,3,64,256]{3,2,1,0:T(8,128)S(1)} %get-tuple-element.35.v1_ref, ...), custom_call_target="tpu_custom_call" | custom-call | tf_op jit(solution)/shard_map/pallas_call | solution.py:643
  32.2 2.4 %collective-permute-done.4.v1_left_ref = f32[2,3,64,256]{3,2,1,0:T(8,128)S(1)} collective-permute-done((f32[2,3,64,256]{3,2,1,0:T(8,128)S(1)}, f32[2,3,64,256]{3,2,1,0:T(8,128)S(1)}, u32[]{:S(2)}, u32[]{:S(2)}) %collective-permute-start.4) | collective-permute-done | bytes 393248 | tf_op jit(solution)/shard_map/ppermute | solution.py:601
  34.7 1.8 %shard_map.72 = (f32[2,3,64,256]{3,2,1,0:T(8,128)S(1)}, f32[16,8,128]{2,1,0:T(8,128)S(1)}) custom-call(f32[2,3,64,256]{3,2,1,0:T(8,128)S(1)} %collective-permute-done.4.v1_left_ref, f32[2,3,64,256]{3,2,1,0:T(8,128)S(1)} %get-tuple-element.35.v1_ref, f32[2,3,64,256]{3,2,1,0:T(8,128)S(1)} %collective-permute-done.2.left_ref.keep_left_ref, ...), custom_call_target="tpu_custom_call" | custom-call | tf_op jit(solution)/shard_map/pallas_call | solution.py:650
  36.4 13.7 %all_to_all.16.mom_ref = f32[16,8,128]{2,1,0:T(8,128)S(1)} all-to-all(f32[16,8,128]{2,1,0:T(8,128)S(1)} %get-tuple-element.49), channel_id=1, replica_groups=mesh['load'=8,'space'=16] {'space'}, dimensions={0} | all-to-all | bytes 131072 | tf_op jit(solution)/shard_map/all_to_all | solution.py:657
  50.1 1.3 %shard_map.73 = (f32[3,2,64,256]{3,2,1,0:T(8,128)}, f32[8,30,256]{2,1,0:T(8,128)S(1)}) custom-call(f32[3,3,64,256]{3,2,1,0:T(8,128)S(1)} %get-tuple-element.34.v0_ref, f32[2,3,64,256]{3,2,1,0:T(8,128)S(1)} %collective-permute-done.4.v1_left_ref, f32[2,3,64,256]{3,2,1,0:T(8,128)S(1)} %get-tuple-element.35.v1_ref, ...), custom_call_target="tpu_custom_call" | custom-call | tf_op jit(solution)/shard_map/pallas_call | solution.py:659
  51.4 12.0 %all_to_all.17 = f32[8,30,256]{2,1,0:T(8,128)S(1)} all-to-all(f32[8,30,256]{2,1,0:T(8,128)S(1)} %get-tuple-element.51), channel_id=1, replica_groups=mesh['load'=8,'space'=16] {'load'}, dimensions={0} | all-to-all | bytes 491520 | tf_op jit(solution)/shard_map/all_to_all | solution.py:666
  63.5 1.7 %collective-permute-start.5 = (f32[20,256]{1,0:T(8,128)S(1)}, f32[20,256]{1,0:T(8,128)S(1)}, u32[]{:S(2)}, u32[]{:S(2)}) collective-permute-start(f32[20,256]{1,0:T(8,128)S(1)} %slice.4), channel_id=1, source_target_pairs={{0,15},{1,0},{2,1},{3,2},{4,3},{5,4},{6,5},{7,6},{8,7},{9,8},{10,9... | collective-permute-start | bytes 61448 | tf_op jit(solution)/shard_map/ppermute | solution.py:601
  65.2 1.7 %collective-permute-done.5.next_ref = f32[20,256]{1,0:T(8,128)S(1)} collective-permute-done((f32[20,256]{1,0:T(8,128)S(1)}, f32[20,256]{1,0:T(8,128)S(1)}, u32[]{:S(2)}, u32[]{:S(2)}) %collective-permute-start.5) | collective-permute-done | bytes 20512 | tf_op jit(solution)/shard_map/ppermute | solution.py:601
  66.9 0.7 %shard_map.74 = f32[2,8,256]{2,1,0:T(8,128)} custom-call(f32[30,256]{1,0:T(8,128)S(1)} %reduce_sum.9.energy_ref, f32[20,256]{1,0:T(8,128)S(1)} %collective-permute-done.5.next_ref, f32[8,6,8,256]{3,2,1,0:T(8,128)S(1)} %all_to_all.15.dens_ref), custom_call_target="tpu_custom_call" | custom-call | tf_op jit(solution)/shard_map/pallas_call | solution.py:668
  (3 shorter events, 0.1 us)
Async XLA Ops:
  0.6 4.0 %collective-permute-start = (f32[2,8,256]{2,1,0:T(8,128)}, f32[2,8,256]{2,1,0:T(8,128)S(1)}, u32[]{:S(2)}, u32[]{:S(2)}) collective-permute-start(f32[2,8,256]{2,1,0:T(8,128)} %own_ref.1), channel_id=1, source_target_pairs={{0,1},{1,2},{2,3},{3,4},{4,5},{5,6},{6,7},{7,8},{8,9},{9,10},{10,1... | collective-permute-start | bytes 49160 | tf_op jit(solution)/shard_map/ppermute | solution.py:601
  3.3 3.7 %collective-permute-start.1 = (f32[2,8,256]{2,1,0:T(8,128)}, f32[2,8,256]{2,1,0:T(8,128)S(1)}, u32[]{:S(2)}, u32[]{:S(2)}) collective-permute-start(f32[2,8,256]{2,1,0:T(8,128)} %own_ref.1), channel_id=1, source_target_pairs={{0,15},{1,0},{2,1},{3,2},{4,3},{5,4},{6,5},{7,6},{8,7},{9,8},{10,9... | collective-permute-start | bytes 49160 | tf_op jit(solution)/shard_map/ppermute | solution.py:601
  3.3 3.7 %copy-start = (f32[2,8,256]{2,1,0:T(8,128)S(1)}, f32[2,8,256]{2,1,0:T(8,128)}, u32[]{:S(2)}) copy-start(f32[2,8,256]{2,1,0:T(8,128)} %own_ref.1) | copy-start | bytes 49156
  7.0 20.9 %collective-permute-start.3 = (f32[3,3,64,256]{3,2,1,0:T(8,128)S(1)}, f32[3,3,64,256]{3,2,1,0:T(8,128)S(1)}, u32[]{:S(2)}, u32[]{:S(2)}) collective-permute-start(f32[3,3,64,256]{3,2,1,0:T(8,128)S(1)} %get-tuple-element.32), channel_id=1, source_target_pairs={{0,15},{1,0},{2,1},{3,2},{4,3},{5,4},{6,5},{7,6},{8,7},{9,8},{10,9... | collective-permute-start | bytes 1769480 | tf_op jit(solution)/shard_map/ppermute | solution.py:601
  7.7 20.2 %collective-permute-start.2 = (f32[2,3,64,256]{3,2,1,0:T(8,128)S(1)}, f32[2,3,64,256]{3,2,1,0:T(8,128)S(1)}, u32[]{:S(2)}, u32[]{:S(2)}) collective-permute-start(f32[2,3,64,256]{3,2,1,0:T(8,128)S(1)} %get-tuple-element.31), channel_id=1, source_target_pairs={{0,1},{1,2},{2,3},{3,4},{4,5},{5,6},{6,7},{7,8},{8,9},{9,10},{10,1... | collective-permute-start | bytes 1179656 | tf_op jit(solution)/shard_map/ppermute | solution.py:601
  29.9 4.8 %collective-permute-start.4 = (f32[2,3,64,256]{3,2,1,0:T(8,128)S(1)}, f32[2,3,64,256]{3,2,1,0:T(8,128)S(1)}, u32[]{:S(2)}, u32[]{:S(2)}) collective-permute-start(f32[2,3,64,256]{3,2,1,0:T(8,128)S(1)} %get-tuple-element.35.v1_ref), channel_id=1, source_target_pairs={{0,1},{1,2},{2,3},{3,4},{4,5},{5,6},{6,7},{7,8},{8,9},{9,10},{10,1... | collective-permute-start | bytes 1179656 | tf_op jit(solution)/shard_map/ppermute | solution.py:601
  63.5 3.4 %collective-permute-start.5 = (f32[20,256]{1,0:T(8,128)S(1)}, f32[20,256]{1,0:T(8,128)S(1)}, u32[]{:S(2)}, u32[]{:S(2)}) collective-permute-start(f32[20,256]{1,0:T(8,128)S(1)} %slice.4), channel_id=1, source_target_pairs={{0,15},{1,0},{2,1},{3,2},{4,3},{5,4},{6,5},{7,6},{8,7},{9,8},{10,9... | collective-permute-start | bytes 61448 | tf_op jit(solution)/shard_map/ppermute | solution.py:601

commit v6 on v5

--- a/solution.py
+++ b/solution.py
@@ -169,7 +169,7 @@
     return low + pltpu.roll(jnp.where(last, prev, high), 1, 0), high
 
 
-def apply_rows(planes, moduli, carry_ref, chunk, first_edge=False, last_edge=False):
+def apply_rows(planes, moduli, carry_ref, chunk, first_edge=False, last_scale=None):
     slot = 0
 
     def finish(acc):
@@ -186,6 +186,8 @@
     partial = None
     for index, modulus in enumerate(moduli):
         high = plane_modes(*planes[index + 1], chunk)
+        if last_scale is not None and index + 1 == len(moduli):
+            high = scaled_modes(high, last_scale)
         to_low, to_high = split_x(element_response(element_modes(low, high), modulus))
         if partial is not None:
             acc = [{p: partial[c][p] + to_low[c][p] for p in PAIRS} for c in range(3)]
@@ -193,12 +195,20 @@
         elif first_edge:
             yield index, finish(to_low)
         partial, low = to_high, high
-    if last_edge:
-        yield len(moduli), finish(partial)
+    if last_scale is not None:
+        yield len(moduli), [force * last_scale for force in finish(partial)]
+
+
+def scaled_modes(modes, scale):
+    return [{pair: field[pair] * scale for pair in PAIRS} for field in modes]
+
+
+def has_left():
+    return jnp.where(lax.axis_index("space") == 0, 0.0, 1.0).astype(F32)
 
 
 def loads_kernel(
-    body_hbm, fixed_hbm, node_hbm, force_hbm, load_ref, keep_ref, right_ref, left_ref,
+    body_hbm, fixed_hbm, node_hbm, force_hbm, load_ref, keep_ref, chip_ref, link_ref,
     body_ref, fixed_ref, node_ref, force_ref, sems,
 ):
     pairs = ((node_hbm, node_ref), (force_hbm, force_ref), (body_hbm, body_ref), (fixed_hbm, fixed_ref))
@@ -226,27 +236,41 @@
     )
     copies[2].wait()
     copies[3].wait()
-    for plane in range(CX):
-        for comp in range(3):
+    on_even = is_even()
+    for comp in range(3):
+        loads, keeps = [], []
+        for plane in range(CX):
             keep = 1.0 - fixed_ref[comp, plane].astype(F32)
             first = (comp * CX + plane) * NY
-            load = keep * (body_ref[0, comp, plane] + added[first : first + NY])
-            load_ref[plane, comp] = load
+            loads.append(keep * (body_ref[0, comp, plane] + added[first : first + NY]))
+            keeps.append(keep)
+            load_ref[plane, comp] = loads[plane]
             keep_ref[plane, comp] = keep
-            left_ref[plane, comp] = load
-            if plane == 0:
-                left_ref[2, comp] = keep
-            else:
-                right_ref[0, comp] = load
-                right_ref[1, comp] = keep
-
-
-def pack_kernel(before_ref, own_ref, after_ref, pack_ref):
-    for block in range(pack_ref.shape[0]):
-        for plane in range(CX):
-            pack_ref[block, plane] = before_ref[plane]
+        to_left, to_right = (loads[1], loads[0], keeps[0]), (loads[1], keeps[1], keeps[1])
+        for part in range(3):
+            chip_ref[part, comp] = jnp.where(on_even, to_right[part], to_left[part])
+            link_ref[part, comp] = jnp.where(on_even, to_left[part], to_right[part])
+
+
+def is_even():
+    return lax.rem(lax.axis_index("space"), 2) == 0
+
+
+def swapped(array, across):
+    size = lax.axis_size("space")
+    partner = lambda i: (i + (1 if (i % 2 == 0) != across else -1)) % size
+    return lax.ppermute(array, "space", [(i, partner(i)) for i in range(size)])
+
+
+def pack_kernel(chip_ref, own_ref, link_ref, pack_ref):
+    on_even = is_even()
+    for plane in range(CX):
+        before = jnp.where(on_even, link_ref[plane], chip_ref[plane])
+        after = jnp.where(on_even, chip_ref[plane], link_ref[plane])
+        for block in range(pack_ref.shape[0]):
+            pack_ref[block, plane] = before
             pack_ref[block, CX + plane] = own_ref[plane]
-            pack_ref[block, 2 * CX + plane] = after_ref[plane]
+            pack_ref[block, 2 * CX + plane] = after
 
 
 def clear_tails(refs):
@@ -276,17 +300,17 @@
     return e_ref[plane, rows_at(chunk + 1)]
 
 
-def inverse_diagonal(e_ref, plane, chunk):
+def inverse_diagonal(e_ref, plane, chunk, scale=1.0):
     last = row_ids((ROWS, NZ)) == ROWS - 1
-    cur = modulus_rows(e_ref, plane, chunk) + modulus_rows(e_ref, plane + 1, chunk)
-    before = modulus_rows(e_ref, plane, chunk - 1) + modulus_rows(e_ref, plane + 1, chunk - 1)
+    cur = scale * modulus_rows(e_ref, plane, chunk) + modulus_rows(e_ref, plane + 1, chunk)
+    before = scale * modulus_rows(e_ref, plane, chunk - 1) + modulus_rows(e_ref, plane + 1, chunk - 1)
     cur = cur + pltpu.roll(jnp.where(last, before, cur), 1, 0)
     diag = KDIAG * (cur + from_below(cur))
     return 1.0 / jnp.where(diag > 0.0, diag, 1.0)
 
 
 def first_kernel(
-    load_ref, keep_ref, left_ref, right_ref, dens_ref,
+    load_ref, keep_ref, chip_ref, link_ref, dens_ref,
     v1_ref, v0_ref, e_ref, inv_ref, zs, zd, mom_ref,
     carry,
 ):
@@ -294,7 +318,7 @@
     limit = lax.axis_size("space") * CX
     for plane in range(6):
         at = first_x - 2 + plane
-        scale = jnp.where((at >= 0) & (at < limit), 1.0, 0.0).astype(F32)
+        scale = jnp.where(at < limit, 1.0, 0.0).astype(F32)
         e_ref[plane, 0:ROWS] = jnp.zeros((ROWS, NZ), F32)
         for block in range(CHUNKS):
             dens = dens_ref[block, plane]
@@ -302,19 +326,22 @@
             e_ref[plane, rows] = scale * (EMIN + (1.0 - EMIN) * (dens * dens * dens))
     clear_tails([zs, zd])
     clear_carry(carry)
-    loads = [left_ref.at[0], load_ref.at[0], load_ref.at[1], right_ref.at[0]]
-    has_right = 1.0 - end_flag()
+    on_even = is_even()
+    has_right, joined = 1.0 - end_flag(), has_left()
     zero = jnp.zeros((ROWS, NZ), F32)
 
     def start(chunk, total):
         here = rows_at(chunk)
         for plane in range(4):
-            inverse = inverse_diagonal(e_ref, plane, chunk)
+            inverse = inverse_diagonal(e_ref, plane, chunk, joined if plane == 1 else 1.0)
             inv_ref[plane, here] = inverse
             for comp in range(3):
-                load = loads[plane][comp, here]
-                if plane == 3:
-                    load = load * has_right
+                if plane == 0:
+                    load = jnp.where(on_even, link_ref[0, comp, here], chip_ref[0, comp, here])
+                elif plane == 3:
+                    load = has_right * jnp.where(on_even, chip_ref[1, comp, here], link_ref[1, comp, here])
+                else:
+                    load = load_ref[plane - 1, comp, here]
                 value = load * inverse
                 if plane < 3:
                     v0_ref[plane, comp, here] = value
@@ -329,6 +356,7 @@
         here = rows_at(chunk)
         odd, even = totals
         moduli = [modulus_rows(e_ref, plane, chunk) for plane in (1, 2, 3)]
+        moduli[0] = moduli[0] * joined
         for plane, forces in apply_rows([(zs, zd, k) for k in range(4)], moduli, carry, chunk):
             inverse = inv_ref[plane, here]
             for comp in range(3):
@@ -340,25 +368,28 @@
                 even = even + value * image
         return odd, even
 
-    mom1, mom2 = lax.fori_loop(0, CHUNKS, apply, (zero, zero), unroll=CHUNKS // 2)
+    mom1, mom2 = lax.fori_loop(0, CHUNKS, apply, (zero, zero), unroll=CHUNKS)
     mom_ref[...] = folded([mom0, mom1, mom2] + [zero] * 5)
 
 
 def middle_kernel(
-    v1_ref, zs0, zd0, e_ref, inv_ref, right_ref, keep_ref, sofar_ref,
+    v1_ref, zs0, zd0, e_ref, inv_ref, chip_ref, link_ref, keep_ref, sofar_ref,
     v2_ref, zs1, zd1, zs2, zd2, force_ref, mom_ref,
     zs, zd, zs_far, zd_far, carry,
 ):
     clear_tails([zs, zd, zs1, zd1, zs2, zd2, zs_far, zd_far])
     clear_carry(carry)
-    has_right = 1.0 - end_flag()
+    has_right, on_even = 1.0 - end_flag(), is_even()
     zero = jnp.zeros((ROWS, NZ), F32)
+
+    def right(part, comp, here):
+        return has_right * jnp.where(on_even, chip_ref[part, comp, here], link_ref[part, comp, here])
 
     def start(chunk, done):
         here = rows_at(chunk)
         inverse = inverse_diagonal(e_ref, 4, chunk)
         for comp in range(3):
-            store_z_modes(zs, zd, 0, comp, here, right_ref[1, comp, here] * has_right * inverse)
+            store_z_modes(zs, zd, 0, comp, here, right(0, comp, here) * inverse)
             store_z_modes(zs1, zd1, 0, comp, here, v1_ref[0, comp, here])
             store_z_modes(zs_far, zd_far, 0, comp, here, v1_ref[1, comp, here])
         return done
@@ -372,8 +403,8 @@
         for _, forces in apply_rows(planes, moduli, carry.at[0:1], chunk):
             inverse = inv_ref[3, here]
             for comp in range(3):
-                kept = right_ref[2, comp, here] * has_right > 0.0
-                before = right_ref[0, comp, here] * has_right * inverse
+                kept = right(2, comp, here) > 0.0
+                before = right(1, comp, here) * inverse
                 _, value = advance(forces[comp], kept, before, inverse)
                 store_z_modes(zs_far, zd_far, 1, comp, here, value)
         return done
@@ -402,23 +433,16 @@
         return odd, even
 
     mom3, mom4 = lax.fori_loop(0, CHUNKS, apply, (zero, zero), unroll=CHUNKS)
-    at_end = end_flag()
-
-    def last(chunk, total):
-        modes = plane_modes(zs2, zd2, 0, chunk)
-        energy = element_energy(element_modes(modes, zero_modes()))
-        return total + modulus_rows(e_ref, 3, chunk) * energy
-
-    mom5 = at_end * lax.fori_loop(0, CHUNKS, last, zero, unroll=CHUNKS)
-    mom_ref[...] = sofar_ref[...] + folded([zero] * 3 + [mom3, mom4, mom5] + [zero] * 2)
+    mom_ref[...] = sofar_ref[...] + folded([zero] * 3 + [mom3, mom4] + [zero] * 3)
 
 
 def second_kernel(
-    v1_left_ref, v1_ref, keep_left_ref, keep_ref, e_ref, inv_ref,
+    v1_left_ref, v1_ref, chip_ref, link_ref, keep_ref, e_ref, inv_ref,
     zs1, zd1, zs2_far, zd2_far, force_ref, sofar_ref,
     v2_ref, mom_ref,
     zs, zd, zs2, zd2, carry,
 ):
+    on_even, joined = is_even(), has_left()
     clear_tails([zs, zd, zs2, zd2])
     clear_carry(carry)
     zero = jnp.zeros((ROWS, NZ), F32)
@@ -437,11 +461,12 @@
         odd, even = totals
         moduli = [modulus_rows(e_ref, plane, chunk) for plane in (0, 1)]
         planes = [(zs, zd, 0), (zs, zd, 1), (zs1, zd1, 0)]
-        for plane, forces in apply_rows(planes, moduli, carry, chunk, last_edge=True):
+        for plane, forces in apply_rows(planes, moduli, carry, chunk, last_scale=joined):
             inverse = inv_ref[plane - 1, here]
             for comp in range(3):
                 if plane == 1:
-                    kept, before = keep_left_ref[1, comp, here] > 0.0, v1_left_ref[1, comp, here]
+                    keep = jnp.where(on_even, link_ref[1, comp, here], chip_ref[1, comp, here])
+                    kept, before = keep > 0.0, v1_left_ref[1, comp, here]
                     force = forces[comp]
                 else:
                     kept, before = keep_ref[0, comp, here] > 0.0, v1_ref[0, comp, here]
@@ -457,12 +482,8 @@
     mom3, mom4 = lax.fori_loop(0, CHUNKS, apply, (zero, zero), unroll=CHUNKS)
 
     def last(chunk, total):
-        low = plane_modes(zs2, zd2, 0, chunk)
-        for plane, where in enumerate(((zs2, zd2, 1), (zs2_far, zd2_far, 0))):
-            high = plane_modes(*where, chunk)
-            energy = element_energy(element_modes(low, high))
+        for plane, energy in enumerate(energies(zs2, zd2, (zs2_far, zd2_far, 0), joined, chunk)):
             total = total + modulus_rows(e_ref, 1 + plane, chunk) * energy
-            low = high
         return total
 
     mom5 = lax.fori_loop(0, CHUNKS, last, zero, unroll=CHUNKS)
@@ -471,20 +492,17 @@
         mom_ref[device] = total
 
 
-def zero_modes():
-    return [{pair: jnp.zeros((ROWS, NZ), F32) for pair in PAIRS}] * 3
-
-
 def end_flag():
     at_end = lax.axis_index("space") == lax.axis_size("space") - 1
     return jnp.where(at_end, 1.0, 0.0).astype(F32)
 
 
-def energies(zs, zd, chunk):
-    planes = [plane_modes(zs, zd, plane, chunk) for plane in range(3)]
-    planes.append(zero_modes())
-    for low, high in zip(planes[:-1], planes[1:]):
-        yield element_energy(element_modes(low, high))
+def energies(zs, zd, last_plane, joined, chunk):
+    low, here, high = [
+        plane_modes(*where, chunk) for where in ((zs, zd, 0), (zs, zd, 1), last_plane)
+    ]
+    yield element_energy(element_modes(low, scaled_modes(here, joined)))
+    yield element_energy(element_modes(here, high))
 
 
 def energy_kernel(v0_ref, v1_left_ref, v1_ref, v2_ref, v2_far_ref, mom_ref, u_ref, out_ref, zs, zd, e_ref):
@@ -510,7 +528,7 @@
     c0, c1, c2 = [jnp.broadcast_to(jnp.concatenate([c, c], axis=1), (ROWS, NZ)) for c in (c0, c1, c2)]
 
     clear_tails([zs, zd])
-    for plane in range(3):
+    for plane in range(2):
         e_ref[plane, 0:ROWS] = jnp.zeros((ROWS, NZ), F32)
         e_ref[plane, NY + ROWS : NY + 2 * ROWS] = jnp.zeros((ROWS, NZ), F32)
     v1_planes = [v1_left_ref.at[1], v1_ref.at[0], v1_ref.at[1]]
@@ -528,17 +546,17 @@
         return done
 
     lax.fori_loop(0, CHUNKS, combine, 0, unroll=CHUNKS)
-    at_end = end_flag()
+    joined = has_left()
 
     def measure(chunk, done):
-        for plane, energy in enumerate(energies(zs, zd, chunk)):
-            e_ref[plane, rows_at(chunk + 1)] = energy * (at_end if plane == 2 else 1.0)
+        for plane, energy in enumerate(energies(zs, zd, (zs, zd, 2), joined, chunk)):
+            e_ref[plane, rows_at(chunk + 1)] = energy
         return done
 
     lax.fori_loop(0, CHUNKS, measure, 0, unroll=CHUNKS)
     span = ROWS + 2
     for block in range(CHUNKS):
-        for plane in range(3):
+        for plane in range(2):
             first = ROWS - 1 + block * ROWS
             out_ref[block, plane * span : (plane + 1) * span] = e_ref[plane, first : first + span]
 
@@ -563,12 +581,7 @@
     n_space, n_load = lax.axis_size("space"), lax.axis_size("load")
     span = ROWS + 2
     part = lambda ref, k: ref[k * span : (k + 1) * span]
-    total = [
-        part(energy_ref, 0),
-        part(energy_ref, 1),
-        part(energy_ref, 2) + (1.0 - end_flag()) * part(next_ref, 0),
-        part(next_ref, 1),
-    ]
+    total = [part(ref, k) for ref in (energy_ref, next_ref) for k in range(2)]
     before = jnp.maximum(load - 1, 0)
     after = jnp.minimum(load + 1, n_load - 1)
     at_y = load * ROWS - 1 + row_ids((span, NZ))
@@ -603,13 +616,13 @@
 
 def body(density, fixed_dofs, body_loads, point_nodes, point_forces):
     n_load, n_space = lax.axis_size("load"), lax.axis_size("space")
-    dens_left = shifted(density, "space", 1)
-    dens_right = shifted(density, "space", -1)
+    dens_chip = swapped(density, False)
+    dens_link = swapped(density, True)
     plane = (3, NY, NZ)
     by_component = jnp.swapaxes(point_forces, 0, 1)
-    load, keep, to_right, to_left = kernel_call(
+    load, keep, to_chip, to_link = kernel_call(
         loads_kernel,
-        [(2,) + plane, (2,) + plane, (2,) + plane, (3,) + plane],
+        [(2,) + plane, (2,) + plane, (3,) + plane, (3,) + plane],
         4,
         0,
         [
@@ -621,11 +634,11 @@
         ],
     )(*[pltpu.with_memory_space_constraint(x, pltpu.HBM) for x in (body_loads, fixed_dofs, point_nodes, by_component)])
     (dens,) = kernel_call(pack_kernel, [(n_load, 3 * CX, ROWS, NZ)], 0, 3)(
-        dens_left, density, dens_right
+        dens_chip, density, dens_link
     )
-    dens, to_right, to_left = lax.optimization_barrier((dens, to_right, to_left))
-    left = shifted(to_right, "space", 1)
-    right = shifted(to_left, "space", -1)
+    dens, to_chip, to_link = lax.optimization_barrier((dens, to_chip, to_link))
+    chip = swapped(to_chip, False)
+    link = swapped(to_link, True)
     dens = lax.all_to_all(dens, "load", 0, 0)
 
     padded = (NY + ROWS, NZ)
@@ -638,33 +651,33 @@
         0,
         5,
         [carried(2)],
-    )(load, keep, left, right, dens)
+    )(load, keep, chip, link, dens)
     v1_left = shifted(v1, "space", 1)
     v2_far, zs1, zd1, zs2, zd2, force, mom = kernel_call(
         middle_kernel,
         [plane, modes(1), modes(1), modes(1), modes(1), plane, (8, 128)],
         0,
-        8,
+        9,
         [zed(1), zed(1), zed(2), zed(2), carried(3)],
-    )(v1, zs0, zd0, modulus, inverse, right, keep, mom)
+    )(v1, zs0, zd0, modulus, inverse, chip, link, keep, mom)
     v2, mom = kernel_call(
         second_kernel,
         [(2,) + plane, (n_space, 8, 128)],
         0,
-        12,
+        13,
         [zed(2), zed(2), zed(2), zed(2), carried(2)],
-    )(v1_left, v1, left, keep, modulus, inverse, zs1, zd1, zs2, zd2, force, mom)
+    )(v1_left, v1, chip, link, keep, modulus, inverse, zs1, zd1, zs2, zd2, force, mom)
     mom = lax.all_to_all(mom, "space", 0, 0)
     span = ROWS + 2
     moved, energy = kernel_call(
         energy_kernel,
-        [(3, CX, NY, NZ), (CHUNKS, 3 * span, NZ)],
+        [(3, CX, NY, NZ), (CHUNKS, 2 * span, NZ)],
         0,
         6,
-        [zed(3), zed(3), pltpu.VMEM((3, NY + 2 * ROWS, NZ), F32)],
+        [zed(3), zed(3), pltpu.VMEM((2, NY + 2 * ROWS, NZ), F32)],
     )(v0, v1_left, v1, v2, v2_far, mom)
     energy = jnp.sum(lax.all_to_all(energy, "load", 0, 0), axis=0)
-    following = shifted(energy[: 2 * span], "space", -1)
+    following = shifted(energy, "space", -1)
     (filtered,) = kernel_call(filter_kernel, [(CX, ROWS, NZ)], 0, 3)(energy, following, dens)
     return (moved[None], filtered)
 

time: 67.8 us -> 65.8 us (0.971)
  blocking collectives: 44.8 us -> 41.4 us
  starting transfers between devices: 6.26 us -> 9.17 us
  waiting for transfers between devices: 6.43 us -> 5.02 us
    ppermute x0 -> x4, starting transfers between devices: none -> 5.44 us  [swapped(): return lax.ppermute(array, 'space', [(i, partner(i)) for i in range(size)])]
    ppermute x6 -> x2, starting transfers between devices: 6.26 us -> 3.73 us  [shifted(): lax.ppermute(array, axis, [(i, (i + distance) % size) for i in range(size)])]
    all_to_all x1, blocking collectives: 19.1 us -> 16.7 us  [body(): dens = lax.all_to_all(dens, 'load', 0, 0)]
    all_to_all x1, blocking collectives: 12 us -> 9.75 us  [body(): energy = jnp.sum(lax.all_to_all(energy, 'load', 0, 0), axis=0)]
    ppermute x6 -> x2, waiting for transfers between devices: 6.43 us -> 4.28 us  [shifted(): lax.ppermute(array, axis, [(i, (i + distance) % size) for i in range(size)])]
    all_to_all x1, blocking collectives: 13.7 us -> 14.9 us  [body(): mom = lax.all_to_all(mom, 'space', 0, 0)]
    ppermute x0 -> x4, waiting for transfers between devices: none -> 0.74 us  [swapped(): return lax.ppermute(array, 'space', [(i, partner(i)) for i in range(size)])]
where the time goes in v6:
time: 65.8 us; the launch traced here: 65.6 us
  blocking collectives  41.4 us (63%)
  Pallas kernels  9.27 us (14%)
  starting transfers between devices  9.17 us (14%)
  waiting for transfers between devices  5.02 us (8%)
  between operations  0.67 us (1%)
    all_to_all x1, blocking collectives, body(): dens = lax.all_to_all(dens, 'load', 0, 0)  16.7 us
    all_to_all x1, blocking collectives, body(): mom = lax.all_to_all(mom, 'space', 0, 0)  14.9 us
    all_to_all x1, blocking collectives, body(): energy = jnp.sum(lax.all_to_all(energy, 'load', 0, 0), axis=0)  9.75 us
    ppermute x4, starting transfers between devices, swapped(): return lax.ppermute(array, 'space', [(i, partner(i)) for i in range(size)])  5.44 us
    ppermute x2, waiting for transfers between devices, shifted(): lax.ppermute(array, axis, [(i, (i + distance) % size) for i in range(size)])  4.28 us
    ppermute x2, starting transfers between devices, shifted(): lax.ppermute(array, axis, [(i, (i + distance) % size) for i in range(size)])  3.73 us
    pallas_call x1, Pallas kernels, body(): kernel_call(middle_kernel, [plane, modes(1), modes(1), modes(1), modes(1)...  2.13 us
    pallas_call x1, Pallas kernels, body(): kernel_call(first_kernel, [(2,) + plane, (3,) + plane, (6,) + padded, (4,...  1.91 us
  transfers between devices with their start and end apart: 6, of which 3 were waited for; matrix products, arithmetic and copies ran while one was open for 0% of the time, Pallas kernels for 5%

profile of v6, /device:TPU:1, one launch (start us, length us, event | category | flops | bytes accessed | tf_op | source)
XLA Modules:
  0.0 65.6 jit_solution(1369512382802923350)
XLA Ops:
  0.6 1.5 %collective-permute-start = (f32[2,8,256]{2,1,0:T(8,128)}, f32[2,8,256]{2,1,0:T(8,128)S(1)}, u32[]{:S(2)}, u32[]{:S(2)}) collective-permute-start(f32[2,8,256]{2,1,0:T(8,128)} %own_ref.1), channel_id=1, source_target_pairs={{0,1},{1,0},{2,3},{3,2},{4,5},{5,4},{6,7},{7,6},{8,9},{9,8},{10,11... | collective-permute-start | bytes 49160 | tf_op jit(solution)/shard_map/ppermute | solution.py:262
  2.1 1.3 %collective-permute-start.1 = (f32[2,8,256]{2,1,0:T(8,128)}, f32[2,8,256]{2,1,0:T(8,128)S(1)}, u32[]{:S(2)}, u32[]{:S(2)}) collective-permute-start(f32[2,8,256]{2,1,0:T(8,128)} %own_ref.1), channel_id=1, source_target_pairs={{0,15},{1,2},{2,1},{3,4},{4,3},{5,6},{6,5},{7,8},{8,7},{9,10},{10,... | collective-permute-start | bytes 49160 | tf_op jit(solution)/shard_map/ppermute | solution.py:262
  3.4 0.0 copy-start
  3.4 1.4 %shard_map.68 = (f32[2,3,64,256]{3,2,1,0:T(8,128)S(1)}, f32[2,3,64,256]{3,2,1,0:T(8,128)S(1)}, f32[3,3,64,256]{3,2,1,0:T(8,128)S(1)}, f32[3,3,64,256]{3,2,1,0:T(8,128)S(1)}) custom-call(f32[1,3,2,64,256]{4,3,2,1,0:T(8,128)} %body_hbm.1, s32[3,2,64,256]{3,2,1,0:T(8,128)} %fixed_hbm.1, s32[1,128]{1,0:T(1,128)} %node_hbm.1, f32[3,1,128]{2,1,0:T(1,128)} %bitcast.2), custom_call_target="tpu_custom_call" | custom-call | tf_op jit(solution)/shard_map/pallas_call | solution.py:623
  4.8 0.0 collective-permute-done.chip_ref
  4.8 0.7 %collective-permute-done.1.link_ref = f32[2,8,256]{2,1,0:T(8,128)S(1)} collective-permute-done((f32[2,8,256]{2,1,0:T(8,128)}, f32[2,8,256]{2,1,0:T(8,128)S(1)}, u32[]{:S(2)}, u32[]{:S(2)}) %collective-permute-start.1) | collective-permute-done | bytes 16416 | tf_op jit(solution)/shard_map/ppermute | solution.py:262
  5.5 0.0 copy-done
  5.5 2.7 %collective-permute-start.2 = (f32[3,3,64,256]{3,2,1,0:T(8,128)S(1)}, f32[3,3,64,256]{3,2,1,0:T(8,128)S(1)}, u32[]{:S(2)}, u32[]{:S(2)}) collective-permute-start(f32[3,3,64,256]{3,2,1,0:T(8,128)S(1)} %get-tuple-element.31), channel_id=1, source_target_pairs={{0,1},{1,0},{2,3},{3,2},{4,5},{5,4},{6,7},{7,6},{8,9},{9,8},{10,11... | collective-permute-start | bytes 1769480 | tf_op jit(solution)/shard_map/ppermute | solution.py:262
  8.2 0.0 collective-permute-start.3
  8.2 16.7 %all_to_all.15.dens_ref = f32[8,6,8,256]{3,2,1,0:T(8,128)S(1)} all-to-all(f32[8,6,8,256]{3,2,1,0:T(8,128)S(1)} %shard_map.69), channel_id=1, replica_groups=mesh['load'=8,'space'=16] {'load'}, dimensions={0} | all-to-all | bytes 786432 | tf_op jit(solution)/shard_map/all_to_all | solution.py:642
  24.9 0.0 collective-permute-done.2.chip_ref
  24.9 0.0 collective-permute-done.3.link_ref
  24.9 1.9 %shard_map.70 = (f32[2,3,64,256]{3,2,1,0:T(8,128)S(1)}, f32[3,3,64,256]{3,2,1,0:T(8,128)S(1)}, f32[6,72,256]{2,1,0:T(8,128)S(1)}, f32[4,64,256]{2,1,0:T(8,128)S(...) custom-call(f32[2,3,64,256]{3,2,1,0:T(8,128)S(1)} %get-tuple-element.27.load_ref, ...), custom_call_target="tpu_custom_call" | custom-call | tf_op jit(solution)/shard_map/pallas_call | solution.py:648
  26.8 2.0 %collective-permute-start.4 = (f32[2,3,64,256]{3,2,1,0:T(8,128)S(1)}, f32[2,3,64,256]{3,2,1,0:T(8,128)S(1)}, u32[]{:S(2)}, u32[]{:S(2)}) collective-permute-start(f32[2,3,64,256]{3,2,1,0:T(8,128)S(1)} %get-tuple-element.35.v1_ref), channel_id=1, source_target_pairs={{0,1},{1,2},{2,3},{3,4},{4,5},{5,6},{6,7},{7,8},{8,9},{9,10},{10,1... | collective-permute-start | bytes 1179656 | tf_op jit(solution)/shard_map/ppermute | solution.py:614
  28.8 2.1 %shard_map.71 = (f32[3,64,256]{2,1,0:T(8,128)S(1)}, f32[1,3,72,256]{3,2,1,0:T(8,128)S(1)}, f32[1,3,72,256]{3,2,1,0:T(8,128)S(1)}, f32[1,3,72,256]{3,2,1,0:T(8,12...) custom-call(f32[2,3,64,256]{3,2,1,0:T(8,128)S(1)} %get-tuple-element.35.v1_ref, ...), custom_call_target="tpu_custom_call" | custom-call | tf_op jit(solution)/shard_map/pallas_call | solution.py:656
  31.0 2.6 %collective-permute-done.4.v1_left_ref = f32[2,3,64,256]{3,2,1,0:T(8,128)S(1)} collective-permute-done((f32[2,3,64,256]{3,2,1,0:T(8,128)S(1)}, f32[2,3,64,256]{3,2,1,0:T(8,128)S(1)}, u32[]{:S(2)}, u32[]{:S(2)}) %collective-permute-start.4) | collective-permute-done | bytes 393248 | tf_op jit(solution)/shard_map/ppermute | solution.py:614
  33.6 1.8 %shard_map.72 = (f32[2,3,64,256]{3,2,1,0:T(8,128)S(1)}, f32[16,8,128]{2,1,0:T(8,128)S(1)}) custom-call(f32[2,3,64,256]{3,2,1,0:T(8,128)S(1)} %collective-permute-done.4.v1_left_ref, f32[2,3,64,256]{3,2,1,0:T(8,128)S(1)} %get-tuple-element.35.v1_ref, f32[3,3,64,256]{3,2,1,0:T(8,128)S(1)} %collective-permute-done.2.chip_ref, ...), custom_call_target="tpu_custom_call" | custom-call | tf_op jit(solution)/shard_map/pallas_call | solution.py:663
  35.4 14.9 %all_to_all.16.mom_ref = f32[16,8,128]{2,1,0:T(8,128)S(1)} all-to-all(f32[16,8,128]{2,1,0:T(8,128)S(1)} %get-tuple-element.49), channel_id=1, replica_groups=mesh['load'=8,'space'=16] {'space'}, dimensions={0} | all-to-all | bytes 131072 | tf_op jit(solution)/shard_map/all_to_all | solution.py:670
  50.3 1.3 %shard_map.73 = (f32[3,2,64,256]{3,2,1,0:T(8,128)}, f32[8,20,256]{2,1,0:T(8,128)S(1)}) custom-call(f32[3,3,64,256]{3,2,1,0:T(8,128)S(1)} %get-tuple-element.34.v0_ref, f32[2,3,64,256]{3,2,1,0:T(8,128)S(1)} %collective-permute-done.4.v1_left_ref, f32[2,3,64,256]{3,2,1,0:T(8,128)S(1)} %get-tuple-element.35.v1_ref, ...), custom_call_target="tpu_custom_call" | custom-call | tf_op jit(solution)/shard_map/pallas_call | solution.py:672
  51.6 9.8 %all_to_all.17 = f32[8,20,256]{2,1,0:T(8,128)S(1)} all-to-all(f32[8,20,256]{2,1,0:T(8,128)S(1)} %get-tuple-element.51), channel_id=1, replica_groups=mesh['load'=8,'space'=16] {'load'}, dimensions={0} | all-to-all | bytes 327680 | tf_op jit(solution)/shard_map/all_to_all | solution.py:679
  61.4 1.7 %collective-permute-start.5 = (f32[20,256]{1,0:T(8,128)S(1)}, f32[20,256]{1,0:T(8,128)S(1)}, u32[]{:S(2)}, u32[]{:S(2)}) collective-permute-start(f32[20,256]{1,0:T(8,128)S(1)} %reduce_sum.9.energy_ref), channel_id=1, source_target_pairs={{0,15},{1,0},{2,1},{3,2},{4,3},{5,4},{6,5},{7,6},{8,7},{9,8},{10,9... | collective-permute-start | bytes 61448 | tf_op jit(solution)/shard_map/ppermute | solution.py:614
  63.1 1.7 %collective-permute-done.5.next_ref = f32[20,256]{1,0:T(8,128)S(1)} collective-permute-done((f32[20,256]{1,0:T(8,128)S(1)}, f32[20,256]{1,0:T(8,128)S(1)}, u32[]{:S(2)}, u32[]{:S(2)}) %collective-permute-start.5) | collective-permute-done | bytes 20512 | tf_op jit(solution)/shard_map/ppermute | solution.py:614
  64.8 0.7 %shard_map.74 = f32[2,8,256]{2,1,0:T(8,128)} custom-call(f32[20,256]{1,0:T(8,128)S(1)} %reduce_sum.9.energy_ref, f32[20,256]{1,0:T(8,128)S(1)} %collective-permute-done.5.next_ref, f32[8,6,8,256]{3,2,1,0:T(8,128)S(1)} %all_to_all.15.dens_ref), custom_call_target="tpu_custom_call" | custom-call | tf_op jit(solution)/shard_map/pallas_call | solution.py:681
  (2 shorter events, 0.0 us)
Async XLA Ops:
  0.6 4.1 %collective-permute-start = (f32[2,8,256]{2,1,0:T(8,128)}, f32[2,8,256]{2,1,0:T(8,128)S(1)}, u32[]{:S(2)}, u32[]{:S(2)}) collective-permute-start(f32[2,8,256]{2,1,0:T(8,128)} %own_ref.1), channel_id=1, source_target_pairs={{0,1},{1,0},{2,3},{3,2},{4,5},{5,4},{6,7},{7,6},{8,9},{9,8},{10,11... | collective-permute-start | bytes 49160 | tf_op jit(solution)/shard_map/ppermute | solution.py:262
  2.1 3.4 %collective-permute-start.1 = (f32[2,8,256]{2,1,0:T(8,128)}, f32[2,8,256]{2,1,0:T(8,128)S(1)}, u32[]{:S(2)}, u32[]{:S(2)}) collective-permute-start(f32[2,8,256]{2,1,0:T(8,128)} %own_ref.1), channel_id=1, source_target_pairs={{0,15},{1,2},{2,1},{3,4},{4,3},{5,6},{6,5},{7,8},{8,7},{9,10},{10,... | collective-permute-start | bytes 49160 | tf_op jit(solution)/shard_map/ppermute | solution.py:262
  3.4 2.1 %copy-start = (f32[2,8,256]{2,1,0:T(8,128)S(1)}, f32[2,8,256]{2,1,0:T(8,128)}, u32[]{:S(2)}) copy-start(f32[2,8,256]{2,1,0:T(8,128)} %own_ref.1) | copy-start | bytes 49156
  5.5 19.4 %collective-permute-start.2 = (f32[3,3,64,256]{3,2,1,0:T(8,128)S(1)}, f32[3,3,64,256]{3,2,1,0:T(8,128)S(1)}, u32[]{:S(2)}, u32[]{:S(2)}) collective-permute-start(f32[3,3,64,256]{3,2,1,0:T(8,128)S(1)} %get-tuple-element.31), channel_id=1, source_target_pairs={{0,1},{1,0},{2,3},{3,2},{4,5},{5,4},{6,7},{7,6},{8,9},{9,8},{10,11... | collective-permute-start | bytes 1769480 | tf_op jit(solution)/shard_map/ppermute | solution.py:262
  8.2 16.7 %collective-permute-start.3 = (f32[3,3,64,256]{3,2,1,0:T(8,128)S(1)}, f32[3,3,64,256]{3,2,1,0:T(8,128)S(1)}, u32[]{:S(2)}, u32[]{:S(2)}) collective-permute-start(f32[3,3,64,256]{3,2,1,0:T(8,128)S(1)} %get-tuple-element.32), channel_id=1, source_target_pairs={{0,15},{1,2},{2,1},{3,4},{4,3},{5,6},{6,5},{7,8},{8,7},{9,10},{10,... | collective-permute-start | bytes 1769480 | tf_op jit(solution)/shard_map/ppermute | solution.py:262
  26.8 6.7 %collective-permute-start.4 = (f32[2,3,64,256]{3,2,1,0:T(8,128)S(1)}, f32[2,3,64,256]{3,2,1,0:T(8,128)S(1)}, u32[]{:S(2)}, u32[]{:S(2)}) collective-permute-start(f32[2,3,64,256]{3,2,1,0:T(8,128)S(1)} %get-tuple-element.35.v1_ref), channel_id=1, source_target_pairs={{0,1},{1,2},{2,3},{3,4},{4,5},{5,6},{6,7},{7,8},{8,9},{9,10},{10,1... | collective-permute-start | bytes 1179656 | tf_op jit(solution)/shard_map/ppermute | solution.py:614
  61.4 3.4 %collective-permute-start.5 = (f32[20,256]{1,0:T(8,128)S(1)}, f32[20,256]{1,0:T(8,128)S(1)}, u32[]{:S(2)}, u32[]{:S(2)}) collective-permute-start(f32[20,256]{1,0:T(8,128)S(1)} %reduce_sum.9.energy_ref), channel_id=1, source_target_pairs={{0,15},{1,0},{2,1},{3,2},{4,3},{5,4},{6,5},{7,6},{8,7},{9,8},{10,9... | collective-permute-start | bytes 61448 | tf_op jit(solution)/shard_map/ppermute | solution.py:614

commit v7 on v6

--- a/solution.py
+++ b/solution.py
@@ -636,7 +636,7 @@
     (dens,) = kernel_call(pack_kernel, [(n_load, 3 * CX, ROWS, NZ)], 0, 3)(
         dens_chip, density, dens_link
     )
-    dens, to_chip, to_link = lax.optimization_barrier((dens, to_chip, to_link))
+    dens, to_chip = lax.optimization_barrier((dens, to_chip))
     chip = swapped(to_chip, False)
     link = swapped(to_link, True)
     dens = lax.all_to_all(dens, "load", 0, 0)

time: 65.8 us -> 64.3 us (0.977)
  starting transfers between devices: 9.17 us -> 8.05 us
    ppermute x2, starting transfers between devices: 3.73 us -> 2.05 us  [shifted(): lax.ppermute(array, axis, [(i, (i + distance) % size) for i in range(size)])]
    all_to_all x1, blocking collectives: 14.9 us -> 13.9 us  [body(): mom = lax.all_to_all(mom, 'space', 0, 0)]
    all_to_all x1, blocking collectives: 9.75 us -> 10.6 us  [body(): energy = jnp.sum(lax.all_to_all(energy, 'load', 0, 0), axis=0)]
where the time goes in v7:
time: 64.3 us; the launch traced here: 64 us
  blocking collectives  41.6 us (65%)
  Pallas kernels  9.27 us (14%)
  starting transfers between devices  8.05 us (13%)
  waiting for transfers between devices  4.45 us (7%)
  between operations  0.67 us (1%)
    all_to_all x1, blocking collectives, body(): dens = lax.all_to_all(dens, 'load', 0, 0)  17 us
    all_to_all x1, blocking collectives, body(): mom = lax.all_to_all(mom, 'space', 0, 0)  13.9 us
    all_to_all x1, blocking collectives, body(): energy = jnp.sum(lax.all_to_all(energy, 'load', 0, 0), axis=0)  10.6 us
    ppermute x4, starting transfers between devices, swapped(): return lax.ppermute(array, 'space', [(i, partner(i)) for i in range(size)])  6 us
    ppermute x2, waiting for transfers between devices, shifted(): lax.ppermute(array, axis, [(i, (i + distance) % size) for i in range(size)])  4.27 us
    pallas_call x1, Pallas kernels, body(): kernel_call(middle_kernel, [plane, modes(1), modes(1), modes(1), modes(1)...  2.13 us
    ppermute x2, starting transfers between devices, shifted(): lax.ppermute(array, axis, [(i, (i + distance) % size) for i in range(size)])  2.05 us
    pallas_call x1, Pallas kernels, body(): kernel_call(first_kernel, [(2,) + plane, (3,) + plane, (6,) + padded, (4,...  1.91 us
  transfers between devices with their start and end apart: 6, of which 3 were waited for; matrix products, arithmetic and copies ran while one was open for 0% of the time, Pallas kernels for 5%

profile of v7, /device:TPU:1, one launch (start us, length us, event | category | flops | bytes accessed | tf_op | source)
XLA Modules:
  0.0 64.0 jit_solution(6326494314398834162)
XLA Ops:
  0.6 1.5 %collective-permute-start = (f32[2,8,256]{2,1,0:T(8,128)}, f32[2,8,256]{2,1,0:T(8,128)S(1)}, u32[]{:S(2)}, u32[]{:S(2)}) collective-permute-start(f32[2,8,256]{2,1,0:T(8,128)} %own_ref.1), channel_id=1, source_target_pairs={{0,1},{1,0},{2,3},{3,2},{4,5},{5,4},{6,7},{7,6},{8,9},{9,8},{10,11... | collective-permute-start | bytes 49160 | tf_op jit(solution)/shard_map/ppermute | solution.py:262
  2.1 1.3 %collective-permute-start.1 = (f32[2,8,256]{2,1,0:T(8,128)}, f32[2,8,256]{2,1,0:T(8,128)S(1)}, u32[]{:S(2)}, u32[]{:S(2)}) collective-permute-start(f32[2,8,256]{2,1,0:T(8,128)} %own_ref.1), channel_id=1, source_target_pairs={{0,15},{1,2},{2,1},{3,4},{4,3},{5,6},{6,5},{7,8},{8,7},{9,10},{10,... | collective-permute-start | bytes 49160 | tf_op jit(solution)/shard_map/ppermute | solution.py:262
  3.4 0.0 copy-start
  3.4 1.4 %shard_map.68 = (f32[2,3,64,256]{3,2,1,0:T(8,128)S(1)}, f32[2,3,64,256]{3,2,1,0:T(8,128)S(1)}, f32[3,3,64,256]{3,2,1,0:T(8,128)S(1)}, f32[3,3,64,256]{3,2,1,0:T(8,128)S(1)}) custom-call(f32[1,3,2,64,256]{4,3,2,1,0:T(8,128)} %body_hbm.1, s32[3,2,64,256]{3,2,1,0:T(8,128)} %fixed_hbm.1, s32[1,128]{1,0:T(1,128)} %node_hbm.1, f32[3,1,128]{2,1,0:T(1,128)} %bitcast.2), custom_call_target="tpu_custom_call" | custom-call | tf_op jit(solution)/shard_map/pallas_call | solution.py:623
  4.8 0.6 collective-permute-start.3
  5.3 0.0 collective-permute-done.chip_ref
  5.3 0.2 collective-permute-done.1.link_ref
  5.5 0.0 copy-done
  5.5 2.7 %collective-permute-start.2 = (f32[3,3,64,256]{3,2,1,0:T(8,128)S(1)}, f32[3,3,64,256]{3,2,1,0:T(8,128)S(1)}, u32[]{:S(2)}, u32[]{:S(2)}) collective-permute-start(f32[3,3,64,256]{3,2,1,0:T(8,128)S(1)} %get-tuple-element.29), channel_id=1, source_target_pairs={{0,1},{1,0},{2,3},{3,2},{4,5},{5,4},{6,7},{7,6},{8,9},{9,8},{10,11... | collective-permute-start | bytes 1769480 | tf_op jit(solution)/shard_map/ppermute | solution.py:262
  8.2 17.0 %all_to_all.15.dens_ref = f32[8,6,8,256]{3,2,1,0:T(8,128)S(1)} all-to-all(f32[8,6,8,256]{3,2,1,0:T(8,128)S(1)} %shard_map.69), channel_id=1, replica_groups=mesh['load'=8,'space'=16] {'load'}, dimensions={0} | all-to-all | bytes 786432 | tf_op jit(solution)/shard_map/all_to_all | solution.py:642
  25.2 0.0 collective-permute-done.3.link_ref
  25.2 0.0 collective-permute-done.2.chip_ref
  25.2 1.9 %shard_map.70 = (f32[2,3,64,256]{3,2,1,0:T(8,128)S(1)}, f32[3,3,64,256]{3,2,1,0:T(8,128)S(1)}, f32[6,72,256]{2,1,0:T(8,128)S(1)}, f32[4,64,256]{2,1,0:T(8,128)S(...) custom-call(f32[2,3,64,256]{3,2,1,0:T(8,128)S(1)} %get-tuple-element.26.load_ref, ...), custom_call_target="tpu_custom_call" | custom-call | tf_op jit(solution)/shard_map/pallas_call | solution.py:648
  27.2 0.2 collective-permute-start.4
  27.3 2.1 %shard_map.71 = (f32[3,64,256]{2,1,0:T(8,128)S(1)}, f32[1,3,72,256]{3,2,1,0:T(8,128)S(1)}, f32[1,3,72,256]{3,2,1,0:T(8,128)S(1)}, f32[1,3,72,256]{3,2,1,0:T(8,12...) custom-call(f32[2,3,64,256]{3,2,1,0:T(8,128)S(1)} %get-tuple-element.33.v1_ref, ...), custom_call_target="tpu_custom_call" | custom-call | tf_op jit(solution)/shard_map/pallas_call | solution.py:656
  29.5 2.6 %collective-permute-done.4.v1_left_ref = f32[2,3,64,256]{3,2,1,0:T(8,128)S(1)} collective-permute-done((f32[2,3,64,256]{3,2,1,0:T(8,128)S(1)}, f32[2,3,64,256]{3,2,1,0:T(8,128)S(1)}, u32[]{:S(2)}, u32[]{:S(2)}) %collective-permute-start.4) | collective-permute-done | bytes 393248 | tf_op jit(solution)/shard_map/ppermute | solution.py:614
  32.0 1.8 %shard_map.72 = (f32[2,3,64,256]{3,2,1,0:T(8,128)S(1)}, f32[16,8,128]{2,1,0:T(8,128)S(1)}) custom-call(f32[2,3,64,256]{3,2,1,0:T(8,128)S(1)} %collective-permute-done.4.v1_left_ref, f32[2,3,64,256]{3,2,1,0:T(8,128)S(1)} %get-tuple-element.33.v1_ref, f32[3,3,64,256]{3,2,1,0:T(8,128)S(1)} %collective-permute-done.2.chip_ref, ...), custom_call_target="tpu_custom_call" | custom-call | tf_op jit(solution)/shard_map/pallas_call | solution.py:663
  33.9 13.9 %all_to_all.16.mom_ref = f32[16,8,128]{2,1,0:T(8,128)S(1)} all-to-all(f32[16,8,128]{2,1,0:T(8,128)S(1)} %get-tuple-element.47), channel_id=1, replica_groups=mesh['load'=8,'space'=16] {'space'}, dimensions={0} | all-to-all | bytes 131072 | tf_op jit(solution)/shard_map/all_to_all | solution.py:670
  47.8 1.3 %shard_map.73 = (f32[3,2,64,256]{3,2,1,0:T(8,128)}, f32[8,20,256]{2,1,0:T(8,128)S(1)}) custom-call(f32[3,3,64,256]{3,2,1,0:T(8,128)S(1)} %get-tuple-element.32.v0_ref, f32[2,3,64,256]{3,2,1,0:T(8,128)S(1)} %collective-permute-done.4.v1_left_ref, f32[2,3,64,256]{3,2,1,0:T(8,128)S(1)} %get-tuple-element.33.v1_ref, ...), custom_call_target="tpu_custom_call" | custom-call | tf_op jit(solution)/shard_map/pallas_call | solution.py:672
  49.1 10.6 %all_to_all.17 = f32[8,20,256]{2,1,0:T(8,128)S(1)} all-to-all(f32[8,20,256]{2,1,0:T(8,128)S(1)} %get-tuple-element.49), channel_id=1, replica_groups=mesh['load'=8,'space'=16] {'load'}, dimensions={0} | all-to-all | bytes 327680 | tf_op jit(solution)/shard_map/all_to_all | solution.py:679
  59.7 1.9 %collective-permute-start.5 = (f32[20,256]{1,0:T(8,128)S(1)}, f32[20,256]{1,0:T(8,128)S(1)}, u32[]{:S(2)}, u32[]{:S(2)}) collective-permute-start(f32[20,256]{1,0:T(8,128)S(1)} %reduce_sum.9.energy_ref), channel_id=1, source_target_pairs={{0,15},{1,0},{2,1},{3,2},{4,3},{5,4},{6,5},{7,6},{8,7},{9,8},{10,9... | collective-permute-start | bytes 61448 | tf_op jit(solution)/shard_map/ppermute | solution.py:614
  61.6 1.7 %collective-permute-done.5.next_ref = f32[20,256]{1,0:T(8,128)S(1)} collective-permute-done((f32[20,256]{1,0:T(8,128)S(1)}, f32[20,256]{1,0:T(8,128)S(1)}, u32[]{:S(2)}, u32[]{:S(2)}) %collective-permute-start.5) | collective-permute-done | bytes 20512 | tf_op jit(solution)/shard_map/ppermute | solution.py:614
  63.3 0.7 %shard_map.74 = f32[2,8,256]{2,1,0:T(8,128)} custom-call(f32[20,256]{1,0:T(8,128)S(1)} %reduce_sum.9.energy_ref, f32[20,256]{1,0:T(8,128)S(1)} %collective-permute-done.5.next_ref, f32[8,6,8,256]{3,2,1,0:T(8,128)S(1)} %all_to_all.15.dens_ref), custom_call_target="tpu_custom_call" | custom-call | tf_op jit(solution)/shard_map/pallas_call | solution.py:681
  (2 shorter events, 0.0 us)
Async XLA Ops:
  0.6 4.7 %collective-permute-start = (f32[2,8,256]{2,1,0:T(8,128)}, f32[2,8,256]{2,1,0:T(8,128)S(1)}, u32[]{:S(2)}, u32[]{:S(2)}) collective-permute-start(f32[2,8,256]{2,1,0:T(8,128)} %own_ref.1), channel_id=1, source_target_pairs={{0,1},{1,0},{2,3},{3,2},{4,5},{5,4},{6,7},{7,6},{8,9},{9,8},{10,11... | collective-permute-start | bytes 49160 | tf_op jit(solution)/shard_map/ppermute | solution.py:262
  2.1 3.4 %collective-permute-start.1 = (f32[2,8,256]{2,1,0:T(8,128)}, f32[2,8,256]{2,1,0:T(8,128)S(1)}, u32[]{:S(2)}, u32[]{:S(2)}) collective-permute-start(f32[2,8,256]{2,1,0:T(8,128)} %own_ref.1), channel_id=1, source_target_pairs={{0,15},{1,2},{2,1},{3,4},{4,3},{5,6},{6,5},{7,8},{8,7},{9,10},{10,... | collective-permute-start | bytes 49160 | tf_op jit(solution)/shard_map/ppermute | solution.py:262
  3.4 2.1 %copy-start = (f32[2,8,256]{2,1,0:T(8,128)S(1)}, f32[2,8,256]{2,1,0:T(8,128)}, u32[]{:S(2)}) copy-start(f32[2,8,256]{2,1,0:T(8,128)} %own_ref.1) | copy-start | bytes 49156
  4.8 20.5 %collective-permute-start.3 = (f32[3,3,64,256]{3,2,1,0:T(8,128)S(1)}, f32[3,3,64,256]{3,2,1,0:T(8,128)S(1)}, u32[]{:S(2)}, u32[]{:S(2)}) collective-permute-start(f32[3,3,64,256]{3,2,1,0:T(8,128)S(1)} %get-tuple-element.30), channel_id=1, source_target_pairs={{0,15},{1,2},{2,1},{3,4},{4,3},{5,6},{6,5},{7,8},{8,7},{9,10},{10,... | collective-permute-start | bytes 1769480 | tf_op jit(solution)/shard_map/ppermute | solution.py:262
  5.5 19.7 %collective-permute-start.2 = (f32[3,3,64,256]{3,2,1,0:T(8,128)S(1)}, f32[3,3,64,256]{3,2,1,0:T(8,128)S(1)}, u32[]{:S(2)}, u32[]{:S(2)}) collective-permute-start(f32[3,3,64,256]{3,2,1,0:T(8,128)S(1)} %get-tuple-element.29), channel_id=1, source_target_pairs={{0,1},{1,0},{2,3},{3,2},{4,5},{5,4},{6,7},{7,6},{8,9},{9,8},{10,11... | collective-permute-start | bytes 1769480 | tf_op jit(solution)/shard_map/ppermute | solution.py:262
  27.2 4.9 %collective-permute-start.4 = (f32[2,3,64,256]{3,2,1,0:T(8,128)S(1)}, f32[2,3,64,256]{3,2,1,0:T(8,128)S(1)}, u32[]{:S(2)}, u32[]{:S(2)}) collective-permute-start(f32[2,3,64,256]{3,2,1,0:T(8,128)S(1)} %get-tuple-element.33.v1_ref), channel_id=1, source_target_pairs={{0,1},{1,2},{2,3},{3,4},{4,5},{5,6},{6,7},{7,8},{8,9},{9,10},{10,1... | collective-permute-start | bytes 1179656 | tf_op jit(solution)/shard_map/ppermute | solution.py:614
  59.7 3.6 %collective-permute-start.5 = (f32[20,256]{1,0:T(8,128)S(1)}, f32[20,256]{1,0:T(8,128)S(1)}, u32[]{:S(2)}, u32[]{:S(2)}) collective-permute-start(f32[20,256]{1,0:T(8,128)S(1)} %reduce_sum.9.energy_ref), channel_id=1, source_target_pairs={{0,15},{1,0},{2,1},{3,2},{4,3},{5,4},{6,5},{7,6},{8,7},{9,8},{10,9... | collective-permute-start | bytes 61448 | tf_op jit(solution)/shard_map/ppermute | solution.py:614

commit v8 on v7

--- a/solution.py
+++ b/solution.py
@@ -330,11 +330,18 @@
     has_right, joined = 1.0 - end_flag(), has_left()
     zero = jnp.zeros((ROWS, NZ), F32)
 
+    def invert(chunk, done):
+        for plane in range(4):
+            inverse = inverse_diagonal(e_ref, plane, chunk, joined if plane == 1 else 1.0)
+            inv_ref[plane, rows_at(chunk)] = inverse
+        return done
+
+    lax.fori_loop(0, CHUNKS, invert, 0, unroll=8)
+
     def start(chunk, total):
         here = rows_at(chunk)
         for plane in range(4):
-            inverse = inverse_diagonal(e_ref, plane, chunk, joined if plane == 1 else 1.0)
-            inv_ref[plane, here] = inverse
+            inverse = inv_ref[plane, here]
             for comp in range(3):
                 if plane == 0:
                     load = jnp.where(on_even, link_ref[0, comp, here], chip_ref[0, comp, here])
@@ -350,7 +357,7 @@
                 store_z_modes(zs, zd, plane, comp, here, value)
         return total
 
-    mom0 = lax.fori_loop(0, CHUNKS, start, zero, unroll=CHUNKS // 2)
+    mom0 = lax.fori_loop(0, CHUNKS, start, zero, unroll=8)
 
     def apply(chunk, totals):
         here = rows_at(chunk)

time: 64.3 us -> 64 us (level)
  transfers between devices with their start and end apart: 6 -> 6, of which waited for: 3 -> 3; matrix products, arithmetic and copies ran while one was open for 0% -> 0% of each run, Pallas kernels for 5% -> 6%
where the time goes in v8:
time: 64 us; the launch traced here: 63.8 us
  blocking collectives  41.6 us (65%)
  Pallas kernels  9.01 us (14%)
  starting transfers between devices  8.05 us (13%)
  waiting for transfers between devices  4.45 us (7%)
  between operations  0.67 us (1%)
    all_to_all x1, blocking collectives, body(): dens = lax.all_to_all(dens, 'load', 0, 0)  17 us
    all_to_all x1, blocking collectives, body(): mom = lax.all_to_all(mom, 'space', 0, 0)  13.9 us
    all_to_all x1, blocking collectives, body(): energy = jnp.sum(lax.all_to_all(energy, 'load', 0, 0), axis=0)  10.6 us
    ppermute x4, starting transfers between devices, swapped(): return lax.ppermute(array, 'space', [(i, partner(i)) for i in range(size)])  6 us
    ppermute x2, waiting for transfers between devices, shifted(): lax.ppermute(array, axis, [(i, (i + distance) % size) for i in range(size)])  4.27 us
    pallas_call x1, Pallas kernels, body(): kernel_call(middle_kernel, [plane, modes(1), modes(1), modes(1), modes(1)...  2.13 us
    ppermute x2, starting transfers between devices, shifted(): lax.ppermute(array, axis, [(i, (i + distance) % size) for i in range(size)])  2.05 us
    pallas_call x1, Pallas kernels, body(): kernel_call(second_kernel, [(2,) + plane, (n_space, 8, 128)], 0, 13, [zed...  1.82 us
  transfers between devices with their start and end apart: 6, of which 3 were waited for; matrix products, arithmetic and copies ran while one was open for 0% of the time, Pallas kernels for 6%

profile of v8, /device:TPU:1, one launch (start us, length us, event | category | flops | bytes accessed | tf_op | source)
XLA Modules:
  0.0 63.8 jit_solution(13757805841592436866)
XLA Ops:
  0.6 1.5 %collective-permute-start = (f32[2,8,256]{2,1,0:T(8,128)}, f32[2,8,256]{2,1,0:T(8,128)S(1)}, u32[]{:S(2)}, u32[]{:S(2)}) collective-permute-start(f32[2,8,256]{2,1,0:T(8,128)} %own_ref.1), channel_id=1, source_target_pairs={{0,1},{1,0},{2,3},{3,2},{4,5},{5,4},{6,7},{7,6},{8,9},{9,8},{10,11... | collective-permute-start | bytes 49160 | tf_op jit(solution)/shard_map/ppermute | solution.py:262
  2.1 1.3 %collective-permute-start.1 = (f32[2,8,256]{2,1,0:T(8,128)}, f32[2,8,256]{2,1,0:T(8,128)S(1)}, u32[]{:S(2)}, u32[]{:S(2)}) collective-permute-start(f32[2,8,256]{2,1,0:T(8,128)} %own_ref.1), channel_id=1, source_target_pairs={{0,15},{1,2},{2,1},{3,4},{4,3},{5,6},{6,5},{7,8},{8,7},{9,10},{10,... | collective-permute-start | bytes 49160 | tf_op jit(solution)/shard_map/ppermute | solution.py:262
  3.4 0.0 copy-start
  3.4 1.4 %shard_map.68 = (f32[2,3,64,256]{3,2,1,0:T(8,128)S(1)}, f32[2,3,64,256]{3,2,1,0:T(8,128)S(1)}, f32[3,3,64,256]{3,2,1,0:T(8,128)S(1)}, f32[3,3,64,256]{3,2,1,0:T(8,128)S(1)}) custom-call(f32[1,3,2,64,256]{4,3,2,1,0:T(8,128)} %body_hbm.1, s32[3,2,64,256]{3,2,1,0:T(8,128)} %fixed_hbm.1, s32[1,128]{1,0:T(1,128)} %node_hbm.1, f32[3,1,128]{2,1,0:T(1,128)} %bitcast.2), custom_call_target="tpu_custom_call" | custom-call | tf_op jit(solution)/shard_map/pallas_call | solution.py:630
  4.8 0.6 collective-permute-start.3
  5.3 0.0 collective-permute-done.chip_ref
  5.3 0.2 collective-permute-done.1.link_ref
  5.5 0.0 copy-done
  5.5 2.7 %collective-permute-start.2 = (f32[3,3,64,256]{3,2,1,0:T(8,128)S(1)}, f32[3,3,64,256]{3,2,1,0:T(8,128)S(1)}, u32[]{:S(2)}, u32[]{:S(2)}) collective-permute-start(f32[3,3,64,256]{3,2,1,0:T(8,128)S(1)} %get-tuple-element.29), channel_id=1, source_target_pairs={{0,1},{1,0},{2,3},{3,2},{4,5},{5,4},{6,7},{7,6},{8,9},{9,8},{10,11... | collective-permute-start | bytes 1769480 | tf_op jit(solution)/shard_map/ppermute | solution.py:262
  8.2 17.0 %all_to_all.15.dens_ref = f32[8,6,8,256]{3,2,1,0:T(8,128)S(1)} all-to-all(f32[8,6,8,256]{3,2,1,0:T(8,128)S(1)} %shard_map.69), channel_id=1, replica_groups=mesh['load'=8,'space'=16] {'load'}, dimensions={0} | all-to-all | bytes 786432 | tf_op jit(solution)/shard_map/all_to_all | solution.py:649
  25.2 0.0 collective-permute-done.3.link_ref
  25.2 0.0 collective-permute-done.2.chip_ref
  25.2 1.7 %shard_map.70 = (f32[2,3,64,256]{3,2,1,0:T(8,128)S(1)}, f32[3,3,64,256]{3,2,1,0:T(8,128)S(1)}, f32[6,72,256]{2,1,0:T(8,128)S(1)}, f32[4,64,256]{2,1,0:T(8,128)S(...) custom-call(f32[2,3,64,256]{3,2,1,0:T(8,128)S(1)} %get-tuple-element.26.load_ref, ...), custom_call_target="tpu_custom_call" | custom-call | tf_op jit(solution)/shard_map/pallas_call | solution.py:655
  26.9 0.2 collective-permute-start.4
  27.1 2.1 %shard_map.71 = (f32[3,64,256]{2,1,0:T(8,128)S(1)}, f32[1,3,72,256]{3,2,1,0:T(8,128)S(1)}, f32[1,3,72,256]{3,2,1,0:T(8,128)S(1)}, f32[1,3,72,256]{3,2,1,0:T(8,12...) custom-call(f32[2,3,64,256]{3,2,1,0:T(8,128)S(1)} %get-tuple-element.33.v1_ref, ...), custom_call_target="tpu_custom_call" | custom-call | tf_op jit(solution)/shard_map/pallas_call | solution.py:663
  29.2 2.6 %collective-permute-done.4.v1_left_ref = f32[2,3,64,256]{3,2,1,0:T(8,128)S(1)} collective-permute-done((f32[2,3,64,256]{3,2,1,0:T(8,128)S(1)}, f32[2,3,64,256]{3,2,1,0:T(8,128)S(1)}, u32[]{:S(2)}, u32[]{:S(2)}) %collective-permute-start.4) | collective-permute-done | bytes 393248 | tf_op jit(solution)/shard_map/ppermute | solution.py:621
  31.8 1.8 %shard_map.72 = (f32[2,3,64,256]{3,2,1,0:T(8,128)S(1)}, f32[16,8,128]{2,1,0:T(8,128)S(1)}) custom-call(f32[2,3,64,256]{3,2,1,0:T(8,128)S(1)} %collective-permute-done.4.v1_left_ref, f32[2,3,64,256]{3,2,1,0:T(8,128)S(1)} %get-tuple-element.33.v1_ref, f32[3,3,64,256]{3,2,1,0:T(8,128)S(1)} %collective-permute-done.2.chip_ref, ...), custom_call_target="tpu_custom_call" | custom-call | tf_op jit(solution)/shard_map/pallas_call | solution.py:670
  33.6 13.9 %all_to_all.16.mom_ref = f32[16,8,128]{2,1,0:T(8,128)S(1)} all-to-all(f32[16,8,128]{2,1,0:T(8,128)S(1)} %get-tuple-element.47), channel_id=1, replica_groups=mesh['load'=8,'space'=16] {'space'}, dimensions={0} | all-to-all | bytes 131072 | tf_op jit(solution)/shard_map/all_to_all | solution.py:677
  47.5 1.3 %shard_map.73 = (f32[3,2,64,256]{3,2,1,0:T(8,128)}, f32[8,20,256]{2,1,0:T(8,128)S(1)}) custom-call(f32[3,3,64,256]{3,2,1,0:T(8,128)S(1)} %get-tuple-element.32.v0_ref, f32[2,3,64,256]{3,2,1,0:T(8,128)S(1)} %collective-permute-done.4.v1_left_ref, f32[2,3,64,256]{3,2,1,0:T(8,128)S(1)} %get-tuple-element.33.v1_ref, ...), custom_call_target="tpu_custom_call" | custom-call | tf_op jit(solution)/shard_map/pallas_call | solution.py:679
  48.8 10.6 %all_to_all.17 = f32[8,20,256]{2,1,0:T(8,128)S(1)} all-to-all(f32[8,20,256]{2,1,0:T(8,128)S(1)} %get-tuple-element.49), channel_id=1, replica_groups=mesh['load'=8,'space'=16] {'load'}, dimensions={0} | all-to-all | bytes 327680 | tf_op jit(solution)/shard_map/all_to_all | solution.py:686
  59.4 1.9 %collective-permute-start.5 = (f32[20,256]{1,0:T(8,128)S(1)}, f32[20,256]{1,0:T(8,128)S(1)}, u32[]{:S(2)}, u32[]{:S(2)}) collective-permute-start(f32[20,256]{1,0:T(8,128)S(1)} %reduce_sum.9.energy_ref), channel_id=1, source_target_pairs={{0,15},{1,0},{2,1},{3,2},{4,3},{5,4},{6,5},{7,6},{8,7},{9,8},{10,9... | collective-permute-start | bytes 61448 | tf_op jit(solution)/shard_map/ppermute | solution.py:621
  61.3 1.7 %collective-permute-done.5.next_ref = f32[20,256]{1,0:T(8,128)S(1)} collective-permute-done((f32[20,256]{1,0:T(8,128)S(1)}, f32[20,256]{1,0:T(8,128)S(1)}, u32[]{:S(2)}, u32[]{:S(2)}) %collective-permute-start.5) | collective-permute-done | bytes 20512 | tf_op jit(solution)/shard_map/ppermute | solution.py:621
  63.0 0.7 %shard_map.74 = f32[2,8,256]{2,1,0:T(8,128)} custom-call(f32[20,256]{1,0:T(8,128)S(1)} %reduce_sum.9.energy_ref, f32[20,256]{1,0:T(8,128)S(1)} %collective-permute-done.5.next_ref, f32[8,6,8,256]{3,2,1,0:T(8,128)S(1)} %all_to_all.15.dens_ref), custom_call_target="tpu_custom_call" | custom-call | tf_op jit(solution)/shard_map/pallas_call | solution.py:688
  (2 shorter events, 0.0 us)
Async XLA Ops:
  0.6 4.7 %collective-permute-start = (f32[2,8,256]{2,1,0:T(8,128)}, f32[2,8,256]{2,1,0:T(8,128)S(1)}, u32[]{:S(2)}, u32[]{:S(2)}) collective-permute-start(f32[2,8,256]{2,1,0:T(8,128)} %own_ref.1), channel_id=1, source_target_pairs={{0,1},{1,0},{2,3},{3,2},{4,5},{5,4},{6,7},{7,6},{8,9},{9,8},{10,11... | collective-permute-start | bytes 49160 | tf_op jit(solution)/shard_map/ppermute | solution.py:262
  2.1 3.4 %collective-permute-start.1 = (f32[2,8,256]{2,1,0:T(8,128)}, f32[2,8,256]{2,1,0:T(8,128)S(1)}, u32[]{:S(2)}, u32[]{:S(2)}) collective-permute-start(f32[2,8,256]{2,1,0:T(8,128)} %own_ref.1), channel_id=1, source_target_pairs={{0,15},{1,2},{2,1},{3,4},{4,3},{5,6},{6,5},{7,8},{8,7},{9,10},{10,... | collective-permute-start | bytes 49160 | tf_op jit(solution)/shard_map/ppermute | solution.py:262
  3.4 2.1 %copy-start = (f32[2,8,256]{2,1,0:T(8,128)S(1)}, f32[2,8,256]{2,1,0:T(8,128)}, u32[]{:S(2)}) copy-start(f32[2,8,256]{2,1,0:T(8,128)} %own_ref.1) | copy-start | bytes 49156
  4.8 20.5 %collective-permute-start.3 = (f32[3,3,64,256]{3,2,1,0:T(8,128)S(1)}, f32[3,3,64,256]{3,2,1,0:T(8,128)S(1)}, u32[]{:S(2)}, u32[]{:S(2)}) collective-permute-start(f32[3,3,64,256]{3,2,1,0:T(8,128)S(1)} %get-tuple-element.30), channel_id=1, source_target_pairs={{0,15},{1,2},{2,1},{3,4},{4,3},{5,6},{6,5},{7,8},{8,7},{9,10},{10,... | collective-permute-start | bytes 1769480 | tf_op jit(solution)/shard_map/ppermute | solution.py:262
  5.5 19.7 %collective-permute-start.2 = (f32[3,3,64,256]{3,2,1,0:T(8,128)S(1)}, f32[3,3,64,256]{3,2,1,0:T(8,128)S(1)}, u32[]{:S(2)}, u32[]{:S(2)}) collective-permute-start(f32[3,3,64,256]{3,2,1,0:T(8,128)S(1)} %get-tuple-element.29), channel_id=1, source_target_pairs={{0,1},{1,0},{2,3},{3,2},{4,5},{5,4},{6,7},{7,6},{8,9},{9,8},{10,11... | collective-permute-start | bytes 1769480 | tf_op jit(solution)/shard_map/ppermute | solution.py:262
  26.9 4.9 %collective-permute-start.4 = (f32[2,3,64,256]{3,2,1,0:T(8,128)S(1)}, f32[2,3,64,256]{3,2,1,0:T(8,128)S(1)}, u32[]{:S(2)}, u32[]{:S(2)}) collective-permute-start(f32[2,3,64,256]{3,2,1,0:T(8,128)S(1)} %get-tuple-element.33.v1_ref), channel_id=1, source_target_pairs={{0,1},{1,2},{2,3},{3,4},{4,5},{5,6},{6,7},{7,8},{8,9},{9,10},{10,1... | collective-permute-start | bytes 1179656 | tf_op jit(solution)/shard_map/ppermute | solution.py:621
  59.4 3.6 %collective-permute-start.5 = (f32[20,256]{1,0:T(8,128)S(1)}, f32[20,256]{1,0:T(8,128)S(1)}, u32[]{:S(2)}, u32[]{:S(2)}) collective-permute-start(f32[20,256]{1,0:T(8,128)S(1)} %reduce_sum.9.energy_ref), channel_id=1, source_target_pairs={{0,15},{1,0},{2,1},{3,2},{4,3},{5,4},{6,5},{7,6},{8,7},{9,8},{10,9... | collective-permute-start | bytes 61448 | tf_op jit(solution)/shard_map/ppermute | solution.py:621
